TPU v7x, 256 devices: a whole 4x4x8 slice. The times are simulated.
256 devices in a mesh: dp: 8 (over x, core), tile: 32 (over z, y).
Axes of the slice: x: 4, y: 4, z: 8, core: 2. Of those that a mesh axis runs over, the one named last changes fastest.
Arguments:
- image_descriptors: bfloat16 [8, 1024, 256], P('dp', 'tile'), may hold values from -50 to 50
- image_distance_scores: bfloat16 [8, 1024, 64], P('dp', 'tile'), may hold values from -104 to 126
- entry_sender_location: int32 [8, 32, 32, 64], P('dp', 'tile'), may hold values from 0 to 2047, as said below
- entry_receiver_square: int32 [8, 32, 32, 64], P('dp', 'tile'), may hold values from 0 to 799
- entry_valid_tally: int32 [8, 32, 32], P('dp', 'tile'), may hold values from 1 to 64, as said below
- predicted_adjoint: bfloat16 [8, 64, 400, 256], P('dp', 'tile'), may hold values from -6 to 6
- initial_plane_filter: bfloat16 [2304, 256], replicated, may hold values from -0.125 to 0.125
- predictor_filter: bfloat16 [2304, 256], replicated, may hold values from -0.125 to 0.125
Outputs:
- predicted_scene: bfloat16 [8, 64, 400, 256], P('dp', 'tile')
- prenonlinear_derivative: bfloat16 [8, 64, 400, 256], P('dp', 'tile')
- predictor_filter_derivative: float32 [2304, 256], P('tile')
Inputs may be any that keep to these rules, and one draw needn't show every extreme that they name: `entry_sender_location`: the entries of one source device's lists, over all strips and slots, are distinct; entry p stands for that device's local pixel p // 64 and depth bin p % 64. `entry_receiver_square`: cell row * 400 + column of the destination strip. The first entry_valid_tally slots of a list are live; in every frame some strip has 64 live slots from every source device.
All inputs are finite; a program needn't handle non-finite values.
Results may differ from a plain program's by a relative error of at most 0.0059.
Values may be sent and summed in bfloat16 or wider, within the bound.
No kernel may reach another device: no remote copies, remote signals or barrier semaphores. Data moves between devices by JAX's collectives and lax.ppermute only.
A program may use at most 64 MiB of HBM per device.

v0:
```python
import math

import jax
import jax.numpy as jnp
from jax import lax
from jax.sharding import PartitionSpec as P

epsilon = 1e-05


def with_halo(cells, sides, width):
    for axis, dim in sides:
        count = lax.axis_size(axis)
        ends = count - 1
        head = lax.slice_in_dim(cells, 0, width, axis=dim)
        tail = lax.slice_in_dim(cells, cells.shape[dim] - width, cells.shape[dim], axis=dim)
        cells = jnp.concatenate(
            [
                lax.ppermute(tail, axis, [(i, (i + 1) % count) for i in range(ends)]),
                cells,
                lax.ppermute(head, axis, [((i + 1) % count, i) for i in range(ends)]),
            ],
            axis=dim,
        )
    return cells


def silu_slope(pre_act):
    sigma = jax.nn.sigmoid(pre_act)
    return sigma * (1.0 + pre_act * (1.0 - sigma))


def tap_window(padded, tap_index, horizontal_tally, vertical_tally, flipped):
    shift_y = tap_index // 3 - 1
    shift_x = tap_index % 3 - 1
    if flipped:
        shift_y = -shift_y
        shift_x = -shift_x
    return padded[
        :,
        1 + shift_y : 1 + shift_y + horizontal_tally,
        1 + shift_x : 1 + shift_x + vertical_tally,
        :,
    ]


def stencil_offsets(padded, weight, horizontal_tally, vertical_tally, flipped):
    plane_tally = weight.shape[1]
    result = None
    for tap_index in range(9):
        window = tap_window(padded, tap_index, horizontal_tally, vertical_tally, flipped)
        block_weight = weight[tap_index * plane_tally : (tap_index + 1) * plane_tally]
        if flipped:
            term = jnp.einsum(
                "fyxo,io->fyxi", window, block_weight, preferred_element_type=jnp.float32
            )
        else:
            term = jnp.einsum(
                "fyxi,io->fyxo", window, block_weight, preferred_element_type=jnp.float32
            )
        result = term if result is None else result + term
    return result


def broadened_verticals(field):
    return jnp.pad(field, ((0, 0), (0, 0), (1, 1), (0, 0)))


def lift_values(features, flat_prob, point_index, live_mask, depth_bins):
    frame_rows = lax.broadcasted_iota(jnp.int32, point_index.shape, 0)
    chosen = flat_prob[frame_rows, point_index]
    weight_row = jnp.where(live_mask, chosen, 0.0)
    rows_taken = features[frame_rows, point_index // depth_bins]
    return (rows_taken.astype(jnp.float32) * weight_row[:, :, None]).astype(jnp.bfloat16)


def splat_frames(values, cell_ids, cell_total):
    snapshot_ordinal, slot_total, plane_tally = values.shape
    block_size = math.gcd(slot_total, 512)
    blocks = slot_total // block_size

    def add_block(block_index, summed):
        part_values = lax.dynamic_slice_in_dim(values, block_index * block_size, block_size, 1)
        part_cells = lax.dynamic_slice_in_dim(cell_ids, block_index * block_size, block_size, 1)
        onehot = (
            lax.broadcasted_iota(jnp.int32, (snapshot_ordinal, cell_total, block_size), 1)
            == part_cells[:, None, :]
        ).astype(jnp.bfloat16)
        return summed + jnp.einsum(
            "fcs,fsk->fck", onehot, part_values, preferred_element_type=jnp.float32
        )

    start_sum = jnp.zeros((snapshot_ordinal, cell_total, plane_tally), jnp.float32)
    return lax.fori_loop(0, blocks, add_block, start_sum)


def on_device(
    image_descriptors,
    image_distance_scores,
    entry_sender_location,
    entry_receiver_square,
    entry_valid_tally,
    predicted_adjoint,
    initial_plane_filter,
    predictor_filter,
):
    snapshot_ordinal, horizontal_tally, vertical_tally, plane_tally = predicted_adjoint.shape
    depth_bins = image_distance_scores.shape[2]
    cell_total = horizontal_tally * vertical_tally
    tile_count = lax.axis_size("tile")
    depth_prob = jax.nn.softmax(image_distance_scores.astype(jnp.float32), axis=-1)
    flat_prob = depth_prob.reshape(snapshot_ordinal, -1)
    own_lists = entry_sender_location[:, 0]
    points = own_lists.reshape(snapshot_ordinal, -1)
    live_mask = (
        lax.broadcasted_iota(jnp.int32, own_lists.shape, 2) < entry_valid_tally[:, 0][:, :, None]
    ).reshape(snapshot_ordinal, -1)
    lifted = lift_values(image_descriptors, flat_prob, points, live_mask, depth_bins)
    lifted = lifted.reshape(own_lists.shape + (plane_tally,))
    arrived, arrived_cells = (
        lax.all_to_all(lifted, "tile", split_axis=1, concat_axis=1, tiled=True),
        lax.all_to_all(
            entry_receiver_square[:, 0], "tile", split_axis=1, concat_axis=1, tiled=True
        ),
    )
    values = arrived.reshape(snapshot_ordinal, -1, plane_tally)
    cell_ids = arrived_cells.reshape(snapshot_ordinal, -1)
    splat_sum = splat_frames(values, cell_ids, cell_total)
    norm_factor = lax.rsqrt(jnp.mean(splat_sum * splat_sum, axis=-1, keepdims=True) + epsilon)
    aerial_scene = (
        (splat_sum * norm_factor)
        .astype(jnp.bfloat16)
        .reshape(snapshot_ordinal, horizontal_tally, vertical_tally, plane_tally)
    )
    bev_wide = broadened_verticals(with_halo(aerial_scene, (("tile", 1),), 1))
    pre_first = stencil_offsets(
        bev_wide, initial_plane_filter, horizontal_tally, vertical_tally, False
    )
    hidden = jax.nn.silu(pre_first).astype(jnp.bfloat16)
    broadened_latent = broadened_verticals(with_halo(hidden, (("tile", 1),), 1))
    predicted_scene = (
        aerial_scene.astype(jnp.float32)
        + stencil_offsets(
            broadened_latent, predictor_filter, horizontal_tally, vertical_tally, False
        )
    ).astype(jnp.bfloat16)
    broadened_derivative = broadened_verticals(with_halo(predicted_adjoint, (("tile", 1),), 1))
    yielded_derivative = stencil_offsets(
        broadened_derivative, predictor_filter, horizontal_tally, vertical_tally, True
    )
    prenonlinear_derivative = (yielded_derivative * silu_slope(pre_first)).astype(jnp.bfloat16)
    patches = jnp.concatenate(
        [
            tap_window(broadened_latent, tap_index, horizontal_tally, vertical_tally, False)
            for tap_index in range(9)
        ],
        axis=-1,
    )
    patches = patches.reshape(-1, 9 * plane_tally)
    linear_derivative = predicted_adjoint.reshape(-1, plane_tally)
    share_rows = 9 * plane_tally // tile_count
    local_grad = lax.dot_general(
        patches, linear_derivative, (((0,), (0,)), ((), ())), preferred_element_type=jnp.float32
    )
    summed = lax.psum(local_grad, ("dp", "tile"))
    local_portion = lax.dynamic_slice_in_dim(
        summed, lax.axis_index("tile") * share_rows, share_rows, 0
    )
    square_tally = (
        snapshot_ordinal * lax.axis_size("dp") * horizontal_tally * tile_count * vertical_tally
    )
    predictor_filter_derivative = local_portion / math.sqrt(square_tally)
    return (predicted_scene, prenonlinear_derivative, predictor_filter_derivative)


def solution(mesh):
    placed = (
        P("dp", "tile", None),
        P("dp", "tile", None),
        P("dp", "tile", None, None),
        P("dp", "tile", None, None),
        P("dp", "tile", None),
        P("dp", "tile", None, None),
        P(),
        P(),
    )
    return jax.shard_map(
        on_device,
        mesh=mesh,
        in_specs=placed,
        out_specs=(P("dp", "tile", None, None), P("dp", "tile", None, None), P("tile", None)),
        check_vma=False,
    )
```

profile of v0, /device:TPU:1, one launch (start us, length us, event | category | flops | bytes accessed | tf_op | source)
XLA Modules:
  0.0 398.5 jit_solution(7517399694128305598)
XLA Ops:
  7.2 12.0 %all-to-all-start = ((s32[1,32,64]{2,0,1:T(1,128)}), s32[1,32,64]{2,0,1:T(1,128)S(1)}, u32[]{:S(2)}, u32[]{:S(2)}) async-start(s32[1,32,64]{2,0,1:T(1,128)} %bitcast.224), calls=%async_computation | async-start | bytes 32768 | tf_op jit(solution)/shard_map/all_to_all | solution.py:122
  19.2 1.1 fusion.135
  20.3 1.3 collective-permute-start.5
  21.6 4.0 %collective-permute-start.4 = (bf16[1,1,400,256]{3,2,1,0:T(8,128)(2,1)S(1)}, bf16[1,1,400,256]{3,2,1,0:T(8,128)(2,1)S(1)}, u32[]{:S(2)}, u32[]{:S(2)}) collective-permute-start(bf16[1,1,400,256]{3,2,1,0:T(8,128)(2,1)S(1)} %get-tuple-element.106), channel_id=1, source_target_pairs={{0,1},{1,2},{2,3},{3,4},{4,5},{5,6},{6,7},{7,8},{8,9},{9,10},{10,1... | collective-permute-start | bytes 614408 | tf_op jit(solution)/shard_map/ppermute | solution.py:19
  25.6 0.8 reshape_squeeze.3
  26.5 0.8 reduce_max.14
  27.3 0.9 fusion.121
  28.2 0.8 fusion.120
  29.1 12.4 %gather_fusion.1 = f32[2048]{0:T(1024)S(1)} fusion(f32[1,2048]{1,0:T(1,128)S(1)} %reshape.505, s32[2048]{0:T(1024)S(1)} %bitcast.209), kind=kCustom, calls=%fused_computation.1 | custom fusion | bytes 32768 | tf_op jit(solution)/shard_map/gather | solution.py:71
  41.6 8.6 %gather_fusion = bf16[2048,256]{1,0:T(8,128)(2,1)S(1)} fusion(bf16[1,32,256]{2,1,0:T(8,128)(2,1)S(1)} %copy-done, s32[2048]{0:T(1024)S(1)} %bitcast.208), kind=kCustom, calls=%fused_computation | custom fusion | bytes 2113536 | tf_op jit(solution)/shard_map/gather | solution.py:73
  50.3 1.3 fusion.14
  51.7 11.2 %all-to-all-start.1 = ((bf16[1,32,64,256]{3,2,0,1:T(8,128)(2,1)}), bf16[1,32,64,256]{3,2,0,1:T(8,128)(2,1)}, u32[]{:S(2)}, u32[]{:S(2)}) async-start(bf16[1,32,64,256]{3,2,0,1:T(8,128)(2,1)} %fusion.14), calls=%async_computation.1 | async-start | bytes 2097152 | tf_op jit(solution)/shard_map/all_to_all | solution.py:121
  62.9 0.5 broadcast.313
  63.4 0.7 reduce.7
  64.4 1.3 fusion.37
  65.7 1.2 convolution_add_fusion.6
  67.0 0.3 convolution_add_fusion.5
  67.3 0.3 convolution_add_fusion.4
  67.6 0.3 convolution_add_fusion.3
  67.9 0.3 convolution_add_fusion.2
  68.2 0.3 convolution_add_fusion.1
  68.5 19.5 %all-to-all-done.1 = bf16[1,32,64,256]{3,2,0,1:T(8,128)(2,1)} async-done(((bf16[1,32,64,256]{3,2,0,1:T(8,128)(2,1)}), bf16[1,32,64,256]{3,2,0,1:T(8,128)(2,1)}, u32[]{:S(2)}, u32[]{:S(2)}) %all-to-all-start.1) | async-done | bytes 1048608 | tf_op jit(solution)/shard_map/all_to_all | solution.py:121
  88.1 6.2 %while.14 = (s32[]{:T(128)}, f32[1,800,256]{2,1,0:T(8,128)S(1)}, s32[1,2048]{1,0:T(1,128)S(1)}, bf16[1,2048,256]{2,1,0:T(8,128)(2,1)}, s32[]{:T(128)}, /*index=5*/s32[]{:T(128)}, s32[]{:T(128)}, s32[]{:T(128)}) while((s32[]{:T(128)}, f32[1,800,256]{2,1,0:T(8,128)S(1)}, s32[1,2048]{1,0:T(1,128)S(1)}, ...), condition=%wide.region_3.4_spmd.clone, body=%wide.region_2.3_spmd.clone.sunk | while | flops 210534400 | bytes 1906845 | solution.py:94
  88.1 1.5 fusion.145
  89.6 1.5 fusion.145
  91.2 1.5 fusion.145
  92.7 1.5 fusion.145
  94.7 1.4 collective-permute-start.1
  96.2 4.6 %collective-permute-start = (bf16[1,1,400,256]{3,2,1,0:T(8,128)(2,1)S(1)}, bf16[1,1,400,256]{3,2,1,0:T(8,128)(2,1)S(1)}, u32[]{:S(2)}, u32[]{:S(2)}) collective-permute-start(bf16[1,1,400,256]{3,2,1,0:T(8,128)(2,1)S(1)} %get-tuple-element.110), channel_id=1, source_target_pairs={{0,1},{1,2},{2,3},{3,4},{4,5},{5,6},{6,7},{7,8},{8,9},{9,10},{10,1... | collective-permute-start | bytes 614408 | tf_op jit(solution)/shard_map/ppermute | solution.py:19
  100.8 0.3 fusion.30
  101.1 0.9 collective-permute-done.1
  102.0 1.5 collective-permute-done
  103.7 0.3 fusion.38
  104.5 0.3 convolution_add_fusion.19
  105.3 0.3 convolution_add_fusion.16
  105.9 0.4 multiply_convert_fusion
  106.3 1.3 collective-permute-start.3
  107.6 4.9 %collective-permute-start.2 = (bf16[1,1,400,256]{3,2,1,0:T(8,128)(2,1)S(1)}, bf16[1,1,400,256]{3,2,1,0:T(8,128)(2,1)S(1)}, u32[]{:S(2)}, u32[]{:S(2)}) collective-permute-start(bf16[1,1,400,256]{3,2,1,0:T(8,128)(2,1)S(1)} %get-tuple-element.108), channel_id=1, source_target_pairs={{0,1},{1,2},{2,3},{3,4},{4,5},{5,6},{6,7},{7,8},{8,9},{9,10},{10,1... | collective-permute-start | bytes 614408 | tf_op jit(solution)/shard_map/ppermute | solution.py:19
  112.6 1.3 fusion.23
  113.8 1.2 collective-permute-done.2
  116.9 2.9 convolution_bitcast_fusion
  119.8 1.2 fusion.48
  121.0 1.2 convolution_add_fusion.10
  122.2 1.2 convolution_add_fusion.9
  123.4 1.2 convolution_add_fusion.8
  124.6 1.9 fusion.24
  126.5 263.6 %all-reduce.7.cloned.1.call-done = f32[2304,256]{1,0:T(8,128)} async-done(((f32[2304,256]{1,0:T(8,128)}), f32[2304,256]{1,0:T(8,128)}) %all-reduce.7.cloned.1.call-update) | async-done | bytes 2359312 | tf_op jit(solution)/shard_map/psum | solution.py:165
  390.2 1.5 dynamic-slice_multiply_fusion
  (58 shorter events, 4.5 us)
Async XLA Ops:
  7.2 34.4 %copy-start = (bf16[1,32,256]{2,1,0:T(8,128)(2,1)S(1)}, bf16[1,32,256]{2,1,0:T(8,128)(2,1)}, u32[]{:S(2)}) copy-start(bf16[1,32,256]{2,1,0:T(8,128)(2,1)} %param.10) | copy-start | bytes 49156
  7.2 44.5 %all-to-all-start = ((s32[1,32,64]{2,0,1:T(1,128)}), s32[1,32,64]{2,0,1:T(1,128)S(1)}, u32[]{:S(2)}, u32[]{:S(2)}) async-start(s32[1,32,64]{2,0,1:T(1,128)} %bitcast.224), calls=%async_computation | async-start | bytes 32768 | tf_op jit(solution)/shard_map/all_to_all | solution.py:122
  20.3 43.9 %collective-permute-start.5 = (bf16[1,1,400,256]{3,2,1,0:T(8,128)(2,1)S(1)}, bf16[1,1,400,256]{3,2,1,0:T(8,128)(2,1)S(1)}, u32[]{:S(2)}, u32[]{:S(2)}) collective-permute-start(bf16[1,1,400,256]{3,2,1,0:T(8,128)(2,1)S(1)} %get-tuple-element.107), channel_id=1, source_target_pairs={{1,0},{2,1},{3,2},{4,3},{5,4},{6,5},{7,6},{8,7},{9,8},{10,9},{11,1... | collective-permute-start | bytes 614408 | tf_op jit(solution)/shard_map/ppermute | solution.py:21
  21.6 42.6 %collective-permute-start.4 = (bf16[1,1,400,256]{3,2,1,0:T(8,128)(2,1)S(1)}, bf16[1,1,400,256]{3,2,1,0:T(8,128)(2,1)S(1)}, u32[]{:S(2)}, u32[]{:S(2)}) collective-permute-start(bf16[1,1,400,256]{3,2,1,0:T(8,128)(2,1)S(1)} %get-tuple-element.106), channel_id=1, source_target_pairs={{0,1},{1,2},{2,3},{3,4},{4,5},{5,6},{6,7},{7,8},{8,9},{9,10},{10,1... | collective-permute-start | bytes 614408 | tf_op jit(solution)/shard_map/ppermute | solution.py:19
  41.6 8.7 %copy-start.5 = (s32[1,1,32]{2,1,0:T(1,128)S(1)}, s32[1,1,32]{2,1,0:T(1,128)}, u32[]{:S(2)}) copy-start(s32[1,1,32]{2,1,0:T(1,128)} %param.14) | copy-start | bytes 388
  50.3 13.9 %copy-start.1 = (bf16[1,2,400,256]{3,2,1,0:T(8,128)(2,1)S(1)}, bf16[1,2,400,256]{3,2,1,0:T(8,128)(2,1)}, u32[]{:S(2)}) copy-start(bf16[1,2,400,256]{3,2,1,0:T(8,128)(2,1)} %param.15) | copy-start | bytes 1228804
  51.7 36.4 %all-to-all-start.1 = ((bf16[1,32,64,256]{3,2,0,1:T(8,128)(2,1)}), bf16[1,32,64,256]{3,2,0,1:T(8,128)(2,1)}, u32[]{:S(2)}, u32[]{:S(2)}) async-start(bf16[1,32,64,256]{3,2,0,1:T(8,128)(2,1)} %fusion.14), calls=%async_computation.1 | async-start | bytes 2097152 | tf_op jit(solution)/shard_map/all_to_all | solution.py:121
  62.8 327.3 %all-reduce.7.cloned.1.call-start = ((), (), s32[]{:S(2)}) async-start(), calls=%async_computation.2 | async-start | bytes 4718592 | tf_op jit(solution)/shard_map/psum | solution.py:165
  64.4 2.5 copy-start.2
  94.3 6.5 %copy-start.3 = (bf16[2304,256]{1,0:T(8,128)(2,1)S(1)}, bf16[2304,256]{1,0:T(8,128)(2,1)}, u32[]{:S(2)}) copy-start(bf16[2304,256]{1,0:T(8,128)(2,1)} %param.17) | copy-start | bytes 3538948
  94.7 9.0 %copy-start.4 = (bf16[2304,256]{1,0:T(8,128)(2,1)S(1)}, bf16[2304,256]{1,0:T(8,128)(2,1)}, u32[]{:S(2)}) copy-start(bf16[2304,256]{1,0:T(8,128)(2,1)} %param.16) | copy-start | bytes 3538948
  94.7 7.3 %collective-permute-start.1 = (bf16[1,1,400,256]{3,2,1,0:T(8,128)(2,1)S(1)}, bf16[1,1,400,256]{3,2,1,0:T(8,128)(2,1)S(1)}, u32[]{:S(2)}, u32[]{:S(2)}) collective-permute-start(bf16[1,1,400,256]{3,2,1,0:T(8,128)(2,1)S(1)} %get-tuple-element.111), channel_id=1, source_target_pairs={{1,0},{2,1},{3,2},{4,3},{5,4},{6,5},{7,6},{8,7},{9,8},{10,9},{11,1... | collective-permute-start | bytes 614408 | tf_op jit(solution)/shard_map/ppermute | solution.py:21
  96.2 7.3 %collective-permute-start = (bf16[1,1,400,256]{3,2,1,0:T(8,128)(2,1)S(1)}, bf16[1,1,400,256]{3,2,1,0:T(8,128)(2,1)S(1)}, u32[]{:S(2)}, u32[]{:S(2)}) collective-permute-start(bf16[1,1,400,256]{3,2,1,0:T(8,128)(2,1)S(1)} %get-tuple-element.110), channel_id=1, source_target_pairs={{0,1},{1,2},{2,3},{3,4},{4,5},{5,6},{6,7},{7,8},{8,9},{9,10},{10,1... | collective-permute-start | bytes 614408 | tf_op jit(solution)/shard_map/ppermute | solution.py:19
  106.3 7.5 %collective-permute-start.3 = (bf16[1,1,400,256]{3,2,1,0:T(8,128)(2,1)S(1)}, bf16[1,1,400,256]{3,2,1,0:T(8,128)(2,1)S(1)}, u32[]{:S(2)}, u32[]{:S(2)}) collective-permute-start(bf16[1,1,400,256]{3,2,1,0:T(8,128)(2,1)S(1)} %get-tuple-element.109), channel_id=1, source_target_pairs={{1,0},{2,1},{3,2},{4,3},{5,4},{6,5},{7,6},{8,7},{9,8},{10,9},{11,1... | collective-permute-start | bytes 614408 | tf_op jit(solution)/shard_map/ppermute | solution.py:21
  107.6 7.4 %collective-permute-start.2 = (bf16[1,1,400,256]{3,2,1,0:T(8,128)(2,1)S(1)}, bf16[1,1,400,256]{3,2,1,0:T(8,128)(2,1)S(1)}, u32[]{:S(2)}, u32[]{:S(2)}) collective-permute-start(bf16[1,1,400,256]{3,2,1,0:T(8,128)(2,1)S(1)} %get-tuple-element.108), channel_id=1, source_target_pairs={{0,1},{1,2},{2,3},{3,4},{4,5},{5,6},{6,7},{7,8},{8,9},{9,10},{10,1... | collective-permute-start | bytes 614408 | tf_op jit(solution)/shard_map/ppermute | solution.py:19
Sparse Core Ops, SparseCore 0:
  119.9 270.1 all-reduce.6
where the time goes:
time: 400 us; the launch traced here: 399 us
  waiting for transfers between devices  287 us (72%)
  starting transfers between devices  40.8 us (10%)
  matrix products  24.8 us (6%)
  local copies, waits for them, and re-layouts  24.2 us (6%)
  between operations  14.5 us (4%)
  other arithmetic  7.3 us (2%)
    psum x1, waiting for transfers between devices, on_device(): summed = lax.psum(local_grad, ('dp', 'tile'))  264 us
    all_to_all x1, waiting for transfers between devices, on_device(): lax.all_to_all(lifted, 'tile', split_axis=1, concat_axis=1, tiled=True)  19.5 us
    ppermute x3, starting transfers between devices, with_halo(): lax.ppermute(tail, axis, [(i, (i + 1) % count) for i in range(ends)])  13.5 us
    gather x2, local copies, waits for them, and re-layouts, lift_values(): chosen = flat_prob[frame_rows, point_index]  12.5 us
    all_to_all x1, starting transfers between devices, on_device(): lax.all_to_all(entry_receiver_square[:, 0], 'tile', split_axis=1, concat_...  12 us
    all_to_all x1, starting transfers between devices, on_device(): lax.all_to_all(lifted, 'tile', split_axis=1, concat_axis=1, tiled=True)  11.2 us
    dot_general x18, matrix products, stencil_offsets(): jnp.einsum('fyxi,io->fyxo', window, block_weight, preferred_element_type=...  10.3 us
    gather x1, local copies, waits for them, and re-layouts, lift_values(): rows_taken = features[frame_rows, point_index // depth_bins]  8.64 us
  transfers between devices with their start and end apart: 9, of which 5 were waited for; matrix products, arithmetic and copies ran while one was open for 10% of the time, Pallas kernels for 0%

commit v1 on v0

--- a/solution.py
+++ b/solution.py
@@ -92,6 +92,25 @@
 
     start_sum = jnp.zeros((snapshot_ordinal, cell_total, plane_tally), jnp.float32)
     return lax.fori_loop(0, blocks, add_block, start_sum)
+
+
+def reduced_gradient(local_grad, share_rows, tile_count):
+    half = local_grad.shape[1] // 2
+    dp_count = lax.axis_size("dp")
+    odd_core = lax.axis_index("dp") % 2 == 1
+    left, right = local_grad[:, :half], local_grad[:, half:]
+    kept = jnp.where(odd_core, right, left)
+    given = jnp.where(odd_core, left, right).astype(jnp.bfloat16)
+    taken = lax.ppermute(given, "dp", [(i, i ^ 1) for i in range(dp_count)])
+    pair_sum = (kept + taken.astype(jnp.float32)).astype(jnp.bfloat16)
+    shares = lax.all_to_all(
+        pair_sum.reshape(tile_count, share_rows, half), "tile", 0, 0, tiled=True
+    )
+    own_share = jnp.sum(shares.astype(jnp.float32), axis=0)
+    copies = jnp.broadcast_to(own_share[None], (dp_count, share_rows, half))
+    dp_shares = lax.all_to_all(copies, "dp", 0, 0, tiled=True)
+    whole = jnp.sum(dp_shares.reshape(dp_count // 2, 2, share_rows, half), axis=0)
+    return jnp.concatenate([whole[0], whole[1]], axis=1)
 
 
 def on_device(
@@ -162,10 +181,7 @@
     local_grad = lax.dot_general(
         patches, linear_derivative, (((0,), (0,)), ((), ())), preferred_element_type=jnp.float32
     )
-    summed = lax.psum(local_grad, ("dp", "tile"))
-    local_portion = lax.dynamic_slice_in_dim(
-        summed, lax.axis_index("tile") * share_rows, share_rows, 0
-    )
+    local_portion = reduced_gradient(local_grad, share_rows, tile_count)
     square_tally = (
         snapshot_ordinal * lax.axis_size("dp") * horizontal_tally * tile_count * vertical_tally
     )

time: 400 us -> 173 us (0.43)
  waiting for transfers between devices: 287 us -> 35.4 us
  starting transfers between devices: 40.8 us -> 75.8 us
  between operations: 14.5 us -> 1.13 us
    psum x1 -> x0, waiting for transfers between devices: 264 us -> none  [on_device(): summed = lax.psum(local_grad, ('dp', 'tile'))]
    all_to_all x0 -> x2, starting transfers between devices: none -> 32.1 us  [the longest x1 25.9 us: reduced_gradient(): lax.all_to_all(pair_sum.reshape(tile_count, share_rows, half), 'tile', 0,...]
    all_to_all x0 -> x2, waiting for transfers between devices: none -> 19.2 us  [the longest x1 14.6 us: reduced_gradient(): lax.all_to_all(pair_sum.reshape(tile_count, share_rows, half), 'tile', 0,...]
    all_to_all x1, waiting for transfers between devices: 19.5 us -> 4.5 us  [on_device(): lax.all_to_all(lifted, 'tile', split_axis=1, concat_axis=1, tiled=True)]
    ppermute x3, waiting for transfers between devices: 0.89 us -> 8.6 us  [with_halo(): lax.ppermute(head, axis, [((i + 1) % count, i) for i in range(ends)])]
    ppermute x0 -> x1, starting transfers between devices: none -> 5.19 us  [reduced_gradient(): taken = lax.ppermute(given, 'dp', [(i, i ^ 1) for i in range(dp_count)])]
  transfers between devices with their start and end apart: 9 -> 11, of which waited for: 5 -> 8; matrix products, arithmetic and copies ran while one was open for 10% -> 25% of each run, Pallas kernels for 0% -> 0%
where the time goes in v1:
time: 173 us; the launch traced here: 171 us
  starting transfers between devices  75.8 us (44%)
  waiting for transfers between devices  35.4 us (20%)
  matrix products  25.4 us (15%)
  local copies, waits for them, and re-layouts  24.8 us (14%)
  other arithmetic  8.71 us (5%)
    all_to_all x1, starting transfers between devices, reduced_gradient(): lax.all_to_all(pair_sum.reshape(tile_count, share_rows, half), 'tile', 0,...  25.9 us
    all_to_all x1, waiting for transfers between devices, reduced_gradient(): lax.all_to_all(pair_sum.reshape(tile_count, share_rows, half), 'tile', 0,...  14.6 us
    ppermute x3, starting transfers between devices, with_halo(): lax.ppermute(tail, axis, [(i, (i + 1) % count) for i in range(ends)])  13.3 us
    gather x2, local copies, waits for them, and re-layouts, lift_values(): chosen = flat_prob[frame_rows, point_index]  12.5 us
    all_to_all x1, starting transfers between devices, on_device(): lax.all_to_all(entry_receiver_square[:, 0], 'tile', split_axis=1, concat_...  12 us
    all_to_all x1, starting transfers between devices, on_device(): lax.all_to_all(lifted, 'tile', split_axis=1, concat_axis=1, tiled=True)  9.34 us
    dot_general x9, matrix products, stencil_offsets(): jnp.einsum('fyxo,io->fyxi', window, block_weight, preferred_element_type=...  9.1 us
    dot_general x18, matrix products, stencil_offsets(): jnp.einsum('fyxi,io->fyxo', window, block_weight, preferred_element_type=...  8.8 us
  transfers between devices with their start and end apart: 11, of which 8 were waited for; matrix products, arithmetic and copies ran while one was open for 25% of the time, Pallas kernels for 0%

profile of v1, /device:TPU:1, one launch (start us, length us, event | category | flops | bytes accessed | tf_op | source)
XLA Modules:
  0.0 171.4 jit_solution(11796693682090543151)
XLA Ops:
  0.6 12.0 %all-to-all-start = ((s32[1,32,64]{2,0,1:T(1,128)}), s32[1,32,64]{2,0,1:T(1,128)S(1)}, u32[]{:S(2)}, u32[]{:S(2)}) async-start(s32[1,32,64]{2,0,1:T(1,128)} %bitcast.232), calls=%async_computation | async-start | bytes 32768 | tf_op jit(solution)/shard_map/all_to_all | solution.py:141
  12.7 0.8 reshape_squeeze.3
  13.6 0.8 reduce_max.14
  14.4 0.9 fusion.121
  15.3 0.8 fusion.120
  16.2 12.4 %gather_fusion.1 = f32[2048]{0:T(1024)S(1)} fusion(f32[1,2048]{1,0:T(1,128)S(1)} %reshape.512, s32[2048]{0:T(1024)S(1)} %bitcast.215), kind=kCustom, calls=%fused_computation.1 | custom fusion | bytes 32768 | tf_op jit(solution)/shard_map/gather | solution.py:71
  28.7 8.6 %gather_fusion = bf16[2048,256]{1,0:T(8,128)(2,1)S(1)} fusion(bf16[1,32,256]{2,1,0:T(8,128)(2,1)S(1)} %copy-done, s32[2048]{0:T(1024)S(1)} %bitcast.214), kind=kCustom, calls=%fused_computation | custom fusion | bytes 2113536 | tf_op jit(solution)/shard_map/gather | solution.py:73
  37.4 1.4 fusion.14
  38.8 9.3 %all-to-all-start.1 = ((bf16[1,32,64,256]{3,2,0,1:T(8,128)(2,1)}), bf16[1,32,64,256]{3,2,0,1:T(8,128)(2,1)}, u32[]{:S(2)}, u32[]{:S(2)}) async-start(bf16[1,32,64,256]{3,2,0,1:T(8,128)(2,1)} %fusion.14), calls=%async_computation.1 | async-start | bytes 2097152 | tf_op jit(solution)/shard_map/all_to_all | solution.py:140
  48.2 1.3 collective-permute-start.5
  49.5 4.0 %collective-permute-start.4 = (bf16[1,1,400,256]{3,2,1,0:T(8,128)(2,1)S(1)}, bf16[1,1,400,256]{3,2,1,0:T(8,128)(2,1)S(1)}, u32[]{:S(2)}, u32[]{:S(2)}) collective-permute-start(bf16[1,1,400,256]{3,2,1,0:T(8,128)(2,1)S(1)} %get-tuple-element.106), channel_id=1, source_target_pairs={{0,1},{1,2},{2,3},{3,4},{4,5},{5,6},{6,7},{7,8},{8,9},{9,10},{10,1... | collective-permute-start | bytes 614408 | tf_op jit(solution)/shard_map/ppermute | solution.py:19
  54.0 0.7 reduce.7
  54.8 7.0 %collective-permute-done.5 = bf16[1,1,400,256]{3,2,1,0:T(8,128)(2,1)S(1)} collective-permute-done((bf16[1,1,400,256]{3,2,1,0:T(8,128)(2,1)S(1)}, bf16[1,1,400,256]{3,2,1,0:T(8,128)(2,1)S(1)}, u32[]{:S(2)}, u32[]{:S(2)}) %collective-permute-start.5) | collective-permute-done | bytes 204832 | tf_op jit(solution)/shard_map/ppermute | solution.py:21
  62.0 1.2 fusion.37
  63.2 1.2 convolution_add_fusion.6
  64.4 1.2 convolution_add_fusion.5
  65.6 1.2 convolution_add_fusion.4
  66.9 1.2 convolution_add_fusion.3
  68.1 1.2 convolution_add_fusion.2
  69.3 4.5 %all-to-all-done.1 = bf16[1,32,64,256]{3,2,0,1:T(8,128)(2,1)} async-done(((bf16[1,32,64,256]{3,2,0,1:T(8,128)(2,1)}), bf16[1,32,64,256]{3,2,0,1:T(8,128)(2,1)}, u32[]{:S(2)}, u32[]{:S(2)}) %all-to-all-start.1) | async-done | bytes 1048608 | tf_op jit(solution)/shard_map/all_to_all | solution.py:140
  73.8 6.2 %while.14 = (s32[]{:T(128)}, f32[1,800,256]{2,1,0:T(8,128)S(1)}, s32[1,2048]{1,0:T(1,128)S(1)}, bf16[1,2048,256]{2,1,0:T(8,128)(2,1)}, s32[]{:T(128)}, /*index=5*/s32[]{:T(128)}, s32[]{:T(128)}, s32[]{:T(128)}) while((s32[]{:T(128)}, f32[1,800,256]{2,1,0:T(8,128)S(1)}, s32[1,2048]{1,0:T(1,128)S(1)}, ...), condition=%wide.region_3.4_spmd.clone, body=%wide.region_2.3_spmd.clone.sunk | while | flops 210534400 | bytes 1906845 | solution.py:94
  73.8 1.5 fusion.145
  75.3 1.5 fusion.145
  76.9 1.5 fusion.145
  78.5 1.5 fusion.145
  80.4 1.3 collective-permute-start.1
  81.7 4.6 %collective-permute-start = (bf16[1,1,400,256]{3,2,1,0:T(8,128)(2,1)S(1)}, bf16[1,1,400,256]{3,2,1,0:T(8,128)(2,1)S(1)}, u32[]{:S(2)}, u32[]{:S(2)}) collective-permute-start(bf16[1,1,400,256]{3,2,1,0:T(8,128)(2,1)S(1)} %get-tuple-element.110), channel_id=1, source_target_pairs={{0,1},{1,2},{2,3},{3,4},{4,5},{5,6},{6,7},{7,8},{8,9},{9,10},{10,1... | collective-permute-start | bytes 614408 | tf_op jit(solution)/shard_map/ppermute | solution.py:19
  86.6 0.7 collective-permute-done.1
  87.4 1.6 collective-permute-done
  91.9 1.3 collective-permute-start.3
  93.2 4.8 %collective-permute-start.2 = (bf16[1,1,400,256]{3,2,1,0:T(8,128)(2,1)S(1)}, bf16[1,1,400,256]{3,2,1,0:T(8,128)(2,1)S(1)}, u32[]{:S(2)}, u32[]{:S(2)}) collective-permute-start(bf16[1,1,400,256]{3,2,1,0:T(8,128)(2,1)S(1)} %get-tuple-element.108), channel_id=1, source_target_pairs={{0,1},{1,2},{2,3},{3,4},{4,5},{5,6},{6,7},{7,8},{8,9},{9,10},{10,1... | collective-permute-start | bytes 614408 | tf_op jit(solution)/shard_map/ppermute | solution.py:19
  98.2 0.9 collective-permute-done.3
  99.1 1.5 collective-permute-done.2
  101.4 1.5 convolution_bitcast_fusion
  103.0 5.2 %collective-permute-start.6 = (bf16[2304,128]{1,0:T(8,128)(2,1)S(1)}, bf16[2304,128]{1,0:T(8,128)(2,1)S(1)}, u32[]{:S(2)}, u32[]{:S(2)}) collective-permute-start(bf16[2304,128]{1,0:T(8,128)(2,1)S(1)} %select_convert_fusion), channel_id=1, source_target_pairs={{0,32},{32,0},{64,96},{96,64},{128,160},{160,128},{192,224},{224,1... | collective-permute-start | bytes 1769480 | tf_op jit(solution)/shard_map/ppermute | solution.py:104
  108.1 1.2 fusion.23
  109.7 1.2 convolution_add_fusion.13
  110.9 1.0 add_convert_fusion
  111.8 25.9 %all-to-all-start.2 = ((bf16[32,72,128]{2,1,0:T(8,128)(2,1)}), bf16[32,72,128]{2,1,0:T(8,128)(2,1)}, u32[]{:S(2)}, u32[]{:S(2)}) async-start(bf16[32,72,128]{2,1,0:T(8,128)(2,1)} %bitcast.229), calls=%async_computation.2 | async-start | bytes 1179648 | tf_op jit(solution)/shard_map/all_to_all | solution.py:106
  137.8 1.4 convolution_add_fusion.12
  140.1 1.2 convolution_add_fusion.8
  141.3 14.6 %all-to-all-done.2 = bf16[32,72,128]{2,1,0:T(8,128)(2,1)} async-done(((bf16[32,72,128]{2,1,0:T(8,128)(2,1)}), bf16[32,72,128]{2,1,0:T(8,128)(2,1)}, u32[]{:S(2)}, u32[]{:S(2)}) %all-to-all-start.2) | async-done | bytes 589856 | tf_op jit(solution)/shard_map/all_to_all | solution.py:106
  155.9 1.2 convert_reduce_fusion
  157.0 0.7 broadcast_in_dim.13
  157.8 6.1 %all-to-all-start.3 = ((f32[8,72,128]{2,1,0:T(8,128)}), f32[8,72,128]{2,1,0:T(8,128)S(1)}, u32[]{:S(2)}, u32[]{:S(2)}) async-start(f32[8,72,128]{2,1,0:T(8,128)} %broadcast_in_dim.13), calls=%async_computation.3 | async-start | bytes 589824 | tf_op jit(solution)/shard_map/all_to_all | solution.py:111
  164.2 0.9 copy-done.4
  165.0 1.0 fusion.24
  166.1 4.6 %all-to-all-done.3 = f32[8,72,128]{2,1,0:T(8,128)S(1)} async-done(((f32[8,72,128]{2,1,0:T(8,128)}), f32[8,72,128]{2,1,0:T(8,128)S(1)}, u32[]{:S(2)}, u32[]{:S(2)}) %all-to-all-start.3) | async-done | bytes 294944 | tf_op jit(solution)/shard_map/all_to_all | solution.py:111
  (69 shorter events, 7.9 us)
Async XLA Ops:
  0.6 28.1 %copy-start = (bf16[1,32,256]{2,1,0:T(8,128)(2,1)S(1)}, bf16[1,32,256]{2,1,0:T(8,128)(2,1)}, u32[]{:S(2)}) copy-start(bf16[1,32,256]{2,1,0:T(8,128)(2,1)} %param.10) | copy-start | bytes 49156
  0.6 38.1 %all-to-all-start = ((s32[1,32,64]{2,0,1:T(1,128)}), s32[1,32,64]{2,0,1:T(1,128)S(1)}, u32[]{:S(2)}, u32[]{:S(2)}) async-start(s32[1,32,64]{2,0,1:T(1,128)} %bitcast.232), calls=%async_computation | async-start | bytes 32768 | tf_op jit(solution)/shard_map/all_to_all | solution.py:141
  28.7 8.7 %copy-start.6 = (s32[1,1,32]{2,1,0:T(1,128)S(1)}, s32[1,1,32]{2,1,0:T(1,128)}, u32[]{:S(2)}) copy-start(s32[1,1,32]{2,1,0:T(1,128)} %param.14) | copy-start | bytes 388
  37.4 10.7 %copy-start.1 = (bf16[1,2,400,256]{3,2,1,0:T(8,128)(2,1)S(1)}, bf16[1,2,400,256]{3,2,1,0:T(8,128)(2,1)}, u32[]{:S(2)}) copy-start(bf16[1,2,400,256]{3,2,1,0:T(8,128)(2,1)} %param.15) | copy-start | bytes 1228804
  38.8 35.0 %all-to-all-start.1 = ((bf16[1,32,64,256]{3,2,0,1:T(8,128)(2,1)}), bf16[1,32,64,256]{3,2,0,1:T(8,128)(2,1)}, u32[]{:S(2)}, u32[]{:S(2)}) async-start(bf16[1,32,64,256]{3,2,0,1:T(8,128)(2,1)} %fusion.14), calls=%async_computation.1 | async-start | bytes 2097152 | tf_op jit(solution)/shard_map/all_to_all | solution.py:140
  48.2 13.6 %collective-permute-start.5 = (bf16[1,1,400,256]{3,2,1,0:T(8,128)(2,1)S(1)}, bf16[1,1,400,256]{3,2,1,0:T(8,128)(2,1)S(1)}, u32[]{:S(2)}, u32[]{:S(2)}) collective-permute-start(bf16[1,1,400,256]{3,2,1,0:T(8,128)(2,1)S(1)} %get-tuple-element.107), channel_id=1, source_target_pairs={{1,0},{2,1},{3,2},{4,3},{5,4},{6,5},{7,6},{8,7},{9,8},{10,9},{11,1... | collective-permute-start | bytes 614408 | tf_op jit(solution)/shard_map/ppermute | solution.py:21
  49.5 12.3 %collective-permute-start.4 = (bf16[1,1,400,256]{3,2,1,0:T(8,128)(2,1)S(1)}, bf16[1,1,400,256]{3,2,1,0:T(8,128)(2,1)S(1)}, u32[]{:S(2)}, u32[]{:S(2)}) collective-permute-start(bf16[1,1,400,256]{3,2,1,0:T(8,128)(2,1)S(1)} %get-tuple-element.106), channel_id=1, source_target_pairs={{0,1},{1,2},{2,3},{3,4},{4,5},{5,6},{6,7},{7,8},{8,9},{9,10},{10,1... | collective-permute-start | bytes 614408 | tf_op jit(solution)/shard_map/ppermute | solution.py:19
  80.0 6.3 %copy-start.2 = (bf16[2304,256]{1,0:T(8,128)(2,1)S(1)}, bf16[2304,256]{1,0:T(8,128)(2,1)}, u32[]{:S(2)}) copy-start(bf16[2304,256]{1,0:T(8,128)(2,1)} %param.17) | copy-start | bytes 3538948
  80.4 6.9 %collective-permute-start.1 = (bf16[1,1,400,256]{3,2,1,0:T(8,128)(2,1)S(1)}, bf16[1,1,400,256]{3,2,1,0:T(8,128)(2,1)S(1)}, u32[]{:S(2)}, u32[]{:S(2)}) collective-permute-start(bf16[1,1,400,256]{3,2,1,0:T(8,128)(2,1)S(1)} %get-tuple-element.111), channel_id=1, source_target_pairs={{1,0},{2,1},{3,2},{4,3},{5,4},{6,5},{7,6},{8,7},{9,8},{10,9},{11,1... | collective-permute-start | bytes 614408 | tf_op jit(solution)/shard_map/ppermute | solution.py:21
  81.7 7.5 %copy-start.5 = (bf16[2304,256]{1,0:T(8,128)(2,1)S(1)}, bf16[2304,256]{1,0:T(8,128)(2,1)}, u32[]{:S(2)}) copy-start(bf16[2304,256]{1,0:T(8,128)(2,1)} %param.16) | copy-start | bytes 3538948
  81.7 7.2 %collective-permute-start = (bf16[1,1,400,256]{3,2,1,0:T(8,128)(2,1)S(1)}, bf16[1,1,400,256]{3,2,1,0:T(8,128)(2,1)S(1)}, u32[]{:S(2)}, u32[]{:S(2)}) collective-permute-start(bf16[1,1,400,256]{3,2,1,0:T(8,128)(2,1)S(1)} %get-tuple-element.110), channel_id=1, source_target_pairs={{0,1},{1,2},{2,3},{3,4},{4,5},{5,6},{6,7},{7,8},{8,9},{9,10},{10,1... | collective-permute-start | bytes 614408 | tf_op jit(solution)/shard_map/ppermute | solution.py:19
  91.9 7.3 %collective-permute-start.3 = (bf16[1,1,400,256]{3,2,1,0:T(8,128)(2,1)S(1)}, bf16[1,1,400,256]{3,2,1,0:T(8,128)(2,1)S(1)}, u32[]{:S(2)}, u32[]{:S(2)}) collective-permute-start(bf16[1,1,400,256]{3,2,1,0:T(8,128)(2,1)S(1)} %get-tuple-element.109), channel_id=1, source_target_pairs={{1,0},{2,1},{3,2},{4,3},{5,4},{6,5},{7,6},{8,7},{9,8},{10,9},{11,1... | collective-permute-start | bytes 614408 | tf_op jit(solution)/shard_map/ppermute | solution.py:21
  93.2 7.4 %collective-permute-start.2 = (bf16[1,1,400,256]{3,2,1,0:T(8,128)(2,1)S(1)}, bf16[1,1,400,256]{3,2,1,0:T(8,128)(2,1)S(1)}, u32[]{:S(2)}, u32[]{:S(2)}) collective-permute-start(bf16[1,1,400,256]{3,2,1,0:T(8,128)(2,1)S(1)} %get-tuple-element.108), channel_id=1, source_target_pairs={{0,1},{1,2},{2,3},{3,4},{4,5},{5,6},{6,7},{7,8},{8,9},{9,10},{10,1... | collective-permute-start | bytes 614408 | tf_op jit(solution)/shard_map/ppermute | solution.py:19
  103.0 7.9 %collective-permute-start.6 = (bf16[2304,128]{1,0:T(8,128)(2,1)S(1)}, bf16[2304,128]{1,0:T(8,128)(2,1)S(1)}, u32[]{:S(2)}, u32[]{:S(2)}) collective-permute-start(bf16[2304,128]{1,0:T(8,128)(2,1)S(1)} %select_convert_fusion), channel_id=1, source_target_pairs={{0,32},{32,0},{64,96},{96,64},{128,160},{160,128},{192,224},{224,1... | collective-permute-start | bytes 1769480 | tf_op jit(solution)/shard_map/ppermute | solution.py:104
  110.8 27.0 %copy-start.3 = (bf16[2304,256]{1,0:T(8,128)(2,1)S(1)}, bf16[2304,256]{1,0:T(8,128)(2,1)}, u32[]{:S(2)}) copy-start(bf16[2304,256]{1,0:T(8,128)(2,1)} %param.17) | copy-start | bytes 3538948
  111.8 44.0 %all-to-all-start.2 = ((bf16[32,72,128]{2,1,0:T(8,128)(2,1)}), bf16[32,72,128]{2,1,0:T(8,128)(2,1)}, u32[]{:S(2)}, u32[]{:S(2)}) async-start(bf16[32,72,128]{2,1,0:T(8,128)(2,1)} %bitcast.229), calls=%async_computation.2 | async-start | bytes 1179648 | tf_op jit(solution)/shard_map/all_to_all | solution.py:106
  157.8 12.9 %all-to-all-start.3 = ((f32[8,72,128]{2,1,0:T(8,128)}), f32[8,72,128]{2,1,0:T(8,128)S(1)}, u32[]{:S(2)}, u32[]{:S(2)}) async-start(f32[8,72,128]{2,1,0:T(8,128)} %broadcast_in_dim.13), calls=%async_computation.3 | async-start | bytes 589824 | tf_op jit(solution)/shard_map/all_to_all | solution.py:111
  163.9 1.1 copy-start.4

commit v2 on v1

v2 whole, which is shorter than its diff:
```python
import functools
import math

import jax
import jax.numpy as jnp
from jax import lax
from jax.experimental import pallas as pl
from jax.experimental.pallas import tpu as pltpu
from jax.sharding import PartitionSpec as P

epsilon = 1e-05

F32 = jnp.float32
BF16 = jnp.bfloat16
LANES = 128
META_ROWS = 8
FINE = 16
VMEM_LIMIT = 48 * 1024 * 1024


def params():
    return pltpu.CompilerParams(vmem_limit_bytes=VMEM_LIMIT)


def vmem():
    return pl.BlockSpec(memory_space=pltpu.VMEM)


def turned(values, shift):
    return pltpu.roll(values, shift % values.shape[0], 0)


def pack_kernel(features, scores, points, cells, counts, message, meta):
    pixels, bins = scores.shape
    strips, slots = points.shape
    logits = scores[...].astype(F32)
    grown = jnp.exp(logits - jnp.max(logits, axis=1, keepdims=True))
    prob = grown / jnp.sum(grown, axis=1, keepdims=True)
    blank = jnp.zeros((pixels, LANES - bins), F32)
    prob = jnp.concatenate([prob, blank], axis=1)
    unused = jnp.zeros((strips, LANES - slots), jnp.int32)
    point = jnp.concatenate([points[...], unused], axis=1)
    cell = jnp.concatenate([cells[...], unused], axis=1)
    bin_index = point % bins
    pixel = point // bins
    weight = jnp.zeros((strips, LANES), F32)
    for p in range(pixels):
        row = jnp.broadcast_to(prob[p : p + 1], (strips, LANES))
        weight = jnp.where(pixel == p, jnp.take_along_axis(row, bin_index, axis=1), weight)
    across = lax.broadcasted_iota(jnp.int32, (strips, strips), 1)
    down = lax.broadcasted_iota(jnp.int32, (strips, strips), 0)
    tally = jnp.sum(
        jnp.where(across == down, counts[...].astype(F32), 0.0), axis=1, keepdims=True
    )
    lane = lax.broadcasted_iota(jnp.int32, (strips, LANES), 1)
    weight = jnp.where(lane.astype(F32) < tally, weight, 0.0)
    coarse = weight.astype(BF16).astype(F32)
    fields = (coarse, weight - coarse, pixel.astype(F32), (cell // FINE).astype(F32), (cell % FINE).astype(F32))
    meta[...] = jnp.zeros_like(meta)
    strip = lax.broadcasted_iota(jnp.int32, (strips, LANES), 0)
    for r, field in enumerate(fields):
        before = jnp.where(strip == 0, 0.0, turned(field, 1))
        after = jnp.where(strip == strips - 1, 0.0, turned(field, -1))
        here = pltpu.roll(field, slots, 1)
        meta[:, r, :LANES] = jnp.where(lane < slots, before, here)
        meta[:, r, LANES:] = jnp.where(lane < slots, after, 0.0)

    @pl.loop(0, strips)
    def _(t):
        message[t, :pixels] = features[...]
        message[t, pixels:] = meta[t].astype(BF16)


def splat_kernel(arrived, bev, meta, lifted, onehot):
    sources, rows, planes = arrived.shape
    pixels = rows - META_ROWS
    slots = LANES // 2
    wide = bev.shape[1]
    breadth = onehot.shape[0]
    lane = lax.broadcasted_iota(jnp.int32, (META_ROWS, LANES), 1)
    for j in range(sources // 2):
        first = arrived[2 * j, pixels:].astype(F32)
        second = arrived[2 * j + 1, pixels:].astype(F32)
        at = slice(j * LANES, (j + 1) * LANES)
        low = lane < slots
        a0, a1 = first[:, :LANES], first[:, LANES:]
        b0, b1 = second[:, :LANES], second[:, LANES:]
        meta[0, :, at] = jnp.where(low, a0, pltpu.roll(b0, slots, 1))
        meta[1, :, at] = jnp.where(low, pltpu.roll(a0, slots, 1), b0)
        meta[2, :, at] = jnp.where(low, a1, pltpu.roll(b1, slots, 1))
    batch = 4
    span = batch * slots
    depth = batch * pixels
    home = (lax.broadcasted_iota(jnp.int32, (1, span), 1) // slots * pixels).astype(F32)
    order = lax.broadcasted_iota(jnp.int32, (depth, span), 0).astype(F32)
    for g in range(sources // batch):
        block = jnp.concatenate([arrived[batch * g + i, :pixels] for i in range(batch)], axis=0)
        turned_block = block.astype(F32).T.astype(BF16)
        twice = jnp.concatenate([turned_block, turned_block], axis=1)
        at = slice(g * span, (g + 1) * span)
        for s in range(3):
            match = order == meta[s, 2:3, at] + home
            coarse = jnp.where(match, meta[s, 0:1, at], 0.0).astype(BF16)
            rest = jnp.where(match, meta[s, 1:2, at], 0.0).astype(BF16)
            lifted[s, :, at] = jnp.dot(
                twice, jnp.concatenate([coarse, rest], axis=0), preferred_element_type=F32
            ).astype(BF16)
    total = sources * slots
    fine = lax.broadcasted_iota(jnp.int32, (FINE, total), 0).astype(F32)
    blocks = breadth // FINE

    @pl.loop(0, 6)
    def _(k):
        s = k // 2
        begin = (k % 2 * blocks).astype(F32)
        comb = jnp.where(fine == meta[s, 4:5, :], 1.0, 0.0).astype(BF16)
        coarse = meta[s, 3:4, :]
        for b in range(blocks):
            chosen = jnp.where(coarse == begin + b, 1.0, 0.0).astype(BF16)
            onehot[b * FINE : (b + 1) * FINE, :] = comb * chosen
        summed = lax.dot_general(
            onehot[...], lifted[s], (((1,), (1,)), ((), ())), preferred_element_type=F32
        )
        factor = lax.rsqrt(jnp.mean(summed * summed, axis=1, keepdims=True) + epsilon)
        bev[k, :breadth] = (summed * factor).astype(BF16)
        bev[k, breadth:] = jnp.zeros((wide - breadth, planes), BF16)


def wide_weight(weight, planes):
    return jnp.concatenate(
        [
            jnp.concatenate(
                [weight[(a * 3 + b) * planes : (a * 3 + b + 1) * planes] for b in range(3)], axis=1
            )
            for a in range(3)
        ],
        axis=0,
    )


def conv_row(field, k, weight):
    planes = field.shape[2]
    stacked = jnp.concatenate([field[k - 1], field[k], field[k + 1]], axis=1)
    product = jnp.dot(stacked, weight, preferred_element_type=F32)
    return (
        product[:, planes : 2 * planes]
        + turned(product[:, :planes], 1)
        + turned(product[:, 2 * planes :], -1)
    )


def inside(shape, breadth):
    return lax.broadcasted_iota(jnp.int32, shape, 0) < breadth


def adjoint_kernel(breadth, own, above, below, weight, shifted, back):
    wide, planes = back.shape[1:]
    filler = jnp.zeros((wide - breadth, planes), F32)
    for k in range(4):
        row = (above[...], own[0], own[1], below[...])[k]
        row = jnp.concatenate([row.astype(F32), filler], axis=0)
        for b in range(3):
            shifted[b, k] = turned(row, b - 1).astype(BF16)
    flipped = jnp.concatenate(
        [weight[tap * planes : (tap + 1) * planes] for tap in range(9)], axis=1
    )
    for y in range(2):
        stacked = jnp.concatenate(
            [shifted[b, y + 2 - a] for a in range(3) for b in range(3)], axis=1
        )
        back[y] = lax.dot_general(
            stacked, flipped, (((1,), (1,)), ((), ())), preferred_element_type=F32
        )


def hidden_kernel(breadth, bev, weight, shifted, pre, hidden, kept, given):
    wide, planes = bev.shape[1:]
    grid = wide_weight(weight, planes)
    for y in range(2):
        value = conv_row(bev, y + 2, grid)
        pre[y] = value
        active = value * jax.nn.sigmoid(value)
        hidden[y] = jnp.where(inside(value.shape, breadth), active, 0.0).astype(BF16)
    turned_hidden = hidden[...].reshape(2 * wide, planes).astype(F32).T.astype(BF16)
    odd = lax.axis_index("dp") % 2 == 1
    half = planes // 2
    for a in range(3):
        for b in range(3):
            cotangent = shifted[b, 2 - a : 4 - a].reshape(2 * wide, planes)
            term = jnp.dot(turned_hidden, cotangent, preferred_element_type=F32)
            left, right = term[:, :half], term[:, half:]
            at = slice((a * 3 + b) * planes, (a * 3 + b + 1) * planes)
            kept[at] = jnp.where(odd, right, left)
            given[at] = jnp.where(odd, left, right).astype(BF16)


def outputs_kernel(breadth, bev, pre, hidden, back, first, second, scene, derivative, latent):
    wide, planes = bev.shape[1:]
    strip = lax.axis_index("tile")
    last = lax.axis_size("tile") - 1
    grid = wide_weight(first, planes)
    mask = inside((wide, planes), breadth)
    for k, edge in ((0, 0), (3, last)):
        value = conv_row(bev, k + 1, grid)
        active = value * jax.nn.sigmoid(value)
        keep = jnp.logical_and(mask, strip != edge)
        latent[k] = jnp.where(keep, active, 0.0).astype(BF16)
    latent[1] = hidden[0]
    latent[2] = hidden[1]
    grid = wide_weight(second, planes)
    for y in range(2):
        value = conv_row(latent, y + 1, grid)
        scene[y] = (bev[y + 2, :breadth].astype(F32) + value[:breadth]).astype(BF16)
        value = pre[y, :breadth]
        sigma = jax.nn.sigmoid(value)
        slope = sigma * (1.0 + value * (1.0 - sigma))
        derivative[y] = (back[y, :breadth] * slope).astype(BF16)


def reduced_gradient(kept, given, tile_count):
    dp_count = lax.axis_size("dp")
    rows, half = kept.shape
    share_rows = rows // tile_count
    taken = lax.ppermute(given, "dp", [(i, i ^ 1) for i in range(dp_count)])
    pair_sum = (kept + taken.astype(F32)).astype(BF16)
    shares = lax.all_to_all(
        pair_sum.reshape(tile_count, share_rows, half), "tile", 0, 0, tiled=True
    )
    own_share = jnp.sum(shares.astype(F32), axis=0)
    copies = jnp.broadcast_to(own_share[None], (dp_count, share_rows, half))
    dp_shares = lax.all_to_all(copies, "dp", 0, 0, tiled=True)
    whole = jnp.sum(dp_shares.reshape(dp_count // 2, 2, share_rows, half), axis=0)
    return jnp.concatenate([whole[0], whole[1]], axis=1)


def on_device(
    image_descriptors,
    image_distance_scores,
    entry_sender_location,
    entry_receiver_square,
    entry_valid_tally,
    predicted_adjoint,
    initial_plane_filter,
    predictor_filter,
):
    _, height, breadth, planes = predicted_adjoint.shape
    pixels = image_descriptors.shape[1]
    strips, slots = entry_sender_location.shape[2:]
    wide = breadth // 16 * 16 + 16
    taps = predictor_filter.shape[0]
    half = planes // 2
    struct = jax.ShapeDtypeStruct

    message = pl.pallas_call(
        pack_kernel,
        out_shape=struct((strips, pixels + META_ROWS, planes), BF16),
        in_specs=[vmem()] * 5,
        out_specs=vmem(),
        scratch_shapes=[pltpu.VMEM((strips, META_ROWS, planes), F32)],
        compiler_params=params(),
        name="pack",
    )(
        image_descriptors[0],
        image_distance_scores[0],
        entry_sender_location[0, 0],
        entry_receiver_square[0, 0],
        entry_valid_tally[0],
    )
    arrived = lax.all_to_all(message, "tile", 0, 0, tiled=True)

    own = predicted_adjoint[0]
    ends = strips - 1
    above = lax.ppermute(own[height - 1], "tile", [(i, i + 1) for i in range(ends)])
    below = lax.ppermute(own[0], "tile", [(i + 1, i) for i in range(ends)])
    shifted, back = pl.pallas_call(
        functools.partial(adjoint_kernel, breadth),
        out_shape=(struct((3, 4, wide, planes), BF16), struct((2, wide, planes), F32)),
        in_specs=[vmem()] * 4,
        out_specs=(vmem(), vmem()),
        compiler_params=params(),
        cost_estimate=pl.CostEstimate(flops=2 * 2 * wide * taps * planes, bytes_accessed=10**7, transcendentals=0),
        name="adjoint",
    )(own, above, below, predictor_filter)

    bev = pl.pallas_call(
        splat_kernel,
        out_shape=struct((6, wide, planes), BF16),
        in_specs=[vmem()],
        out_specs=vmem(),
        scratch_shapes=[
            pltpu.VMEM((3, META_ROWS, strips * slots), F32),
            pltpu.VMEM((3, planes, strips * slots), BF16),
            pltpu.VMEM((breadth, strips * slots), BF16),
        ],
        compiler_params=params(),
        name="splat",
    )(arrived)
    pre, hidden, kept, given = pl.pallas_call(
        functools.partial(hidden_kernel, breadth),
        out_shape=(
            struct((2, wide, planes), F32),
            struct((2, wide, planes), BF16),
            struct((taps, half), F32),
            struct((taps, half), BF16),
        ),
        in_specs=[vmem()] * 3,
        out_specs=(vmem(),) * 4,
        compiler_params=params(),
        name="hidden",
    )(bev, initial_plane_filter, shifted)
    scene, derivative = pl.pallas_call(
        functools.partial(outputs_kernel, breadth),
        out_shape=(struct((2, breadth, planes), BF16),) * 2,
        in_specs=[vmem()] * 6,
        out_specs=(vmem(),) * 2,
        scratch_shapes=[pltpu.VMEM((4, wide, planes), BF16)],
        compiler_params=params(),
        cost_estimate=pl.CostEstimate(flops=4 * 2 * wide * taps * planes, bytes_accessed=10**7, transcendentals=10**6),
        name="outputs",
    )(bev, pre, hidden, back, initial_plane_filter, predictor_filter)
    gradient = reduced_gradient(kept, given, strips)
    square_tally = lax.axis_size("dp") * height * strips * breadth
    return scene[None], derivative[None], gradient / math.sqrt(square_tally)


def solution(mesh):
    placed = (
        P("dp", "tile", None),
        P("dp", "tile", None),
        P("dp", "tile", None, None),
        P("dp", "tile", None, None),
        P("dp", "tile", None),
        P("dp", "tile", None, None),
        P(),
        P(),
    )
    return jax.shard_map(
        on_device,
        mesh=mesh,
        in_specs=placed,
        out_specs=(P("dp", "tile", None, None), P("dp", "tile", None, None), P("tile", None)),
        check_vma=False,
    )
```

time: 173 us -> 95.9 us (0.55)
  starting transfers between devices: 75.8 us -> 27 us
  blocking collectives: 0 us -> 28.9 us
  matrix products: 25.4 us -> 0 us
  waiting for transfers between devices: 35.4 us -> 11.4 us
  Pallas kernels: 0 us -> 16 us
  local copies, waits for them, and re-layouts: 24.8 us -> 10.3 us
  other arithmetic: 8.71 us -> 0.87 us
    all_to_all x3 -> x1, starting transfers between devices: 47.3 us -> 12.2 us  [on_device(): arrived = lax.all_to_all(message, 'tile', 0, 0, tiled=True)]
    all_to_all x0 -> x1, blocking collectives: none -> 28.9 us  [reduced_gradient(): lax.all_to_all(pair_sum.reshape(tile_count, share_rows, half), 'tile', 0,...]
    dot_general x32 -> x0, matrix products: 25.4 us -> none  [the longest x9 9.1 us: stencil_offsets(): jnp.einsum('fyxo,io->fyxi', window, block_weight, preferred_element_type=...]
    gather x3 -> x0, local copies, waits for them, and re-layouts: 21.1 us -> none  [the longest x2 12.5 us: lift_values(): chosen = flat_prob[frame_rows, point_index]]
    pallas_call x0 -> x5, Pallas kernels: none -> 16 us  [the longest x1 5.41 us: on_device(): pl.pallas_call(splat_kernel, out_shape=struct((6, wide, planes), BF16), i...]
    all_to_all x3 -> x1, waiting for transfers between devices: 19.1 us -> 3.69 us  [on_device(): arrived = lax.all_to_all(message, 'tile', 0, 0, tiled=True)]
    ppermute x6 -> x2, starting transfers between devices: 17.2 us -> 5.29 us  [the longest x1 4 us: on_device(): lax.ppermute(own[height - 1], 'tile', [(i, i + 1) for i in range(ends)])]
    unnamed x20 -> x28, local copies, waits for them, and re-layouts: 1.21 us -> 9.51 us
  transfers between devices with their start and end apart: 11 -> 5, of which waited for: 8 -> 3; matrix products, arithmetic and copies ran while one was open for 25% -> 0% of each run, Pallas kernels for 0% -> 5%
where the time goes in v2:
time: 95.9 us; the launch traced here: 95.2 us
  blocking collectives  28.9 us (30%)
  starting transfers between devices  27 us (28%)
  Pallas kernels  16 us (17%)
  waiting for transfers between devices  11.4 us (12%)
  local copies, waits for them, and re-layouts  10.3 us (11%)
    all_to_all x1, blocking collectives, reduced_gradient(): lax.all_to_all(pair_sum.reshape(tile_count, share_rows, half), 'tile', 0,...  28.9 us
    all_to_all x1, starting transfers between devices, on_device(): arrived = lax.all_to_all(message, 'tile', 0, 0, tiled=True)  12.2 us
    unnamed x28, local copies, waits for them, and re-layouts  9.51 us
    all_to_all x1, starting transfers between devices, reduced_gradient(): dp_shares = lax.all_to_all(copies, 'dp', 0, 0, tiled=True)  6.65 us
    ppermute x1, waiting for transfers between devices, on_device(): below = lax.ppermute(own[0], 'tile', [(i + 1, i) for i in range(ends)])  6.05 us
    pallas_call x1, Pallas kernels, on_device(): pl.pallas_call(splat_kernel, out_shape=struct((6, wide, planes), BF16), i...  5.41 us
    pallas_call x1, Pallas kernels, on_device(): pl.pallas_call(functools.partial(hidden_kernel, breadth), out_shape=(stru...  4.38 us
    ppermute x1, starting transfers between devices, on_device(): lax.ppermute(own[height - 1], 'tile', [(i, i + 1) for i in range(ends)])  4 us
  transfers between devices with their start and end apart: 5, of which 3 were waited for; matrix products, arithmetic and copies ran while one was open for 0% of the time, Pallas kernels for 5%

profile of v2, /device:TPU:1, one launch (start us, length us, event | category | flops | bytes accessed | tf_op | source)
XLA Modules:
  0.0 95.2 jit_solution(6414129049881171549)
XLA Ops:
  0.6 0.0 copy-start.2
  0.6 0.0 copy-start.3
  0.7 0.8 copy-done.3
  1.4 0.0 copy-start.4
  1.4 0.7 copy-done.4
  2.1 0.0 copy-start.5
  2.1 0.7 copy-done.5
  2.8 0.0 copy-start.6
  2.8 0.7 copy-done.6
  3.5 0.0 copy-start.7
  3.5 0.7 copy-done.7
  4.2 1.7 %pack.1 = bf16[32,40,256]{2,1,0:T(8,128)(2,1)} custom-call(bf16[32,256]{1,0:T(8,128)(2,1)S(1)} %bitcast.19, bf16[32,64]{1,0:T(8,128)(2,1)S(1)} %bitcast.22, s32[32,64]{1,0:T(8,128)S(1)} %bitcast.20, s32[32,64]{1,0:T(8,128)S(1)} %bitcast.21, s32[1,32]{1,0:T(1,128)S(1)} %bitcast.23), custom_call_target="tpu_custom_call" | custom-call | tf_op jit(solution)/shard_map/pack/pallas_call | solution.py:254
  5.9 0.0 copy-start.8
  5.9 12.2 %all-to-all-start = ((bf16[32,40,256]{2,1,0:T(8,128)(2,1)}), bf16[32,40,256]{2,1,0:T(8,128)(2,1)S(1)}, u32[]{:S(2)}, u32[]{:S(2)}) async-start(bf16[32,40,256]{2,1,0:T(8,128)(2,1)} %pack.1), calls=%async_computation | async-start | bytes 1310720 | tf_op jit(solution)/shard_map/all_to_all | solution.py:269
  18.1 0.0 copy-done.2
  18.2 1.3 %collective-permute-start.1 = (bf16[400,256]{1,0:T(8,128)(2,1)S(1)}, bf16[400,256]{1,0:T(8,128)(2,1)S(1)}, u32[]{:S(2)}, u32[]{:S(2)}) collective-permute-start(bf16[400,256]{1,0:T(8,128)(2,1)S(1)} %get-tuple-element.19), channel_id=1, source_target_pairs={{1,0},{2,1},{3,2},{4,3},{5,4},{6,5},{7,6},{8,7},{9,8},{10,9},{11,1... | collective-permute-start | bytes 614408 | tf_op jit(solution)/shard_map/ppermute | solution.py:274
  19.5 4.0 %collective-permute-start = (bf16[400,256]{1,0:T(8,128)(2,1)S(1)}, bf16[400,256]{1,0:T(8,128)(2,1)S(1)}, u32[]{:S(2)}, u32[]{:S(2)}) collective-permute-start(bf16[400,256]{1,0:T(8,128)(2,1)S(1)} %get-tuple-element.20), channel_id=1, source_target_pairs={{0,1},{1,2},{2,3},{3,4},{4,5},{5,6},{6,7},{7,8},{8,9},{9,10},{10,1... | collective-permute-start | bytes 614408 | tf_op jit(solution)/shard_map/ppermute | solution.py:273
  23.5 6.0 %collective-permute-done.1.below = bf16[400,256]{1,0:T(8,128)(2,1)S(1)} collective-permute-done((bf16[400,256]{1,0:T(8,128)(2,1)S(1)}, bf16[400,256]{1,0:T(8,128)(2,1)S(1)}, u32[]{:S(2)}, u32[]{:S(2)}) %collective-permute-start.1) | collective-permute-done | bytes 204832 | tf_op jit(solution)/shard_map/ppermute | solution.py:274
  29.5 0.0 collective-permute-done.above
  29.5 0.0 copy-done.8
  29.5 1.2 %adjoint.1 = (bf16[3,4,416,256]{3,2,1,0:T(8,128)(2,1)S(1)}, f32[2,416,256]{2,1,0:T(8,128)S(1)}) custom-call(bf16[2,400,256]{2,1,0:T(8,128)(2,1)S(1)} %bitcast.18, bf16[400,256]{1,0:T(8,128)(2,1)S(1)} %collective-permute-done.above, bf16[400,256]{1,0:T(8,128)(2,1)S(1)} %collective-permute-done.1.below, bf16[2304,256]{1,0:T(8,128)(2,1)S(1)} %copy-done.8), custom_call_target="tpu_custom_call" | custom-call | flops 981467136 | bytes 10000000 | tf_op jit(solution)/shard_map/adjoint/pallas_call | solution.py:275
  30.7 0.0 copy-start
  30.7 1.5 %copy-done = bf16[3,4,416,256]{3,2,1,0:T(8,128)(2,1)} copy-done((bf16[3,4,416,256]{3,2,1,0:T(8,128)(2,1)}, bf16[3,4,416,256]{3,2,1,0:T(8,128)(2,1)S(1)}, u32[]{:S(2)}) %copy-start) | copy-done | bytes 2555928
  32.2 0.0 copy-start.12
  32.2 0.9 copy-done.12
  33.1 0.0 copy-start.1
  33.1 3.7 %all-to-all-done.arrived = bf16[32,40,256]{2,1,0:T(8,128)(2,1)S(1)} async-done(((bf16[32,40,256]{2,1,0:T(8,128)(2,1)}), bf16[32,40,256]{2,1,0:T(8,128)(2,1)S(1)}, u32[]{:S(2)}, u32[]{:S(2)}) %all-to-all-start) | async-done | bytes 655392 | tf_op jit(solution)/shard_map/all_to_all | solution.py:269
  36.8 5.4 %splat.1.bev = bf16[6,416,256]{2,1,0:T(8,128)(2,1)S(1)} custom-call(bf16[32,40,256]{2,1,0:T(8,128)(2,1)S(1)} %all-to-all-done.arrived), custom_call_target="tpu_custom_call" | custom-call | tf_op jit(solution)/shard_map/splat/pallas_call | solution.py:285
  42.2 0.0 copy-done.1
  42.2 4.4 %hidden.1 = (f32[2,416,256]{2,1,0:T(8,128)S(1)}, bf16[2,416,256]{2,1,0:T(8,128)(2,1)S(1)}, f32[2304,128]{1,0:T(8,128)S(1)}, bf16[2304,128]{1,0:T(8,128)(2,1)S(1)}) custom-call(bf16[6,416,256]{2,1,0:T(8,128)(2,1)S(1)} %splat.1.bev, bf16[2304,256]{1,0:T(8,128)(2,1)S(1)} %copy-done.1, bf16[3,4,416,256]{3,2,1,0:T(8,128)(2,1)} %copy-done), custom_call_target="tpu_custom_call" | custom-call | tf_op jit(solution)/shard_map/hidden/pallas_call | solution.py:298
  46.6 0.0 copy-start.10
  46.6 2.9 %collective-permute-start.2 = (bf16[2304,128]{1,0:T(8,128)(2,1)S(1)}, bf16[2304,128]{1,0:T(8,128)(2,1)S(1)}, u32[]{:S(2)}, u32[]{:S(2)}) collective-permute-start(bf16[2304,128]{1,0:T(8,128)(2,1)S(1)} %get-tuple-element.18), channel_id=1, source_target_pairs={{0,32},{32,0},{64,96},{96,64},{128,160},{160,128},{192,224},{224,1... | collective-permute-start | bytes 1769480 | tf_op jit(solution)/shard_map/ppermute | solution.py:224
  49.5 1.6 %collective-permute-done.2 = bf16[2304,128]{1,0:T(8,128)(2,1)S(1)} collective-permute-done((bf16[2304,128]{1,0:T(8,128)(2,1)S(1)}, bf16[2304,128]{1,0:T(8,128)(2,1)S(1)}, u32[]{:S(2)}, u32[]{:S(2)}) %collective-permute-start.2) | collective-permute-done | bytes 589856 | tf_op jit(solution)/shard_map/ppermute | solution.py:224
  51.2 0.1 add_convert_fusion
  51.3 0.0 copy-done.10
  51.3 28.9 %all_to_all.15 = bf16[32,72,128]{2,1,0:T(8,128)(2,1)S(1)} all-to-all(bf16[32,72,128]{2,1,0:T(8,128)(2,1)S(1)} %bitcast.24), channel_id=1, replica_groups=mesh['dp'=8,'tile'=32] {'tile'}, dimensions={0} | all-to-all | bytes 1179648 | tf_op jit(solution)/shard_map/all_to_all | solution.py:226
  80.2 0.1 convert_reduce_fusion
  80.3 0.7 broadcast_in_dim.14
  81.0 6.6 %all-to-all-start.2 = ((f32[8,72,128]{2,1,0:T(8,128)}), f32[8,72,128]{2,1,0:T(8,128)S(1)}, u32[]{:S(2)}, u32[]{:S(2)}) async-start(f32[8,72,128]{2,1,0:T(8,128)} %broadcast_in_dim.14), calls=%async_computation.2 | async-start | bytes 589824 | tf_op jit(solution)/shard_map/all_to_all | solution.py:231
  87.7 0.0 copy-start.9
  87.7 1.3 %copy-done.9 = bf16[2304,256]{1,0:T(8,128)(2,1)S(1)} copy-done((bf16[2304,256]{1,0:T(8,128)(2,1)S(1)}, bf16[2304,256]{1,0:T(8,128)(2,1)}, u32[]{:S(2)}) %copy-start.9) | copy-done | bytes 1179672
  89.0 0.0 copy-start.11
  89.0 1.2 %copy-done.11 = f32[2,416,256]{2,1,0:T(8,128)S(1)} copy-done((f32[2,416,256]{2,1,0:T(8,128)S(1)}, f32[2,416,256]{2,1,0:T(8,128)}, u32[]{:S(2)}) %copy-start.11) | copy-done | bytes 851992
  90.1 0.0 copy-start.13
  90.1 1.2 %copy-done.13 = f32[2,416,256]{2,1,0:T(8,128)S(1)} copy-done((f32[2,416,256]{2,1,0:T(8,128)S(1)}, f32[2,416,256]{2,1,0:T(8,128)}, u32[]{:S(2)}) %copy-start.13) | copy-done | bytes 851992
  91.3 3.2 %outputs.1 = (bf16[2,400,256]{2,1,0:T(8,128)(2,1)}, bf16[2,400,256]{2,1,0:T(8,128)(2,1)}) custom-call(bf16[6,416,256]{2,1,0:T(8,128)(2,1)S(1)} %splat.1.bev, f32[2,416,256]{2,1,0:T(8,128)S(1)} %copy-done.11, bf16[2,416,256]{2,1,0:T(8,128)(2,1)S(1)} %get-tuple-element.13.hidden, f32[2,416,256]{2,1,0:T(8,128)S(1)} %copy-done.13, ...), custom_call_target="tpu_custom_call" | custom-call | flops 1962934272 | bytes 10000000 | tf_op jit(solution)/shard_map/outputs/pallas_call | solution.py:311
  94.5 0.0 all-to-all-done.2
  94.6 0.6 maximum_multiply_fusion
  (3 shorter events, 0.1 us)
Async XLA Ops:
  0.6 17.5 %copy-start.2 = (bf16[1,2,400,256]{3,2,1,0:T(8,128)(2,1)S(1)}, bf16[1,2,400,256]{3,2,1,0:T(8,128)(2,1)}, u32[]{:S(2)}) copy-start(bf16[1,2,400,256]{3,2,1,0:T(8,128)(2,1)} %param.13) | copy-start | bytes 1228804
  0.6 0.8 copy-start.3
  1.4 0.7 copy-start.4
  2.1 0.7 copy-start.5
  2.8 0.7 copy-start.6
  3.5 0.7 copy-start.7
  5.9 23.6 %copy-start.8 = (bf16[2304,256]{1,0:T(8,128)(2,1)S(1)}, bf16[2304,256]{1,0:T(8,128)(2,1)}, u32[]{:S(2)}) copy-start(bf16[2304,256]{1,0:T(8,128)(2,1)} %second.1) | copy-start | bytes 3538948
  5.9 30.9 %all-to-all-start = ((bf16[32,40,256]{2,1,0:T(8,128)(2,1)}), bf16[32,40,256]{2,1,0:T(8,128)(2,1)S(1)}, u32[]{:S(2)}, u32[]{:S(2)}) async-start(bf16[32,40,256]{2,1,0:T(8,128)(2,1)} %pack.1), calls=%async_computation | async-start | bytes 1310720 | tf_op jit(solution)/shard_map/all_to_all | solution.py:269
  18.2 11.4 %collective-permute-start.1 = (bf16[400,256]{1,0:T(8,128)(2,1)S(1)}, bf16[400,256]{1,0:T(8,128)(2,1)S(1)}, u32[]{:S(2)}, u32[]{:S(2)}) collective-permute-start(bf16[400,256]{1,0:T(8,128)(2,1)S(1)} %get-tuple-element.19), channel_id=1, source_target_pairs={{1,0},{2,1},{3,2},{4,3},{5,4},{6,5},{7,6},{8,7},{9,8},{10,9},{11,1... | collective-permute-start | bytes 614408 | tf_op jit(solution)/shard_map/ppermute | solution.py:274
  19.5 10.1 %collective-permute-start = (bf16[400,256]{1,0:T(8,128)(2,1)S(1)}, bf16[400,256]{1,0:T(8,128)(2,1)S(1)}, u32[]{:S(2)}, u32[]{:S(2)}) collective-permute-start(bf16[400,256]{1,0:T(8,128)(2,1)S(1)} %get-tuple-element.20), channel_id=1, source_target_pairs={{0,1},{1,2},{2,3},{3,4},{4,5},{5,6},{6,7},{7,8},{8,9},{9,10},{10,1... | collective-permute-start | bytes 614408 | tf_op jit(solution)/shard_map/ppermute | solution.py:273
  30.7 1.5 %copy-start = (bf16[3,4,416,256]{3,2,1,0:T(8,128)(2,1)}, bf16[3,4,416,256]{3,2,1,0:T(8,128)(2,1)S(1)}, u32[]{:S(2)}) copy-start(bf16[3,4,416,256]{3,2,1,0:T(8,128)(2,1)S(1)} %get-tuple-element.11.shifted) | copy-start | bytes 7667716
  32.2 0.9 copy-start.12
  33.1 9.1 %copy-start.1 = (bf16[2304,256]{1,0:T(8,128)(2,1)S(1)}, bf16[2304,256]{1,0:T(8,128)(2,1)}, u32[]{:S(2)}) copy-start(bf16[2304,256]{1,0:T(8,128)(2,1)} %first.1) | copy-start | bytes 3538948
  46.6 4.7 %copy-start.10 = (f32[2,416,256]{2,1,0:T(8,128)}, f32[2,416,256]{2,1,0:T(8,128)S(1)}, u32[]{:S(2)}) copy-start(f32[2,416,256]{2,1,0:T(8,128)S(1)} %get-tuple-element.12.pre) | copy-start | bytes 2555908
  46.6 4.5 %collective-permute-start.2 = (bf16[2304,128]{1,0:T(8,128)(2,1)S(1)}, bf16[2304,128]{1,0:T(8,128)(2,1)S(1)}, u32[]{:S(2)}, u32[]{:S(2)}) collective-permute-start(bf16[2304,128]{1,0:T(8,128)(2,1)S(1)} %get-tuple-element.18), channel_id=1, source_target_pairs={{0,32},{32,0},{64,96},{96,64},{128,160},{160,128},{192,224},{224,1... | collective-permute-start | bytes 1769480 | tf_op jit(solution)/shard_map/ppermute | solution.py:224
  81.0 13.5 %all-to-all-start.2 = ((f32[8,72,128]{2,1,0:T(8,128)}), f32[8,72,128]{2,1,0:T(8,128)S(1)}, u32[]{:S(2)}, u32[]{:S(2)}) async-start(f32[8,72,128]{2,1,0:T(8,128)} %broadcast_in_dim.14), calls=%async_computation.2 | async-start | bytes 589824 | tf_op jit(solution)/shard_map/all_to_all | solution.py:231
  87.7 1.3 %copy-start.9 = (bf16[2304,256]{1,0:T(8,128)(2,1)S(1)}, bf16[2304,256]{1,0:T(8,128)(2,1)}, u32[]{:S(2)}) copy-start(bf16[2304,256]{1,0:T(8,128)(2,1)} %second.1) | copy-start | bytes 3538948
  89.0 1.2 %copy-start.11 = (f32[2,416,256]{2,1,0:T(8,128)S(1)}, f32[2,416,256]{2,1,0:T(8,128)}, u32[]{:S(2)}) copy-start(f32[2,416,256]{2,1,0:T(8,128)} %copy-done.10) | copy-start | bytes 2555908
  90.1 1.2 %copy-start.13 = (f32[2,416,256]{2,1,0:T(8,128)S(1)}, f32[2,416,256]{2,1,0:T(8,128)}, u32[]{:S(2)}) copy-start(f32[2,416,256]{2,1,0:T(8,128)} %copy-done.12) | copy-start | bytes 2555908

commit v3 on v2

v3 whole, which is shorter than its diff:
```python
import functools
import math

import jax
import jax.numpy as jnp
from jax import lax
from jax.experimental import pallas as pl
from jax.experimental.pallas import tpu as pltpu
from jax.sharding import PartitionSpec as P

epsilon = 1e-05

F32 = jnp.float32
BF16 = jnp.bfloat16
LANES = 128
CODE = 128
FINE = 16


def params(mebibytes):
    return pltpu.CompilerParams(vmem_limit_bytes=mebibytes * 1024 * 1024)


def vmem():
    return pl.BlockSpec(memory_space=pltpu.VMEM)


def turned(values, shift):
    return pltpu.roll(values, shift % values.shape[0], 0)


def pack_kernel(features, scores, points, cells, counts, packed, score_buf, point_buf, cell_buf, count_buf, sems):
    copies = [
        pltpu.make_async_copy(source, target, sems.at[i])
        for i, (source, target) in enumerate(
            (
                (points, point_buf),
                (scores, score_buf),
                (cells, cell_buf),
                (counts, count_buf),
                (features, packed.at[: features.shape[0]]),
            )
        )
    ]
    for copy in copies:
        copy.start()
    for copy in copies:
        copy.wait()
    pixels, bins = scores.shape
    strips, slots = points.shape
    logits = score_buf[...].astype(F32)
    grown = jnp.exp(logits - jnp.max(logits, axis=1, keepdims=True))
    prob = grown / jnp.sum(grown, axis=1, keepdims=True)
    blank = jnp.zeros((pixels, LANES - bins), F32)
    prob = jnp.concatenate([prob, blank], axis=1)
    unused = jnp.zeros((strips, LANES - slots), jnp.int32)
    point = jnp.concatenate([point_buf[...], unused], axis=1)
    cell = jnp.concatenate([cell_buf[...], unused], axis=1)
    bin_index = point % bins
    pixel = point // bins
    weight = jnp.zeros((strips, LANES), F32)
    for p in range(pixels):
        row = jnp.broadcast_to(prob[p : p + 1], (strips, LANES))
        weight = jnp.where(pixel == p, jnp.take_along_axis(row, bin_index, axis=1), weight)
    across = lax.broadcasted_iota(jnp.int32, (strips, strips), 1)
    down = lax.broadcasted_iota(jnp.int32, (strips, strips), 0)
    tally = jnp.sum(
        jnp.where(across == down, count_buf[...].astype(F32), 0.0), axis=1, keepdims=True
    )
    lane = lax.broadcasted_iota(jnp.int32, (strips, LANES), 1)
    low = lane < slots
    weight = jnp.where(lane.astype(F32) < tally, weight, 0.0)
    coarse = weight.astype(BF16).astype(F32)
    upper = (pixel * 8 + cell // CODE).astype(F32)
    under = (cell % CODE).astype(F32)
    weights = jnp.where(low, coarse, pltpu.roll(weight - coarse, slots, 1))
    codes = jnp.where(low, upper, pltpu.roll(under, slots, 1))
    packed[pixels:] = jnp.concatenate([weights, codes], axis=1).astype(BF16)


def line_kernel(*refs):
    sources, messages, lists = refs[:2], refs[2:6], refs[6]
    strips = lax.axis_size("tile")
    plane = lax.axis_index("tile") // 4
    pixels, planes = sources[0].shape[0] - strips, sources[0].shape[1]
    for i in range(2):
        lists[i] = sources[i][pixels:].astype(F32)
    lane = lax.broadcasted_iota(jnp.int32, (1, planes), 1)
    for k in range(4):
        rows = []
        for i in range(2):
            messages[k][i * pixels : (i + 1) * pixels] = sources[i][:pixels]
            for j in range(8):
                wanted = 4 * (plane ^ k) + (j - 1)
                there = jnp.logical_and(wanted >= 0, wanted < strips)
                row = lists[i, pl.ds(jnp.clip(wanted, 0, strips - 1), 1), :]
                rows.append(jnp.where(jnp.logical_or(there, lane >= planes // 2), row, 0.0))
        messages[k][2 * pixels :] = jnp.concatenate(rows, axis=0).astype(BF16)


def strip_kernel(*refs):
    sources, messages, lists = refs[:4], refs[4:8], refs[8]
    pixels, planes = messages[0].shape[0] // 9, messages[0].shape[1]
    own = lax.axis_index("tile") % 4
    for i in range(4):
        lists[i] = sources[i][2 * pixels :].astype(F32)
    for k in range(4):
        rows = []
        for i in range(8):
            begin = i % 2 * pixels
            messages[k][i * pixels : (i + 1) * pixels] = sources[i // 2][begin : begin + pixels]
            for j in range(3):
                rows.append(lists[i // 2, pl.ds(i % 2 * 8 + (own ^ k) + j, 1), :])
        rows.append(jnp.zeros((8, planes), F32))
        messages[k][8 * pixels :] = jnp.concatenate(rows, axis=0).astype(BF16)


def lift(messages, meta, lifted):
    pixels = messages[0].shape[0] // 9
    slots = LANES // 2
    batch = 4
    span = batch * slots
    depth = batch * pixels
    low = lax.broadcasted_iota(jnp.int32, (1, LANES), 1) < slots
    home = (lax.broadcasted_iota(jnp.int32, (1, span), 1) // slots * pixels).astype(F32)
    order = lax.broadcasted_iota(jnp.int32, (depth, span), 0).astype(F32)
    for m, message in enumerate(messages):
        lists = message[8 * pixels :].astype(F32)
        halves = []
        for h in range(2):
            straight = lists[:, h * LANES : (h + 1) * LANES]
            halves.append((straight, pltpu.roll(straight, slots, 1)))
        for g in range(2):
            block = message[g * depth : (g + 1) * depth]
            turned_block = block.astype(F32).T.astype(BF16)
            twice = jnp.concatenate([turned_block, turned_block], axis=1)
            at = slice((2 * m + g) * span, (2 * m + g + 1) * span)
            for s in range(3):
                fields = []
                for straight, rolled in halves:
                    first, second = [], []
                    for p in range(2):
                        r0 = 3 * (batch * g + 2 * p) + s
                        r1 = r0 + 3
                        first.append(jnp.where(low, straight[r0 : r0 + 1], rolled[r1 : r1 + 1]))
                        second.append(jnp.where(low, rolled[r0 : r0 + 1], straight[r1 : r1 + 1]))
                    fields.append(jnp.concatenate(first, axis=1))
                    fields.append(jnp.concatenate(second, axis=1))
                coarse, rest, upper, under = fields
                pixel = jnp.floor(upper * 0.125)
                sixteenths = jnp.floor(under * (1.0 / FINE))
                meta[s, 0:1, at] = (upper - 8.0 * pixel) * (CODE // FINE) + sixteenths
                meta[s, 1:2, at] = under - FINE * sixteenths
                match = order == pixel + home
                coarse = jnp.where(match, coarse, 0.0).astype(BF16)
                rest = jnp.where(match, rest, 0.0).astype(BF16)
                lifted[s, :, at] = jnp.dot(
                    twice, jnp.concatenate([coarse, rest], axis=0), preferred_element_type=F32
                ).astype(BF16)


def splat_row(s, r, meta, lifted, onehot):
    breadth, total = onehot.shape
    blocks = breadth // FINE
    fine = lax.broadcasted_iota(jnp.int32, (FINE, total), 0).astype(F32)
    comb = jnp.where(fine == meta[s, 1:2, :], 1.0, 0.0).astype(BF16)
    coarse = meta[s, 0:1, :]
    begin = r * blocks
    for b in range(blocks):
        chosen = jnp.where(coarse == (begin + b).astype(F32), 1.0, 0.0).astype(BF16)
        onehot[b * FINE : (b + 1) * FINE, :] = comb * chosen
    return lax.dot_general(
        onehot[...], lifted[s], (((1,), (1,)), ((), ())), preferred_element_type=F32
    )


def normalized(summed, bev, k):
    breadth, planes = summed.shape
    wide = bev.shape[1]
    factor = lax.rsqrt(jnp.mean(summed * summed, axis=1, keepdims=True) + epsilon)
    bev[k, :breadth] = (summed * factor).astype(BF16)
    bev[k, breadth:] = jnp.zeros((wide - breadth, planes), BF16)


def plane_kernel(message, partial, meta, lifted, onehot):
    lift([message], meta, lifted)

    @pl.loop(0, 6)
    def _(k):
        partial[k] = splat_row(k // 2, k % 2, meta, lifted, onehot)


def splat_kernel(one, two, three, partial, bev, meta, lifted, onehot):
    lift([one, two, three], meta, lifted)

    @pl.loop(0, 6)
    def _(k):
        normalized(partial[k] + splat_row(k // 2, k % 2, meta, lifted, onehot), bev, k)


def wide_weight(weight, planes):
    return jnp.concatenate(
        [
            jnp.concatenate(
                [weight[(a * 3 + b) * planes : (a * 3 + b + 1) * planes] for b in range(3)], axis=1
            )
            for a in range(3)
        ],
        axis=0,
    )


def conv_row(field, k, weight):
    planes = field.shape[2]
    stacked = jnp.concatenate([field[k - 1], field[k], field[k + 1]], axis=1)
    product = jnp.dot(stacked, weight, preferred_element_type=F32)
    return (
        product[:, planes : 2 * planes]
        + turned(product[:, :planes], 1)
        + turned(product[:, 2 * planes :], -1)
    )


def inside(shape, breadth):
    return lax.broadcasted_iota(jnp.int32, shape, 0) < breadth


def moved_kernel(breadth, own, shifted):
    wide = shifted.shape[1]
    planes = own.shape[2]
    filler = jnp.zeros((wide - breadth, planes), F32)
    for y in range(2):
        row = jnp.concatenate([own[y].astype(F32), filler], axis=0)
        for b in range(3):
            shifted[y, :, b * planes : (b + 1) * planes] = turned(row, b - 1).astype(BF16)


def hidden_kernel(breadth, bev, weight, shifted, pre, hidden, kept, given):
    wide, planes = bev.shape[1:]
    strip = lax.axis_index("tile")
    last = lax.axis_size("tile") - 1
    odd = lax.axis_index("dp") % 2 == 1
    half = planes // 2
    grid = wide_weight(weight, planes)
    mask = inside((wide, planes), breadth)
    columns = []
    for k in range(4):
        value = conv_row(bev, k + 1, grid)
        if k in (1, 2):
            pre[k - 1] = value
        keep = mask
        if k == 0:
            keep = jnp.logical_and(mask, strip != 0)
        if k == 3:
            keep = jnp.logical_and(mask, strip != last)
        active = jnp.where(keep, value * jax.nn.sigmoid(value), 0.0)
        hidden[k] = active.astype(BF16)
        columns.append(active.T.astype(BF16))
    for a in range(3):
        terms = jnp.dot(columns[a], shifted[0], preferred_element_type=F32)
        terms = terms + jnp.dot(columns[a + 1], shifted[1], preferred_element_type=F32)
        for b in range(3):
            left = terms[:, b * planes : b * planes + half]
            right = terms[:, b * planes + half : (b + 1) * planes]
            at = slice((a * 3 + b) * planes, (a * 3 + b + 1) * planes)
            kept[at] = jnp.where(odd, right, left)
            given[at] = jnp.where(odd, left, right).astype(BF16)


def scene_kernel(breadth, bev, hidden, weight, scene):
    grid = wide_weight(weight, bev.shape[2])
    for y in range(2):
        value = conv_row(hidden, y + 1, grid)
        scene[y] = (bev[y + 2, :breadth].astype(F32) + value[:breadth]).astype(BF16)


def derivative_kernel(breadth, own, first, second, weight, pre, derivative, field):
    wide, planes = pre.shape[1:]
    strip = lax.axis_index("tile")
    odd = strip % 2 == 1
    blank = jnp.zeros((wide - breadth, planes), BF16)
    zero = jnp.zeros((breadth, planes), BF16)
    above = jnp.where(odd, first[...], jnp.where(strip == 0, zero, second[...]))
    below = jnp.where(
        odd, jnp.where(strip == lax.axis_size("tile") - 1, zero, second[...]), first[...]
    )
    for k, row in enumerate((above, own[0], own[1], below)):
        field[k, :breadth] = row
        field[k, breadth:] = blank
    flipped = jnp.concatenate(
        [
            jnp.concatenate(
                [weight[(a * 3 + b) * planes : (a * 3 + b + 1) * planes] for a in (2, 1, 0)], axis=1
            )
            for b in (2, 1, 0)
        ],
        axis=0,
    )
    for y in range(2):
        stacked = jnp.concatenate([field[y], field[y + 1], field[y + 2]], axis=1)
        product = lax.dot_general(
            stacked, flipped, (((1,), (1,)), ((), ())), preferred_element_type=F32
        )
        back = (
            product[:, planes : 2 * planes]
            + turned(product[:, :planes], 1)
            + turned(product[:, 2 * planes :], -1)
        )
        value = pre[y, :breadth]
        sigma = jax.nn.sigmoid(value)
        slope = sigma * (1.0 + value * (1.0 - sigma))
        derivative[y] = (back[:breadth] * slope).astype(BF16)


def parts_kernel(kept, taken, *parts):
    own = lax.axis_index("tile") % 4
    for p in range(kept.shape[0] // 4):
        for k in range(4):
            t = 4 * p + (own ^ k)
            parts[k][p] = (kept[t] + taken[t].astype(F32)).astype(parts[k].dtype)


def planes_kernel(first, one, two, three, *parts):
    plane = lax.axis_index("tile") // 4
    for k in range(4):
        for i, p in enumerate((plane ^ k, 7 - (plane ^ k))):
            total = first[p] + one[p].astype(F32) + two[p].astype(F32) + three[p].astype(F32)
            parts[k][i] = total.astype(parts[k].dtype)


def swap(values, axis, partner):
    return lax.ppermute(values, axis, [(i, partner(i)) for i in range(lax.axis_size(axis))])


def line_swap(k):
    return lambda i: i ^ k


def mirror(i):
    return 28 - i // 4 * 4 + i % 4


def added(first, *others):
    for other in others:
        first = first + other.astype(F32)
    return first


def on_device(
    image_descriptors,
    image_distance_scores,
    entry_sender_location,
    entry_receiver_square,
    entry_valid_tally,
    predicted_adjoint,
    initial_plane_filter,
    predictor_filter,
):
    _, height, breadth, planes = predicted_adjoint.shape
    pixels = image_descriptors.shape[1]
    strips, slots = entry_sender_location.shape[2:]
    wide = breadth // 16 * 16 + 16
    taps = predictor_filter.shape[0]
    half = planes // 2
    struct = jax.ShapeDtypeStruct

    places = pixels + strips
    packed = pl.pallas_call(
        pack_kernel,
        out_shape=struct((places, planes), BF16),
        in_specs=[pl.BlockSpec(memory_space=pl.ANY)] * 5,
        out_specs=vmem(),
        scratch_shapes=[
            pltpu.VMEM((pixels, image_distance_scores.shape[2]), BF16),
            pltpu.VMEM((strips, slots), jnp.int32),
            pltpu.VMEM((strips, slots), jnp.int32),
            pltpu.VMEM((1, strips), jnp.int32),
            pltpu.SemaphoreType.DMA((5,)),
        ],
        compiler_params=params(60),
        name="pack",
    )(
        image_descriptors[0],
        image_distance_scores[0],
        entry_sender_location[0, 0],
        entry_receiver_square[0, 0],
        entry_valid_tally[0],
    )
    line = pl.pallas_call(
        line_kernel,
        out_shape=(struct((2 * pixels + 16, planes), BF16),) * 4,
        in_specs=[vmem()] * 2,
        out_specs=(vmem(),) * 4,
        scratch_shapes=[pltpu.VMEM((2, strips, planes), F32)],
        compiler_params=params(4),
        name="line",
    )(packed, swap(packed, "tile", mirror))
    line = [line[0]] + [swap(line[k], "tile", line_swap(4 * k)) for k in (1, 2, 3)]
    messages = pl.pallas_call(
        strip_kernel,
        out_shape=(struct((9 * pixels, planes), BF16),) * 4,
        in_specs=[vmem()] * 4,
        out_specs=(vmem(),) * 4,
        scratch_shapes=[pltpu.VMEM((4, 16, planes), F32)],
        compiler_params=params(4),
        name="strip",
    )(*line)
    arrived = [swap(messages[k], "tile", line_swap(k)) for k in (1, 2, 3)]

    own = predicted_adjoint[0]
    shifted = pl.pallas_call(
        functools.partial(moved_kernel, breadth),
        out_shape=struct((2, wide, 3 * planes), BF16),
        in_specs=[vmem()],
        out_specs=vmem(),
        compiler_params=params(8),
        cost_estimate=pl.CostEstimate(flops=10**6, bytes_accessed=10**6, transcendentals=0),
        name="moved",
    )(own)

    def splat_scratch(count):
        total = count * 8 * slots
        return [
            pltpu.VMEM((3, 8, total), F32),
            pltpu.VMEM((3, planes, total), BF16),
            pltpu.VMEM((breadth, total), BF16),
        ]

    partial = pl.pallas_call(
        plane_kernel,
        out_shape=struct((6, breadth, planes), F32),
        in_specs=[vmem()],
        out_specs=vmem(),
        scratch_shapes=splat_scratch(1),
        compiler_params=params(16),
        cost_estimate=pl.CostEstimate(flops=2 * 6 * breadth * 8 * slots * planes, bytes_accessed=10**6, transcendentals=0),
        name="plane",
    )(messages[0])
    bev = pl.pallas_call(
        splat_kernel,
        out_shape=struct((6, wide, planes), BF16),
        in_specs=[vmem()] * 4,
        out_specs=vmem(),
        scratch_shapes=splat_scratch(3),
        compiler_params=params(20),
        name="splat",
    )(*arrived, partial)
    pre, hidden, kept, given = pl.pallas_call(
        functools.partial(hidden_kernel, breadth),
        out_shape=(
            struct((2, wide, planes), F32),
            struct((4, wide, planes), BF16),
            struct((taps, half), F32),
            struct((taps, half), BF16),
        ),
        in_specs=[vmem()] * 3,
        out_specs=(vmem(),) * 4,
        compiler_params=params(20),
        name="hidden",
    )(bev, initial_plane_filter, shifted)

    share = taps // strips
    taken = swap(given, "dp", line_swap(1))
    parts = pl.pallas_call(
        parts_kernel,
        out_shape=tuple(struct((strips // 4, share, half), F32 if k == 0 else BF16) for k in range(4)),
        in_specs=[vmem()] * 2,
        out_specs=(vmem(),) * 4,
        compiler_params=params(8),
        name="parts",
    )(kept.reshape(strips, share, half), taken.reshape(strips, share, half))
    fetched = [swap(parts[k], "tile", line_swap(k)) for k in (1, 2, 3)]
    scene = pl.pallas_call(
        functools.partial(scene_kernel, breadth),
        out_shape=struct((2, breadth, planes), BF16),
        in_specs=[vmem()] * 3,
        out_specs=vmem(),
        compiler_params=params(16),
        cost_estimate=pl.CostEstimate(flops=2 * 2 * wide * taps * planes, bytes_accessed=10**6, transcendentals=0),
        name="scene",
    )(bev, hidden, predictor_filter)
    fetched, scene = lax.optimization_barrier((fetched, scene))
    pairs = pl.pallas_call(
        planes_kernel,
        out_shape=tuple(struct((2, share, half), F32 if k == 0 else BF16) for k in range(4)),
        in_specs=[vmem()] * 4,
        out_specs=(vmem(),) * 4,
        compiler_params=params(8),
        name="planes",
    )(parts[0], *fetched)
    fetched = [swap(pairs[k], "tile", line_swap(4 * k)) for k in (1, 2, 3)]
    pair = added(pairs[0], *fetched)
    ours = pair[0]
    theirs = pair[1].astype(BF16)
    strip = lax.axis_index("tile")
    near = jnp.where(strip % 2 == 1, own[0], own[height - 1])
    far = jnp.where(strip % 2 == 1, own[height - 1], own[0])
    theirs, near, far = lax.optimization_barrier((theirs, near, far))
    ours = added(ours, swap(theirs, "tile", mirror))
    first = swap(near, "tile", line_swap(1))
    second = swap(far, "tile", lambda i: (i - 1 + 2 * (i % 2)) % strips)
    fetched = [swap(ours, "dp", line_swap(2 * k)) for k in (1, 2, 3)]
    derivative = pl.pallas_call(
        functools.partial(derivative_kernel, breadth),
        out_shape=struct((2, breadth, planes), BF16),
        in_specs=[vmem()] * 5,
        out_specs=vmem(),
        scratch_shapes=[pltpu.VMEM((4, wide, planes), BF16)],
        compiler_params=params(16),
        cost_estimate=pl.CostEstimate(flops=2 * 2 * wide * taps * planes, bytes_accessed=10**6, transcendentals=10**6),
        name="derivative",
    )(own, first, second, predictor_filter, pre)
    fetched, derivative = lax.optimization_barrier((fetched, derivative))
    ours = added(ours, *fetched)
    other = swap(ours, "dp", line_swap(1))
    odd = lax.axis_index("dp") % 2 == 1
    gradient = jnp.concatenate([jnp.where(odd, other, ours), jnp.where(odd, ours, other)], axis=1)
    square_tally = lax.axis_size("dp") * height * strips * breadth
    return scene[None], derivative[None], gradient / math.sqrt(square_tally)


def solution(mesh):
    placed = (
        P("dp", "tile", None),
        P("dp", "tile", None),
        P("dp", "tile", None, None),
        P("dp", "tile", None, None),
        P("dp", "tile", None),
        P("dp", "tile", None, None),
        P(),
        P(),
    )
    return jax.shard_map(
        on_device,
        mesh=mesh,
        in_specs=placed,
        out_specs=(P("dp", "tile", None, None), P("dp", "tile", None, None), P("tile", None)),
        check_vma=False,
    )
```

time: 95.9 us -> 82.8 us (0.86)
  blocking collectives: 28.9 us -> 0 us
  starting transfers between devices: 27 us -> 39.1 us
  waiting for transfers between devices: 11.4 us -> 20.5 us
  local copies, waits for them, and re-layouts: 10.3 us -> 2.51 us
  Pallas kernels: 16 us -> 18.9 us
    ppermute x3 -> x21, starting transfers between devices: 8.21 us -> 39.1 us  [swap(): lax.ppermute(values, axis, [(i, partner(i)) for i in range(lax.axis_size(...]
    all_to_all x1 -> x0, blocking collectives: 28.9 us -> none  [reduced_gradient(): lax.all_to_all(pair_sum.reshape(tile_count, share_rows, half), 'tile', 0,...]
    all_to_all x2 -> x0, starting transfers between devices: 18.8 us -> none  [the longest x1 12.2 us: on_device(): arrived = lax.all_to_all(message, 'tile', 0, 0, tiled=True)]
    ppermute x3 -> x21, waiting for transfers between devices: 7.68 us -> 20.5 us  [swap(): lax.ppermute(values, axis, [(i, partner(i)) for i in range(lax.axis_size(...]
    unnamed x28 -> x18, local copies, waits for them, and re-layouts: 9.51 us -> 2.5 us
    pallas_call x3 -> x9, Pallas kernels: 6.19 us -> 10.8 us  [the longest x1 2.39 us: on_device(): pl.pallas_call(plane_kernel, out_shape=struct((6, breadth, planes), F32),...]
    all_to_all x2 -> x0, waiting for transfers between devices: 3.69 us -> none  [the longest x1 3.69 us: on_device(): arrived = lax.all_to_all(message, 'tile', 0, 0, tiled=True)]
    pallas_call x1, Pallas kernels: 4.38 us -> 3.41 us  [on_device(): pl.pallas_call(functools.partial(hidden_kernel, breadth), out_shape=(stru...]
  transfers between devices with their start and end apart: 5 -> 21, of which waited for: 3 -> 13; matrix products, arithmetic and copies ran while one was open for 0% -> 0% of each run, Pallas kernels for 5% -> 8%
where the time goes in v3:
time: 82.8 us; the launch traced here: 82.6 us
  starting transfers between devices  39.1 us (47%)
  waiting for transfers between devices  20.5 us (25%)
  Pallas kernels  18.9 us (23%)
  local copies, waits for them, and re-layouts  2.51 us (3%)
    ppermute x21, starting transfers between devices, swap(): lax.ppermute(values, axis, [(i, partner(i)) for i in range(lax.axis_size(...  39.1 us
    ppermute x21, waiting for transfers between devices, swap(): lax.ppermute(values, axis, [(i, partner(i)) for i in range(lax.axis_size(...  20.5 us
    pallas_call x1, Pallas kernels, on_device(): pl.pallas_call(splat_kernel, out_shape=struct((6, wide, planes), BF16), i...  4.62 us
    pallas_call x1, Pallas kernels, on_device(): pl.pallas_call(functools.partial(hidden_kernel, breadth), out_shape=(stru...  3.41 us
    unnamed x18, local copies, waits for them, and re-layouts  2.5 us
    pallas_call x1, Pallas kernels, on_device(): pl.pallas_call(plane_kernel, out_shape=struct((6, breadth, planes), F32),...  2.39 us
    pallas_call x1, Pallas kernels, on_device(): pl.pallas_call(pack_kernel, out_shape=struct((places, planes), BF16), in_...  2.13 us
    pallas_call x1, Pallas kernels, on_device(): pl.pallas_call(functools.partial(derivative_kernel, breadth), out_shape=s...  2.02 us
  transfers between devices with their start and end apart: 21, of which 13 were waited for; matrix products, arithmetic and copies ran while one was open for 0% of the time, Pallas kernels for 8%

profile of v3, /device:TPU:1, one launch (start us, length us, event | category | flops | bytes accessed | tf_op | source)
XLA Modules:
  0.0 82.6 jit_solution(12989700492518288276)
XLA Ops:
  0.6 2.1 %pack.1.refs_0_ = bf16[64,256]{1,0:T(8,128)(2,1)} custom-call(bf16[32,256]{1,0:T(8,128)(2,1)} %bitcast.25, bf16[32,64]{1,0:T(8,128)(2,1)} %bitcast.28, s32[32,64]{1,0:T(8,128)} %bitcast.26, s32[32,64]{1,0:T(8,128)} %bitcast.27, s32[1,32]{1,0:T(1,128)} %bitcast.29), custom_call_target="tpu_custom_call" | custom-call | tf_op jit(solution)/shard_map/pack/pallas_call | solution.py:368
  2.8 6.5 %collective-permute-start = (bf16[64,256]{1,0:T(8,128)(2,1)}, bf16[64,256]{1,0:T(8,128)(2,1)S(1)}, u32[]{:S(2)}, u32[]{:S(2)}) collective-permute-start(bf16[64,256]{1,0:T(8,128)(2,1)} %pack.1.refs_0_), channel_id=1, source_target_pairs={{0,28},{1,29},{2,30},{3,31},{4,24},{5,25},{6,26},{7,27},{8,20},{9,... | collective-permute-start | bytes 98312 | tf_op jit(solution)/shard_map/ppermute | solution.py:332
  9.3 1.5 %collective-permute-done.refs_1_ = bf16[64,256]{1,0:T(8,128)(2,1)S(1)} collective-permute-done((bf16[64,256]{1,0:T(8,128)(2,1)}, bf16[64,256]{1,0:T(8,128)(2,1)S(1)}, u32[]{:S(2)}, u32[]{:S(2)}) %collective-permute-start) | collective-permute-done | bytes 32800 | tf_op jit(solution)/shard_map/ppermute | solution.py:332
  10.8 0.8 copy-done.6
  11.5 0.2 line.1
  11.7 1.7 %collective-permute-start.1 = (bf16[80,256]{1,0:T(8,128)(2,1)S(1)}, bf16[80,256]{1,0:T(8,128)(2,1)S(1)}, u32[]{:S(2)}, u32[]{:S(2)}) collective-permute-start(bf16[80,256]{1,0:T(8,128)(2,1)S(1)} %get-tuple-element.35), channel_id=1, source_target_pairs={{0,4},{1,5},{2,6},{3,7},{4,0},{5,1},{6,2},{7,3},{8,12},{9,13},{10,... | collective-permute-start | bytes 122888 | tf_op jit(solution)/shard_map/ppermute | solution.py:332
  13.4 0.5 collective-permute-start.2
  14.0 1.6 %collective-permute-start.3 = (bf16[80,256]{1,0:T(8,128)(2,1)S(1)}, bf16[80,256]{1,0:T(8,128)(2,1)S(1)}, u32[]{:S(2)}, u32[]{:S(2)}) collective-permute-start(bf16[80,256]{1,0:T(8,128)(2,1)S(1)} %get-tuple-element.37), channel_id=1, source_target_pairs={{0,12},{1,13},{2,14},{3,15},{4,8},{5,9},{6,10},{7,11},{8,4},{9,5},... | collective-permute-start | bytes 122888 | tf_op jit(solution)/shard_map/ppermute | solution.py:332
  15.6 1.8 %collective-permute-done.2.refs_2_ = bf16[80,256]{1,0:T(8,128)(2,1)S(1)} collective-permute-done((bf16[80,256]{1,0:T(8,128)(2,1)S(1)}, bf16[80,256]{1,0:T(8,128)(2,1)S(1)}, u32[]{:S(2)}, u32[]{:S(2)}) %collective-permute-start.2) | collective-permute-done | bytes 40992 | tf_op jit(solution)/shard_map/ppermute | solution.py:332
  17.4 1.6 %collective-permute-done.3.refs_3_ = bf16[80,256]{1,0:T(8,128)(2,1)S(1)} collective-permute-done((bf16[80,256]{1,0:T(8,128)(2,1)S(1)}, bf16[80,256]{1,0:T(8,128)(2,1)S(1)}, u32[]{:S(2)}, u32[]{:S(2)}) %collective-permute-start.3) | collective-permute-done | bytes 40992 | tf_op jit(solution)/shard_map/ppermute | solution.py:332
  19.1 0.1 strip.1
  19.1 1.4 %collective-permute-start.4 = (bf16[288,256]{1,0:T(8,128)(2,1)S(1)}, bf16[288,256]{1,0:T(8,128)(2,1)S(1)}, u32[]{:S(2)}, u32[]{:S(2)}) collective-permute-start(bf16[288,256]{1,0:T(8,128)(2,1)S(1)} %get-tuple-element.38), channel_id=1, source_target_pairs={{0,1},{1,0},{2,3},{3,2},{4,5},{5,4},{6,7},{7,6},{8,9},{9,8},{10,11... | collective-permute-start | bytes 442376 | tf_op jit(solution)/shard_map/ppermute | solution.py:332
  20.5 2.6 %collective-permute-start.5 = (bf16[288,256]{1,0:T(8,128)(2,1)S(1)}, bf16[288,256]{1,0:T(8,128)(2,1)S(1)}, u32[]{:S(2)}, u32[]{:S(2)}) collective-permute-start(bf16[288,256]{1,0:T(8,128)(2,1)S(1)} %get-tuple-element.39), channel_id=1, source_target_pairs={{0,2},{1,3},{2,0},{3,1},{4,6},{5,7},{6,4},{7,5},{8,10},{9,11},{10,... | collective-permute-start | bytes 442376 | tf_op jit(solution)/shard_map/ppermute | solution.py:332
  23.2 1.0 %copy-done = bf16[1,2,400,256]{3,2,1,0:T(8,128)(2,1)S(1)} copy-done((bf16[1,2,400,256]{3,2,1,0:T(8,128)(2,1)S(1)}, bf16[1,2,400,256]{3,2,1,0:T(8,128)(2,1)}, u32[]{:S(2)}) %copy-start) | copy-done | bytes 409624
  24.2 0.2 moved.1.shifted
  24.4 2.4 %plane.1.partial = f32[6,400,256]{2,1,0:T(8,128)S(1)} custom-call(bf16[288,256]{1,0:T(8,128)(2,1)S(1)} %get-tuple-element.41.message), custom_call_target="tpu_custom_call" | custom-call | flops 629145600 | bytes 1000000 | tf_op jit(solution)/shard_map/plane/pallas_call | solution.py:429
  26.8 0.0 copy-start.2
  26.8 0.5 collective-permute-done.5.two
  27.3 1.5 %collective-permute-done.6.three = bf16[288,256]{1,0:T(8,128)(2,1)S(1)} collective-permute-done((bf16[288,256]{1,0:T(8,128)(2,1)S(1)}, bf16[288,256]{1,0:T(8,128)(2,1)S(1)}, u32[]{:S(2)}, u32[]{:S(2)}) %collective-permute-start.6) | collective-permute-done | bytes 147488 | tf_op jit(solution)/shard_map/ppermute | solution.py:332
  28.8 4.6 %splat.1.bev = bf16[6,416,256]{2,1,0:T(8,128)(2,1)S(1)} custom-call(bf16[288,256]{1,0:T(8,128)(2,1)S(1)} %collective-permute-done.4.one, bf16[288,256]{1,0:T(8,128)(2,1)S(1)} %collective-permute-done.5.two, bf16[288,256]{1,0:T(8,128)(2,1)S(1)} %collective-permute-done.6.three, f32[6,400,256]{2,1,0:T(8,128)S(1)} %plane.1.partial), custom_call_target="tpu_custom_call" | custom-call | tf_op jit(solution)/shard_map/splat/pallas_call | solution.py:439
  33.5 3.4 %hidden.1 = (f32[2,416,256]{2,1,0:T(8,128)S(1)}, bf16[4,416,256]{2,1,0:T(8,128)(2,1)S(1)}, f32[2304,128]{1,0:T(8,128)S(1)}, bf16[2304,128]{1,0:T(8,128)(2,1)S(1)}) custom-call(bf16[6,416,256]{2,1,0:T(8,128)(2,1)S(1)} %splat.1.bev, bf16[2304,256]{1,0:T(8,128)(2,1)S(1)} %copy-done.2, bf16[2,416,768]{2,1,0:T(8,128)(2,1)S(1)} %moved.1.shifted), custom_call_target="tpu_custom_call" | custom-call | tf_op jit(solution)/shard_map/hidden/pallas_call | solution.py:448
  36.9 0.0 copy-start.3
  36.9 4.0 %collective-permute-start.7 = (bf16[2304,128]{1,0:T(8,128)(2,1)S(1)}, bf16[2304,128]{1,0:T(8,128)(2,1)S(1)}, u32[]{:S(2)}, u32[]{:S(2)}) collective-permute-start(bf16[2304,128]{1,0:T(8,128)(2,1)S(1)} %get-tuple-element.43), channel_id=1, source_target_pairs={{0,32},{32,0},{64,96},{96,64},{128,160},{160,128},{192,224},{224,1... | collective-permute-start | bytes 1769480 | tf_op jit(solution)/shard_map/ppermute | solution.py:332
  40.9 1.6 %collective-permute-done.7 = bf16[2304,128]{1,0:T(8,128)(2,1)S(1)} collective-permute-done((bf16[2304,128]{1,0:T(8,128)(2,1)S(1)}, bf16[2304,128]{1,0:T(8,128)(2,1)S(1)}, u32[]{:S(2)}, u32[]{:S(2)}) %collective-permute-start.7) | collective-permute-done | bytes 589856 | tf_op jit(solution)/shard_map/ppermute | solution.py:332
  42.6 0.9 %parts.1 = (f32[8,72,128]{2,1,0:T(8,128)S(1)}, bf16[8,72,128]{2,1,0:T(8,128)(2,1)}, bf16[8,72,128]{2,1,0:T(8,128)(2,1)}, bf16[8,72,128]{2,1,0:T(8,128)(2,1)}) custom-call(f32[32,72,128]{2,1,0:T(8,128)S(1)} %bitcast.22, bf16[32,72,128]{2,1,0:T(8,128)(2,1)S(1)} %bitcast.23), custom_call_target="tpu_custom_call" | custom-call | tf_op jit(solution)/shard_map/parts/pallas_call | solution.py:464
  43.4 0.7 copy-done.4
  44.1 0.9 %collective-permute-start.10 = (bf16[8,72,128]{2,1,0:T(8,128)(2,1)}, bf16[8,72,128]{2,1,0:T(8,128)(2,1)S(1)}, u32[]{:S(2)}, u32[]{:S(2)}) collective-permute-start(bf16[8,72,128]{2,1,0:T(8,128)(2,1)} %get-tuple-element.46), channel_id=1, source_target_pairs={{0,3},{1,2},{2,1},{3,0},{4,7},{5,6},{6,5},{7,4},{8,11},{9,10},{10,... | collective-permute-start | bytes 442376 | tf_op jit(solution)/shard_map/ppermute | solution.py:332
  45.0 3.0 %collective-permute-start.9 = (bf16[8,72,128]{2,1,0:T(8,128)(2,1)}, bf16[8,72,128]{2,1,0:T(8,128)(2,1)}, u32[]{:S(2)}, u32[]{:S(2)}) collective-permute-start(bf16[8,72,128]{2,1,0:T(8,128)(2,1)} %get-tuple-element.45), channel_id=1, source_target_pairs={{0,2},{1,3},{2,0},{3,1},{4,6},{5,7},{6,4},{7,5},{8,10},{9,11},{10,... | collective-permute-start | bytes 442376 | tf_op jit(solution)/shard_map/ppermute | solution.py:332
  48.0 1.9 %scene.1 = bf16[2,400,256]{2,1,0:T(8,128)(2,1)} custom-call(bf16[6,416,256]{2,1,0:T(8,128)(2,1)S(1)} %splat.1.bev, bf16[4,416,256]{2,1,0:T(8,128)(2,1)S(1)} %get-tuple-element.47.hidden, bf16[2304,256]{1,0:T(8,128)(2,1)S(1)} %copy-done.3), custom_call_target="tpu_custom_call" | custom-call | flops 981467136 | bytes 1000000 | tf_op jit(solution)/shard_map/scene/pallas_call | solution.py:473
  49.9 0.7 collective-permute-done.10.three
  50.6 4.1 %collective-permute-done.9.two = bf16[8,72,128]{2,1,0:T(8,128)(2,1)} collective-permute-done((bf16[8,72,128]{2,1,0:T(8,128)(2,1)}, bf16[8,72,128]{2,1,0:T(8,128)(2,1)}, u32[]{:S(2)}, u32[]{:S(2)}) %collective-permute-start.9) | collective-permute-done | bytes 147488 | tf_op jit(solution)/shard_map/ppermute | solution.py:332
  54.7 1.1 %planes.1 = (f32[2,72,128]{2,1,0:T(8,128)S(1)}, bf16[2,72,128]{2,1,0:T(8,128)(2,1)S(1)}, bf16[2,72,128]{2,1,0:T(8,128)(2,1)S(1)}, bf16[2,72,128]{2,1,0:T(8,128)(2,1)S(1)}) custom-call(f32[8,72,128]{2,1,0:T(8,128)S(1)} %copy-done.5, bf16[8,72,128]{2,1,0:T(8,128)(2,1)} %collective-permute-done.8.one, bf16[8,72,128]{2,1,0:T(8,128)(2,1)} %collective-permute-done.9.two, ...), custom_call_target="tpu_custom_call" | custom-call | tf_op jit(solution)/shard_map/planes/pallas_call | solution.py:483
  55.8 0.1 collective-permute-start.11
  55.9 1.9 %collective-permute-start.12 = (bf16[2,72,128]{2,1,0:T(8,128)(2,1)S(1)}, bf16[2,72,128]{2,1,0:T(8,128)(2,1)S(1)}, u32[]{:S(2)}, u32[]{:S(2)}) collective-permute-start(bf16[2,72,128]{2,1,0:T(8,128)(2,1)S(1)} %get-tuple-element.55), channel_id=1, source_target_pairs={{0,8},{1,9},{2,10},{3,11},{4,12},{5,13},{6,14},{7,15},{8,0},{9,1},... | collective-permute-start | bytes 110600 | tf_op jit(solution)/shard_map/ppermute | solution.py:332
  57.8 1.7 %collective-permute-start.13 = (bf16[2,72,128]{2,1,0:T(8,128)(2,1)S(1)}, bf16[2,72,128]{2,1,0:T(8,128)(2,1)S(1)}, u32[]{:S(2)}, u32[]{:S(2)}) collective-permute-start(bf16[2,72,128]{2,1,0:T(8,128)(2,1)S(1)} %get-tuple-element.56), channel_id=1, source_target_pairs={{0,12},{1,13},{2,14},{3,15},{4,8},{5,9},{6,10},{7,11},{8,4},{9,5},... | collective-permute-start | bytes 110600 | tf_op jit(solution)/shard_map/ppermute | solution.py:332
  59.5 0.2 collective-permute-done.12
  59.7 2.7 %collective-permute-done.13 = bf16[2,72,128]{2,1,0:T(8,128)(2,1)S(1)} collective-permute-done((bf16[2,72,128]{2,1,0:T(8,128)(2,1)S(1)}, bf16[2,72,128]{2,1,0:T(8,128)(2,1)S(1)}, u32[]{:S(2)}, u32[]{:S(2)}) %collective-permute-start.13) | collective-permute-done | bytes 36896 | tf_op jit(solution)/shard_map/ppermute | solution.py:332
  62.4 3.8 %collective-permute-start.14 = (bf16[72,128]{1,0:T(8,128)(2,1)S(1)}, bf16[72,128]{1,0:T(8,128)(2,1)S(1)}, u32[]{:S(2)}, u32[]{:S(2)}) collective-permute-start(bf16[72,128]{1,0:T(8,128)(2,1)S(1)} %fusion.1), channel_id=1, source_target_pairs={{0,28},{1,29},{2,30},{3,31},{4,24},{5,25},{6,26},{7,27},{8,20},{9,... | collective-permute-start | bytes 55304 | tf_op jit(solution)/shard_map/ppermute | solution.py:332
  66.2 0.8 collective-permute-start.19
  67.0 0.4 collective-permute-done.14
  67.4 1.3 %collective-permute-start.15 = (f32[72,128]{1,0:T(8,128)S(1)}, f32[72,128]{1,0:T(8,128)S(1)}, u32[]{:S(2)}, u32[]{:S(2)}) collective-permute-start(f32[72,128]{1,0:T(8,128)S(1)} %fusion), channel_id=1, source_target_pairs={{0,64},{32,96},{64,0},{96,32},{128,192},{160,224},{192,128},{224,1... | collective-permute-start | bytes 110600 | tf_op jit(solution)/shard_map/ppermute | solution.py:332
  68.7 2.5 %collective-permute-start.16 = (f32[72,128]{1,0:T(8,128)S(1)}, f32[72,128]{1,0:T(8,128)S(1)}, u32[]{:S(2)}, u32[]{:S(2)}) collective-permute-start(f32[72,128]{1,0:T(8,128)S(1)} %fusion), channel_id=1, source_target_pairs={{0,128},{32,160},{64,192},{96,224},{128,0},{160,32},{192,64},{224,... | collective-permute-start | bytes 110600 | tf_op jit(solution)/shard_map/ppermute | solution.py:332
  71.1 0.1 collective-permute-start.17
  71.3 2.9 %collective-permute-done.19.second = bf16[400,256]{1,0:T(8,128)(2,1)S(1)} collective-permute-done((bf16[400,256]{1,0:T(8,128)(2,1)S(1)}, bf16[400,256]{1,0:T(8,128)(2,1)S(1)}, u32[]{:S(2)}, u32[]{:S(2)}) %collective-permute-start.19) | collective-permute-done | bytes 204832 | tf_op jit(solution)/shard_map/ppermute | solution.py:332
  74.2 2.0 %derivative.1 = bf16[2,400,256]{2,1,0:T(8,128)(2,1)} custom-call(bf16[2,400,256]{2,1,0:T(8,128)(2,1)S(1)} %bitcast.21, bf16[400,256]{1,0:T(8,128)(2,1)S(1)} %collective-permute-done.18.first, bf16[400,256]{1,0:T(8,128)(2,1)S(1)} %collective-permute-done.19.second, bf16[2304,256]{1,0:T(8,128)(2,1)S(1)} %copy-done.3, f32[2,416,256]{2,1,0:T(8,128)S(1)} %copy-done.8), custom_call_target="tpu_custom_call" | custom-call | flops 981467136 | bytes 1000000 | tf_op jit(solution)/shard_map/derivative/pallas_call | solution.py:503
  76.2 4.8 %collective-permute-start.20 = (f32[72,128]{1,0:T(8,128)S(1)}, f32[72,128]{1,0:T(8,128)S(1)}, u32[]{:S(2)}, u32[]{:S(2)}) collective-permute-start(f32[72,128]{1,0:T(8,128)S(1)} %add_add_fusion), channel_id=1, source_target_pairs={{0,32},{32,0},{64,96},{96,64},{128,160},{160,128},{192,224},{224,1... | collective-permute-start | bytes 110600 | tf_op jit(solution)/shard_map/ppermute | solution.py:332
  81.0 0.9 %collective-permute-done.20 = f32[72,128]{1,0:T(8,128)S(1)} collective-permute-done((f32[72,128]{1,0:T(8,128)S(1)}, f32[72,128]{1,0:T(8,128)S(1)}, u32[]{:S(2)}, u32[]{:S(2)}) %collective-permute-start.20) | collective-permute-done | bytes 36896 | tf_op jit(solution)/shard_map/ppermute | solution.py:332
  81.9 0.6 maximum_multiply_fusion
  (30 shorter events, 0.1 us)
Async XLA Ops:
  2.8 8.0 %collective-permute-start = (bf16[64,256]{1,0:T(8,128)(2,1)}, bf16[64,256]{1,0:T(8,128)(2,1)S(1)}, u32[]{:S(2)}, u32[]{:S(2)}) collective-permute-start(bf16[64,256]{1,0:T(8,128)(2,1)} %pack.1.refs_0_), channel_id=1, source_target_pairs={{0,28},{1,29},{2,30},{3,31},{4,24},{5,25},{6,26},{7,27},{8,20},{9,... | collective-permute-start | bytes 98312 | tf_op jit(solution)/shard_map/ppermute | solution.py:332
  10.8 0.8 copy-start.6
  11.7 3.9 %collective-permute-start.1 = (bf16[80,256]{1,0:T(8,128)(2,1)S(1)}, bf16[80,256]{1,0:T(8,128)(2,1)S(1)}, u32[]{:S(2)}, u32[]{:S(2)}) collective-permute-start(bf16[80,256]{1,0:T(8,128)(2,1)S(1)} %get-tuple-element.35), channel_id=1, source_target_pairs={{0,4},{1,5},{2,6},{3,7},{4,0},{5,1},{6,2},{7,3},{8,12},{9,13},{10,... | collective-permute-start | bytes 122888 | tf_op jit(solution)/shard_map/ppermute | solution.py:332
  13.4 4.0 %collective-permute-start.2 = (bf16[80,256]{1,0:T(8,128)(2,1)S(1)}, bf16[80,256]{1,0:T(8,128)(2,1)S(1)}, u32[]{:S(2)}, u32[]{:S(2)}) collective-permute-start(bf16[80,256]{1,0:T(8,128)(2,1)S(1)} %get-tuple-element.36), channel_id=1, source_target_pairs={{0,8},{1,9},{2,10},{3,11},{4,12},{5,13},{6,14},{7,15},{8,0},{9,1},... | collective-permute-start | bytes 122888 | tf_op jit(solution)/shard_map/ppermute | solution.py:332
  14.0 5.1 %collective-permute-start.3 = (bf16[80,256]{1,0:T(8,128)(2,1)S(1)}, bf16[80,256]{1,0:T(8,128)(2,1)S(1)}, u32[]{:S(2)}, u32[]{:S(2)}) collective-permute-start(bf16[80,256]{1,0:T(8,128)(2,1)S(1)} %get-tuple-element.37), channel_id=1, source_target_pairs={{0,12},{1,13},{2,14},{3,15},{4,8},{5,9},{6,10},{7,11},{8,4},{9,5},... | collective-permute-start | bytes 122888 | tf_op jit(solution)/shard_map/ppermute | solution.py:332
  19.1 7.6 %collective-permute-start.4 = (bf16[288,256]{1,0:T(8,128)(2,1)S(1)}, bf16[288,256]{1,0:T(8,128)(2,1)S(1)}, u32[]{:S(2)}, u32[]{:S(2)}) collective-permute-start(bf16[288,256]{1,0:T(8,128)(2,1)S(1)} %get-tuple-element.38), channel_id=1, source_target_pairs={{0,1},{1,0},{2,3},{3,2},{4,5},{5,4},{6,7},{7,6},{8,9},{9,8},{10,11... | collective-permute-start | bytes 442376 | tf_op jit(solution)/shard_map/ppermute | solution.py:332
  20.5 6.8 %collective-permute-start.5 = (bf16[288,256]{1,0:T(8,128)(2,1)S(1)}, bf16[288,256]{1,0:T(8,128)(2,1)S(1)}, u32[]{:S(2)}, u32[]{:S(2)}) collective-permute-start(bf16[288,256]{1,0:T(8,128)(2,1)S(1)} %get-tuple-element.39), channel_id=1, source_target_pairs={{0,2},{1,3},{2,0},{3,1},{4,6},{5,7},{6,4},{7,5},{8,10},{9,11},{10,... | collective-permute-start | bytes 442376 | tf_op jit(solution)/shard_map/ppermute | solution.py:332
  23.1 5.7 %collective-permute-start.6 = (bf16[288,256]{1,0:T(8,128)(2,1)S(1)}, bf16[288,256]{1,0:T(8,128)(2,1)S(1)}, u32[]{:S(2)}, u32[]{:S(2)}) collective-permute-start(bf16[288,256]{1,0:T(8,128)(2,1)S(1)} %get-tuple-element.40), channel_id=1, source_target_pairs={{0,3},{1,2},{2,1},{3,0},{4,7},{5,6},{6,5},{7,4},{8,11},{9,10},{10,... | collective-permute-start | bytes 442376 | tf_op jit(solution)/shard_map/ppermute | solution.py:332
  23.2 1.0 %copy-start = (bf16[1,2,400,256]{3,2,1,0:T(8,128)(2,1)S(1)}, bf16[1,2,400,256]{3,2,1,0:T(8,128)(2,1)}, u32[]{:S(2)}) copy-start(bf16[1,2,400,256]{3,2,1,0:T(8,128)(2,1)} %param.13) | copy-start | bytes 1228804
  26.8 6.7 %copy-start.2 = (bf16[2304,256]{1,0:T(8,128)(2,1)S(1)}, bf16[2304,256]{1,0:T(8,128)(2,1)}, u32[]{:S(2)}) copy-start(bf16[2304,256]{1,0:T(8,128)(2,1)} %weight.3) | copy-start | bytes 3538948
  36.9 6.5 %copy-start.7 = (f32[2,416,256]{2,1,0:T(8,128)}, f32[2,416,256]{2,1,0:T(8,128)S(1)}, u32[]{:S(2)}) copy-start(f32[2,416,256]{2,1,0:T(8,128)S(1)} %get-tuple-element.60.pre) | copy-start | bytes 2555908
  36.9 11.1 %copy-start.3 = (bf16[2304,256]{1,0:T(8,128)(2,1)S(1)}, bf16[2304,256]{1,0:T(8,128)(2,1)}, u32[]{:S(2)}) copy-start(bf16[2304,256]{1,0:T(8,128)(2,1)} %weight.5) | copy-start | bytes 3538948
  36.9 5.6 %collective-permute-start.7 = (bf16[2304,128]{1,0:T(8,128)(2,1)S(1)}, bf16[2304,128]{1,0:T(8,128)(2,1)S(1)}, u32[]{:S(2)}, u32[]{:S(2)}) collective-permute-start(bf16[2304,128]{1,0:T(8,128)(2,1)S(1)} %get-tuple-element.43), channel_id=1, source_target_pairs={{0,32},{32,0},{64,96},{96,64},{128,160},{160,128},{192,224},{224,1... | collective-permute-start | bytes 1769480 | tf_op jit(solution)/shard_map/ppermute | solution.py:332
  43.4 0.7 copy-start.4
  44.1 6.5 %collective-permute-start.10 = (bf16[8,72,128]{2,1,0:T(8,128)(2,1)}, bf16[8,72,128]{2,1,0:T(8,128)(2,1)S(1)}, u32[]{:S(2)}, u32[]{:S(2)}) collective-permute-start(bf16[8,72,128]{2,1,0:T(8,128)(2,1)} %get-tuple-element.46), channel_id=1, source_target_pairs={{0,3},{1,2},{2,1},{3,0},{4,7},{5,6},{6,5},{7,4},{8,11},{9,10},{10,... | collective-permute-start | bytes 442376 | tf_op jit(solution)/shard_map/ppermute | solution.py:332
  45.0 5.6 %collective-permute-start.8 = (bf16[8,72,128]{2,1,0:T(8,128)(2,1)}, bf16[8,72,128]{2,1,0:T(8,128)(2,1)}, u32[]{:S(2)}, u32[]{:S(2)}) collective-permute-start(bf16[8,72,128]{2,1,0:T(8,128)(2,1)} %get-tuple-element.44), channel_id=1, source_target_pairs={{0,1},{1,0},{2,3},{3,2},{4,5},{5,4},{6,7},{7,6},{8,9},{9,8},{10,11... | collective-permute-start | bytes 442376 | tf_op jit(solution)/shard_map/ppermute | solution.py:332
  45.0 9.7 %collective-permute-start.9 = (bf16[8,72,128]{2,1,0:T(8,128)(2,1)}, bf16[8,72,128]{2,1,0:T(8,128)(2,1)}, u32[]{:S(2)}, u32[]{:S(2)}) collective-permute-start(bf16[8,72,128]{2,1,0:T(8,128)(2,1)} %get-tuple-element.45), channel_id=1, source_target_pairs={{0,2},{1,3},{2,0},{3,1},{4,6},{5,7},{6,4},{7,5},{8,10},{9,11},{10,... | collective-permute-start | bytes 442376 | tf_op jit(solution)/shard_map/ppermute | solution.py:332
  48.0 6.7 %copy-start.5 = (f32[8,72,128]{2,1,0:T(8,128)S(1)}, f32[8,72,128]{2,1,0:T(8,128)}, u32[]{:S(2)}) copy-start(f32[8,72,128]{2,1,0:T(8,128)} %copy-done.4) | copy-start | bytes 884740
  48.0 11.4 %copy-start.1 = (bf16[1,2,400,256]{3,2,1,0:T(8,128)(2,1)S(1)}, bf16[1,2,400,256]{3,2,1,0:T(8,128)(2,1)}, u32[]{:S(2)}) copy-start(bf16[1,2,400,256]{3,2,1,0:T(8,128)(2,1)} %param.13) | copy-start | bytes 1228804
  49.9 24.3 %copy-start.8 = (f32[2,416,256]{2,1,0:T(8,128)S(1)}, f32[2,416,256]{2,1,0:T(8,128)}, u32[]{:S(2)}) copy-start(f32[2,416,256]{2,1,0:T(8,128)} %copy-done.7) | copy-start | bytes 2555908
  55.8 3.7 %collective-permute-start.11 = (bf16[2,72,128]{2,1,0:T(8,128)(2,1)S(1)}, bf16[2,72,128]{2,1,0:T(8,128)(2,1)S(1)}, u32[]{:S(2)}, u32[]{:S(2)}) collective-permute-start(bf16[2,72,128]{2,1,0:T(8,128)(2,1)S(1)} %get-tuple-element.54), channel_id=1, source_target_pairs={{0,4},{1,5},{2,6},{3,7},{4,0},{5,1},{6,2},{7,3},{8,12},{9,13},{10,... | collective-permute-start | bytes 110600 | tf_op jit(solution)/shard_map/ppermute | solution.py:332
  55.9 3.8 %collective-permute-start.12 = (bf16[2,72,128]{2,1,0:T(8,128)(2,1)S(1)}, bf16[2,72,128]{2,1,0:T(8,128)(2,1)S(1)}, u32[]{:S(2)}, u32[]{:S(2)}) collective-permute-start(bf16[2,72,128]{2,1,0:T(8,128)(2,1)S(1)} %get-tuple-element.55), channel_id=1, source_target_pairs={{0,8},{1,9},{2,10},{3,11},{4,12},{5,13},{6,14},{7,15},{8,0},{9,1},... | collective-permute-start | bytes 110600 | tf_op jit(solution)/shard_map/ppermute | solution.py:332
  57.8 4.6 %collective-permute-start.13 = (bf16[2,72,128]{2,1,0:T(8,128)(2,1)S(1)}, bf16[2,72,128]{2,1,0:T(8,128)(2,1)S(1)}, u32[]{:S(2)}, u32[]{:S(2)}) collective-permute-start(bf16[2,72,128]{2,1,0:T(8,128)(2,1)S(1)} %get-tuple-element.56), channel_id=1, source_target_pairs={{0,12},{1,13},{2,14},{3,15},{4,8},{5,9},{6,10},{7,11},{8,4},{9,5},... | collective-permute-start | bytes 110600 | tf_op jit(solution)/shard_map/ppermute | solution.py:332
  62.4 4.9 %collective-permute-start.14 = (bf16[72,128]{1,0:T(8,128)(2,1)S(1)}, bf16[72,128]{1,0:T(8,128)(2,1)S(1)}, u32[]{:S(2)}, u32[]{:S(2)}) collective-permute-start(bf16[72,128]{1,0:T(8,128)(2,1)S(1)} %fusion.1), channel_id=1, source_target_pairs={{0,28},{1,29},{2,30},{3,31},{4,24},{5,25},{6,26},{7,27},{8,20},{9,... | collective-permute-start | bytes 55304 | tf_op jit(solution)/shard_map/ppermute | solution.py:332
  66.2 5.0 %collective-permute-start.18 = (bf16[400,256]{1,0:T(8,128)(2,1)S(1)}, bf16[400,256]{1,0:T(8,128)(2,1)S(1)}, u32[]{:S(2)}, u32[]{:S(2)}) collective-permute-start(bf16[400,256]{1,0:T(8,128)(2,1)S(1)} %get-tuple-element.58), channel_id=1, source_target_pairs={{0,1},{1,0},{2,3},{3,2},{4,5},{5,4},{6,7},{7,6},{8,9},{9,8},{10,11... | collective-permute-start | bytes 614408 | tf_op jit(solution)/shard_map/ppermute | solution.py:332
  66.2 7.9 %collective-permute-start.19 = (bf16[400,256]{1,0:T(8,128)(2,1)S(1)}, bf16[400,256]{1,0:T(8,128)(2,1)S(1)}, u32[]{:S(2)}, u32[]{:S(2)}) collective-permute-start(bf16[400,256]{1,0:T(8,128)(2,1)S(1)} %get-tuple-element.59), channel_id=1, source_target_pairs={{0,31},{1,2},{2,1},{3,4},{4,3},{5,6},{6,5},{7,8},{8,7},{9,10},{10,... | collective-permute-start | bytes 614408 | tf_op jit(solution)/shard_map/ppermute | solution.py:332
  67.4 8.8 %collective-permute-start.15 = (f32[72,128]{1,0:T(8,128)S(1)}, f32[72,128]{1,0:T(8,128)S(1)}, u32[]{:S(2)}, u32[]{:S(2)}) collective-permute-start(f32[72,128]{1,0:T(8,128)S(1)} %fusion), channel_id=1, source_target_pairs={{0,64},{32,96},{64,0},{96,32},{128,192},{160,224},{192,128},{224,1... | collective-permute-start | bytes 110600 | tf_op jit(solution)/shard_map/ppermute | solution.py:332
  68.7 7.5 %collective-permute-start.16 = (f32[72,128]{1,0:T(8,128)S(1)}, f32[72,128]{1,0:T(8,128)S(1)}, u32[]{:S(2)}, u32[]{:S(2)}) collective-permute-start(f32[72,128]{1,0:T(8,128)S(1)} %fusion), channel_id=1, source_target_pairs={{0,128},{32,160},{64,192},{96,224},{128,0},{160,32},{192,64},{224,... | collective-permute-start | bytes 110600 | tf_op jit(solution)/shard_map/ppermute | solution.py:332
  71.1 5.1 %collective-permute-start.17 = (f32[72,128]{1,0:T(8,128)S(1)}, f32[72,128]{1,0:T(8,128)S(1)}, u32[]{:S(2)}, u32[]{:S(2)}) collective-permute-start(f32[72,128]{1,0:T(8,128)S(1)} %fusion), channel_id=1, source_target_pairs={{0,192},{32,224},{64,128},{96,160},{128,64},{160,96},{192,0},{224,... | collective-permute-start | bytes 110600 | tf_op jit(solution)/shard_map/ppermute | solution.py:332
  76.2 5.7 %collective-permute-start.20 = (f32[72,128]{1,0:T(8,128)S(1)}, f32[72,128]{1,0:T(8,128)S(1)}, u32[]{:S(2)}, u32[]{:S(2)}) collective-permute-start(f32[72,128]{1,0:T(8,128)S(1)} %add_add_fusion), channel_id=1, source_target_pairs={{0,32},{32,0},{64,96},{96,64},{128,160},{160,128},{192,224},{224,1... | collective-permute-start | bytes 110600 | tf_op jit(solution)/shard_map/ppermute | solution.py:332

commit v4 on v3

--- a/solution.py
+++ b/solution.py
@@ -23,6 +23,10 @@
 
 def vmem():
     return pl.BlockSpec(memory_space=pltpu.VMEM)
+
+
+def far_held(values):
+    return pltpu.with_memory_space_constraint(values, pltpu.HBM)
 
 
 def turned(values, shift):
@@ -159,18 +163,18 @@
                 ).astype(BF16)
 
 
-def splat_row(s, r, meta, lifted, onehot):
-    breadth, total = onehot.shape
+def splat_row(k, meta, lifted, onehot):
+    s, r = k // 2, k % 2
+    breadth, total = onehot.shape[1:]
     blocks = breadth // FINE
     fine = lax.broadcasted_iota(jnp.int32, (FINE, total), 0).astype(F32)
     comb = jnp.where(fine == meta[s, 1:2, :], 1.0, 0.0).astype(BF16)
     coarse = meta[s, 0:1, :]
-    begin = r * blocks
     for b in range(blocks):
-        chosen = jnp.where(coarse == (begin + b).astype(F32), 1.0, 0.0).astype(BF16)
-        onehot[b * FINE : (b + 1) * FINE, :] = comb * chosen
+        chosen = jnp.where(coarse == float(r * blocks + b), 1.0, 0.0).astype(BF16)
+        onehot[k % 2, b * FINE : (b + 1) * FINE, :] = comb * chosen
     return lax.dot_general(
-        onehot[...], lifted[s], (((1,), (1,)), ((), ())), preferred_element_type=F32
+        onehot[k % 2], lifted[s], (((1,), (1,)), ((), ())), preferred_element_type=F32
     )
 
 
@@ -182,20 +186,22 @@
     bev[k, breadth:] = jnp.zeros((wide - breadth, planes), BF16)
 
 
-def plane_kernel(message, partial, meta, lifted, onehot):
+def plane_kernel(message, sums, meta, lifted, onehot):
     lift([message], meta, lifted)
-
-    @pl.loop(0, 6)
-    def _(k):
-        partial[k] = splat_row(k // 2, k % 2, meta, lifted, onehot)
-
-
-def splat_kernel(one, two, three, partial, bev, meta, lifted, onehot):
-    lift([one, two, three], meta, lifted)
-
-    @pl.loop(0, 6)
-    def _(k):
-        normalized(partial[k] + splat_row(k // 2, k % 2, meta, lifted, onehot), bev, k)
+    for k in range(6):
+        sums[k] = splat_row(k, meta, lifted, onehot)
+
+
+def more_kernel(message, before, sums, meta, lifted, onehot):
+    lift([message], meta, lifted)
+    for k in range(6):
+        sums[k] = before[k] + splat_row(k, meta, lifted, onehot)
+
+
+def splat_kernel(two, three, before, bev, meta, lifted, onehot):
+    lift([two, three], meta, lifted)
+    for k in range(6):
+        normalized(before[k] + splat_row(k, meta, lifted, onehot), bev, k)
 
 
 def wide_weight(weight, planes):
@@ -225,7 +231,10 @@
     return lax.broadcasted_iota(jnp.int32, shape, 0) < breadth
 
 
-def moved_kernel(breadth, own, shifted):
+def moved_kernel(breadth, own, shifted, near, far):
+    odd = lax.axis_index("tile") % 2 == 1
+    near[...] = jnp.where(odd, own[0], own[1])
+    far[...] = jnp.where(odd, own[1], own[0])
     wide = shifted.shape[1]
     planes = own.shape[2]
     filler = jnp.zeros((wide - breadth, planes), F32)
@@ -328,6 +337,14 @@
             parts[k][i] = total.astype(parts[k].dtype)
 
 
+def gradient_kernel(scale, ours, other, gradient):
+    odd = lax.axis_index("dp") % 2 == 1
+    half = ours.shape[1]
+    mine, theirs = ours[...] * scale, other[...] * scale
+    gradient[:, :half] = jnp.where(odd, theirs, mine)
+    gradient[:, half:] = jnp.where(odd, mine, theirs)
+
+
 def swap(values, axis, partner):
     return lax.ppermute(values, axis, [(i, partner(i)) for i in range(lax.axis_size(axis))])
 
@@ -363,11 +380,12 @@
     taps = predictor_filter.shape[0]
     half = planes // 2
     struct = jax.ShapeDtypeStruct
+    held = pltpu.VMEM
 
     places = pixels + strips
     packed = pl.pallas_call(
         pack_kernel,
-        out_shape=struct((places, planes), BF16),
+        out_shape=held((places, planes), BF16),
         in_specs=[pl.BlockSpec(memory_space=pl.ANY)] * 5,
         out_specs=vmem(),
         scratch_shapes=[
@@ -377,18 +395,18 @@
             pltpu.VMEM((1, strips), jnp.int32),
             pltpu.SemaphoreType.DMA((5,)),
         ],
-        compiler_params=params(60),
+        compiler_params=params(8),
         name="pack",
     )(
-        image_descriptors[0],
-        image_distance_scores[0],
-        entry_sender_location[0, 0],
-        entry_receiver_square[0, 0],
-        entry_valid_tally[0],
+        far_held(image_descriptors[0]),
+        far_held(image_distance_scores[0]),
+        far_held(entry_sender_location[0, 0]),
+        far_held(entry_receiver_square[0, 0]),
+        far_held(entry_valid_tally[0]),
     )
     line = pl.pallas_call(
         line_kernel,
-        out_shape=(struct((2 * pixels + 16, planes), BF16),) * 4,
+        out_shape=(held((2 * pixels + 16, planes), BF16),) * 4,
         in_specs=[vmem()] * 2,
         out_specs=(vmem(),) * 4,
         scratch_shapes=[pltpu.VMEM((2, strips, planes), F32)],
@@ -396,9 +414,20 @@
         name="line",
     )(packed, swap(packed, "tile", mirror))
     line = [line[0]] + [swap(line[k], "tile", line_swap(4 * k)) for k in (1, 2, 3)]
+    own = predicted_adjoint[0]
+    shifted, near, far = pl.pallas_call(
+        functools.partial(moved_kernel, breadth),
+        out_shape=(held((2, wide, 3 * planes), BF16),) + (held((breadth, planes), BF16),) * 2,
+        in_specs=[vmem()],
+        out_specs=(vmem(),) * 3,
+        compiler_params=params(4),
+        cost_estimate=pl.CostEstimate(flops=10**6, bytes_accessed=10**6, transcendentals=0),
+        name="moved",
+    )(own)
+    line, shifted = lax.optimization_barrier((line, shifted))
     messages = pl.pallas_call(
         strip_kernel,
-        out_shape=(struct((9 * pixels, planes), BF16),) * 4,
+        out_shape=(held((9 * pixels, planes), BF16),) * 4,
         in_specs=[vmem()] * 4,
         out_specs=(vmem(),) * 4,
         scratch_shapes=[pltpu.VMEM((4, 16, planes), F32)],
@@ -407,55 +436,54 @@
     )(*line)
     arrived = [swap(messages[k], "tile", line_swap(k)) for k in (1, 2, 3)]
 
-    own = predicted_adjoint[0]
-    shifted = pl.pallas_call(
-        functools.partial(moved_kernel, breadth),
-        out_shape=struct((2, wide, 3 * planes), BF16),
-        in_specs=[vmem()],
-        out_specs=vmem(),
-        compiler_params=params(8),
-        cost_estimate=pl.CostEstimate(flops=10**6, bytes_accessed=10**6, transcendentals=0),
-        name="moved",
-    )(own)
-
     def splat_scratch(count):
         total = count * 8 * slots
         return [
             pltpu.VMEM((3, 8, total), F32),
             pltpu.VMEM((3, planes, total), BF16),
-            pltpu.VMEM((breadth, total), BF16),
+            pltpu.VMEM((2, breadth, total), BF16),
         ]
 
-    partial = pl.pallas_call(
+    sums = pl.pallas_call(
         plane_kernel,
-        out_shape=struct((6, breadth, planes), F32),
+        out_shape=held((6, breadth, planes), F32),
         in_specs=[vmem()],
         out_specs=vmem(),
         scratch_shapes=splat_scratch(1),
-        compiler_params=params(16),
+        compiler_params=params(8),
         cost_estimate=pl.CostEstimate(flops=2 * 6 * breadth * 8 * slots * planes, bytes_accessed=10**6, transcendentals=0),
         name="plane",
     )(messages[0])
+    sums = pl.pallas_call(
+        more_kernel,
+        out_shape=held((6, breadth, planes), F32),
+        in_specs=[vmem()] * 2,
+        out_specs=vmem(),
+        scratch_shapes=splat_scratch(1),
+        compiler_params=params(8),
+        cost_estimate=pl.CostEstimate(flops=2 * 6 * breadth * 8 * slots * planes, bytes_accessed=10**6, transcendentals=0),
+        name="more",
+    )(arrived[0], sums)
     bev = pl.pallas_call(
         splat_kernel,
-        out_shape=struct((6, wide, planes), BF16),
-        in_specs=[vmem()] * 4,
-        out_specs=vmem(),
-        scratch_shapes=splat_scratch(3),
-        compiler_params=params(20),
+        out_shape=held((6, wide, planes), BF16),
+        in_specs=[vmem()] * 3,
+        out_specs=vmem(),
+        scratch_shapes=splat_scratch(2),
+        compiler_params=params(12),
         name="splat",
-    )(*arrived, partial)
+    )(arrived[1], arrived[2], sums)
     pre, hidden, kept, given = pl.pallas_call(
         functools.partial(hidden_kernel, breadth),
         out_shape=(
-            struct((2, wide, planes), F32),
-            struct((4, wide, planes), BF16),
-            struct((taps, half), F32),
-            struct((taps, half), BF16),
+            held((2, wide, planes), F32),
+            held((4, wide, planes), BF16),
+            held((taps, half), F32),
+            held((taps, half), BF16),
         ),
         in_specs=[vmem()] * 3,
         out_specs=(vmem(),) * 4,
-        compiler_params=params(20),
+        compiler_params=params(10),
         name="hidden",
     )(bev, initial_plane_filter, shifted)
 
@@ -463,10 +491,10 @@
     taken = swap(given, "dp", line_swap(1))
     parts = pl.pallas_call(
         parts_kernel,
-        out_shape=tuple(struct((strips // 4, share, half), F32 if k == 0 else BF16) for k in range(4)),
+        out_shape=tuple(held((strips // 4, share, half), F32 if k == 0 else BF16) for k in range(4)),
         in_specs=[vmem()] * 2,
         out_specs=(vmem(),) * 4,
-        compiler_params=params(8),
+        compiler_params=params(2),
         name="parts",
     )(kept.reshape(strips, share, half), taken.reshape(strips, share, half))
     fetched = [swap(parts[k], "tile", line_swap(k)) for k in (1, 2, 3)]
@@ -475,26 +503,23 @@
         out_shape=struct((2, breadth, planes), BF16),
         in_specs=[vmem()] * 3,
         out_specs=vmem(),
-        compiler_params=params(16),
+        compiler_params=params(8),
         cost_estimate=pl.CostEstimate(flops=2 * 2 * wide * taps * planes, bytes_accessed=10**6, transcendentals=0),
         name="scene",
     )(bev, hidden, predictor_filter)
     fetched, scene = lax.optimization_barrier((fetched, scene))
     pairs = pl.pallas_call(
         planes_kernel,
-        out_shape=tuple(struct((2, share, half), F32 if k == 0 else BF16) for k in range(4)),
+        out_shape=tuple(held((2, share, half), F32 if k == 0 else BF16) for k in range(4)),
         in_specs=[vmem()] * 4,
         out_specs=(vmem(),) * 4,
-        compiler_params=params(8),
+        compiler_params=params(2),
         name="planes",
     )(parts[0], *fetched)
     fetched = [swap(pairs[k], "tile", line_swap(4 * k)) for k in (1, 2, 3)]
     pair = added(pairs[0], *fetched)
     ours = pair[0]
     theirs = pair[1].astype(BF16)
-    strip = lax.axis_index("tile")
-    near = jnp.where(strip % 2 == 1, own[0], own[height - 1])
-    far = jnp.where(strip % 2 == 1, own[height - 1], own[0])
     theirs, near, far = lax.optimization_barrier((theirs, near, far))
     ours = added(ours, swap(theirs, "tile", mirror))
     first = swap(near, "tile", line_swap(1))
@@ -506,17 +531,23 @@
         in_specs=[vmem()] * 5,
         out_specs=vmem(),
         scratch_shapes=[pltpu.VMEM((4, wide, planes), BF16)],
-        compiler_params=params(16),
+        compiler_params=params(8),
         cost_estimate=pl.CostEstimate(flops=2 * 2 * wide * taps * planes, bytes_accessed=10**6, transcendentals=10**6),
         name="derivative",
     )(own, first, second, predictor_filter, pre)
     fetched, derivative = lax.optimization_barrier((fetched, derivative))
     ours = added(ours, *fetched)
     other = swap(ours, "dp", line_swap(1))
-    odd = lax.axis_index("dp") % 2 == 1
-    gradient = jnp.concatenate([jnp.where(odd, other, ours), jnp.where(odd, ours, other)], axis=1)
     square_tally = lax.axis_size("dp") * height * strips * breadth
-    return scene[None], derivative[None], gradient / math.sqrt(square_tally)
+    gradient = pl.pallas_call(
+        functools.partial(gradient_kernel, 1.0 / math.sqrt(square_tally)),
+        out_shape=struct((share, planes), F32),
+        in_specs=[vmem()] * 2,
+        out_specs=vmem(),
+        compiler_params=params(2),
+        name="gradient",
+    )(ours, other)
+    return scene[None], derivative[None], gradient
 
 
 def solution(mesh):

time: 82.8 us -> 76.7 us (0.926)
  Pallas kernels: 18.9 us -> 14.5 us
  local copies, waits for them, and re-layouts: 2.51 us -> 1.02 us
    pallas_call x9 -> x11, Pallas kernels: 14.9 us -> 10.6 us  [the longest x1 3.41 us: on_device(): pl.pallas_call(functools.partial(hidden_kernel, breadth), out_shape=(held...]
    unnamed x18 -> x8, local copies, waits for them, and re-layouts: 2.5 us -> 1.02 us
  transfers between devices with their start and end apart: 21 -> 21, of which waited for: 13 -> 12; matrix products, arithmetic and copies ran while one was open for 0% -> 0% of each run, Pallas kernels for 8% -> 8%
where the time goes in v4:
time: 76.7 us; the launch traced here: 76.4 us
  starting transfers between devices  39.1 us (51%)
  waiting for transfers between devices  20.9 us (27%)
  Pallas kernels  14.5 us (19%)
  local copies, waits for them, and re-layouts  1.02 us (1%)
  between operations  0.79 us (1%)
    ppermute x21, starting transfers between devices, swap(): lax.ppermute(values, axis, [(i, partner(i)) for i in range(lax.axis_size(...  39.1 us
    ppermute x21, waiting for transfers between devices, swap(): lax.ppermute(values, axis, [(i, partner(i)) for i in range(lax.axis_size(...  20.9 us
    pallas_call x1, Pallas kernels, on_device(): pl.pallas_call(functools.partial(hidden_kernel, breadth), out_shape=(held...  3.41 us
    pallas_call x1, Pallas kernels, on_device(): pl.pallas_call(splat_kernel, out_shape=held((6, wide, planes), BF16), in_...  2.11 us
    pallas_call x1, Pallas kernels, on_device(): pl.pallas_call(functools.partial(derivative_kernel, breadth), out_shape=s...  2.01 us
    pallas_call x1, Pallas kernels, on_device(): pl.pallas_call(functools.partial(scene_kernel, breadth), out_shape=struct...  1.92 us
  transfers between devices with their start and end apart: 21, of which 12 were waited for; matrix products, arithmetic and copies ran while one was open for 0% of the time, Pallas kernels for 8%

profile of v4, /device:TPU:1, one launch (start us, length us, event | category | flops | bytes accessed | tf_op | source)
XLA Modules:
  0.0 76.4 jit_solution(10669847008776873779)
XLA Ops:
  0.6 1.5 %pack.1.refs_0_ = bf16[64,256]{1,0:T(8,128)(2,1)S(1)} custom-call(bf16[32,256]{1,0:T(8,128)(2,1)} %bitcast.21, bf16[32,64]{1,0:T(8,128)(2,1)} %bitcast.24, s32[32,64]{1,0:T(8,128)} %bitcast.22, s32[32,64]{1,0:T(8,128)} %bitcast.23, s32[1,32]{1,0:T(1,128)} %bitcast.25), custom_call_target="tpu_custom_call" | custom-call | tf_op jit(solution)/shard_map/pack/pallas_call | solution.py:386
  2.2 6.5 %collective-permute-start = (bf16[64,256]{1,0:T(8,128)(2,1)S(1)}, bf16[64,256]{1,0:T(8,128)(2,1)S(1)}, u32[]{:S(2)}, u32[]{:S(2)}) collective-permute-start(bf16[64,256]{1,0:T(8,128)(2,1)S(1)} %pack.1.refs_0_), channel_id=1, source_target_pairs={{0,28},{1,29},{2,30},{3,31},{4,24},{5,25},{6,26},{7,27},{8,20},{9,... | collective-permute-start | bytes 98312 | tf_op jit(solution)/shard_map/ppermute | solution.py:349
  8.7 1.3 %collective-permute-done.refs_1_ = bf16[64,256]{1,0:T(8,128)(2,1)S(1)} collective-permute-done((bf16[64,256]{1,0:T(8,128)(2,1)S(1)}, bf16[64,256]{1,0:T(8,128)(2,1)S(1)}, u32[]{:S(2)}, u32[]{:S(2)}) %collective-permute-start) | collective-permute-done | bytes 32800 | tf_op jit(solution)/shard_map/ppermute | solution.py:349
  10.0 0.2 line.1
  10.1 1.7 %collective-permute-start.1 = (bf16[80,256]{1,0:T(8,128)(2,1)S(1)}, bf16[80,256]{1,0:T(8,128)(2,1)S(1)}, u32[]{:S(2)}, u32[]{:S(2)}) collective-permute-start(bf16[80,256]{1,0:T(8,128)(2,1)S(1)} %get-tuple-element.43), channel_id=1, source_target_pairs={{0,4},{1,5},{2,6},{3,7},{4,0},{5,1},{6,2},{7,3},{8,12},{9,13},{10,... | collective-permute-start | bytes 122888 | tf_op jit(solution)/shard_map/ppermute | solution.py:349
  11.8 0.5 collective-permute-start.2
  12.4 1.6 %collective-permute-start.3 = (bf16[80,256]{1,0:T(8,128)(2,1)S(1)}, bf16[80,256]{1,0:T(8,128)(2,1)S(1)}, u32[]{:S(2)}, u32[]{:S(2)}) collective-permute-start(bf16[80,256]{1,0:T(8,128)(2,1)S(1)} %get-tuple-element.45), channel_id=1, source_target_pairs={{0,12},{1,13},{2,14},{3,15},{4,8},{5,9},{6,10},{7,11},{8,4},{9,5},... | collective-permute-start | bytes 122888 | tf_op jit(solution)/shard_map/ppermute | solution.py:349
  14.0 1.0 %copy-done.2 = bf16[1,2,400,256]{3,2,1,0:T(8,128)(2,1)S(1)} copy-done((bf16[1,2,400,256]{3,2,1,0:T(8,128)(2,1)S(1)}, bf16[1,2,400,256]{3,2,1,0:T(8,128)(2,1)}, u32[]{:S(2)}) %copy-start.2) | copy-done | bytes 409624
  15.0 0.2 moved.1
  15.3 0.6 collective-permute-done.2.refs_2_
  15.9 1.6 %collective-permute-done.3.refs_3_ = bf16[80,256]{1,0:T(8,128)(2,1)S(1)} collective-permute-done((bf16[80,256]{1,0:T(8,128)(2,1)S(1)}, bf16[80,256]{1,0:T(8,128)(2,1)S(1)}, u32[]{:S(2)}, u32[]{:S(2)}) %collective-permute-start.3) | collective-permute-done | bytes 40992 | tf_op jit(solution)/shard_map/ppermute | solution.py:349
  17.5 0.1 strip.1
  17.6 1.4 %collective-permute-start.6 = (bf16[288,256]{1,0:T(8,128)(2,1)S(1)}, bf16[288,256]{1,0:T(8,128)(2,1)S(1)}, u32[]{:S(2)}, u32[]{:S(2)}) collective-permute-start(bf16[288,256]{1,0:T(8,128)(2,1)S(1)} %get-tuple-element.53), channel_id=1, source_target_pairs={{0,1},{1,0},{2,3},{3,2},{4,5},{5,4},{6,7},{7,6},{8,9},{9,8},{10,11... | collective-permute-start | bytes 442376 | tf_op jit(solution)/shard_map/ppermute | solution.py:349
  18.9 2.6 %collective-permute-start.4 = (bf16[288,256]{1,0:T(8,128)(2,1)S(1)}, bf16[288,256]{1,0:T(8,128)(2,1)S(1)}, u32[]{:S(2)}, u32[]{:S(2)}) collective-permute-start(bf16[288,256]{1,0:T(8,128)(2,1)S(1)} %get-tuple-element.51), channel_id=1, source_target_pairs={{0,2},{1,3},{2,0},{3,1},{4,6},{5,7},{6,4},{7,5},{8,10},{9,11},{10,... | collective-permute-start | bytes 442376 | tf_op jit(solution)/shard_map/ppermute | solution.py:349
  21.6 0.0 collective-permute-start.5
  21.6 1.1 %plane.1.before = f32[6,400,256]{2,1,0:T(8,128)S(1)} custom-call(bf16[288,256]{1,0:T(8,128)(2,1)S(1)} %get-tuple-element.54.message), custom_call_target="tpu_custom_call" | custom-call | flops 629145600 | bytes 1000000 | tf_op jit(solution)/shard_map/plane/pallas_call | solution.py:447
  22.7 1.1 %more.1.before = f32[6,400,256]{2,1,0:T(8,128)S(1)} custom-call(bf16[288,256]{1,0:T(8,128)(2,1)S(1)} %collective-permute-done.6.message, f32[6,400,256]{2,1,0:T(8,128)S(1)} %plane.1.before), custom_call_target="tpu_custom_call" | custom-call | flops 629145600 | bytes 1000000 | tf_op jit(solution)/shard_map/more/pallas_call | solution.py:457
  23.8 0.0 copy-start
  23.8 1.9 %collective-permute-done.4.two = bf16[288,256]{1,0:T(8,128)(2,1)S(1)} collective-permute-done((bf16[288,256]{1,0:T(8,128)(2,1)S(1)}, bf16[288,256]{1,0:T(8,128)(2,1)S(1)}, u32[]{:S(2)}, u32[]{:S(2)}) %collective-permute-start.4) | collective-permute-done | bytes 147488 | tf_op jit(solution)/shard_map/ppermute | solution.py:349
  25.7 1.5 %collective-permute-done.5.three = bf16[288,256]{1,0:T(8,128)(2,1)S(1)} collective-permute-done((bf16[288,256]{1,0:T(8,128)(2,1)S(1)}, bf16[288,256]{1,0:T(8,128)(2,1)S(1)}, u32[]{:S(2)}, u32[]{:S(2)}) %collective-permute-start.5) | collective-permute-done | bytes 147488 | tf_op jit(solution)/shard_map/ppermute | solution.py:349
  27.3 2.1 %splat.1.bev = bf16[6,416,256]{2,1,0:T(8,128)(2,1)S(1)} custom-call(bf16[288,256]{1,0:T(8,128)(2,1)S(1)} %collective-permute-done.4.two, bf16[288,256]{1,0:T(8,128)(2,1)S(1)} %collective-permute-done.5.three, f32[6,400,256]{2,1,0:T(8,128)S(1)} %more.1.before), custom_call_target="tpu_custom_call" | custom-call | tf_op jit(solution)/shard_map/splat/pallas_call | solution.py:467
  29.4 3.4 %hidden.1 = (f32[2,416,256]{2,1,0:T(8,128)S(1)}, bf16[4,416,256]{2,1,0:T(8,128)(2,1)S(1)}, f32[2304,128]{1,0:T(8,128)S(1)}, bf16[2304,128]{1,0:T(8,128)(2,1)S(1)}) custom-call(bf16[6,416,256]{2,1,0:T(8,128)(2,1)S(1)} %splat.1.bev, bf16[2304,256]{1,0:T(8,128)(2,1)S(1)} %copy-done, bf16[2,416,768]{2,1,0:T(8,128)(2,1)S(1)} %get-tuple-element.55.shifted), custom_call_target="tpu_custom_call" | custom-call | tf_op jit(solution)/shard_map/hidden/pallas_call | solution.py:476
  32.8 0.0 copy-start.1
  32.8 4.0 %collective-permute-start.7 = (bf16[2304,128]{1,0:T(8,128)(2,1)S(1)}, bf16[2304,128]{1,0:T(8,128)(2,1)S(1)}, u32[]{:S(2)}, u32[]{:S(2)}) collective-permute-start(bf16[2304,128]{1,0:T(8,128)(2,1)S(1)} %get-tuple-element.57), channel_id=1, source_target_pairs={{0,32},{32,0},{64,96},{96,64},{128,160},{160,128},{192,224},{224,1... | collective-permute-start | bytes 1769480 | tf_op jit(solution)/shard_map/ppermute | solution.py:349
  36.8 1.6 %collective-permute-done.7 = bf16[2304,128]{1,0:T(8,128)(2,1)S(1)} collective-permute-done((bf16[2304,128]{1,0:T(8,128)(2,1)S(1)}, bf16[2304,128]{1,0:T(8,128)(2,1)S(1)}, u32[]{:S(2)}, u32[]{:S(2)}) %collective-permute-start.7) | collective-permute-done | bytes 589856 | tf_op jit(solution)/shard_map/ppermute | solution.py:349
  38.4 0.1 parts.1
  38.5 0.1 collective-permute-start.8
  38.6 2.0 %collective-permute-start.9 = (bf16[8,72,128]{2,1,0:T(8,128)(2,1)S(1)}, bf16[8,72,128]{2,1,0:T(8,128)(2,1)S(1)}, u32[]{:S(2)}, u32[]{:S(2)}) collective-permute-start(bf16[8,72,128]{2,1,0:T(8,128)(2,1)S(1)} %get-tuple-element.59), channel_id=1, source_target_pairs={{0,2},{1,3},{2,0},{3,1},{4,6},{5,7},{6,4},{7,5},{8,10},{9,11},{10,... | collective-permute-start | bytes 442376 | tf_op jit(solution)/shard_map/ppermute | solution.py:349
  40.7 1.8 %collective-permute-start.10 = (bf16[8,72,128]{2,1,0:T(8,128)(2,1)S(1)}, bf16[8,72,128]{2,1,0:T(8,128)(2,1)S(1)}, u32[]{:S(2)}, u32[]{:S(2)}) collective-permute-start(bf16[8,72,128]{2,1,0:T(8,128)(2,1)S(1)} %get-tuple-element.60), channel_id=1, source_target_pairs={{0,3},{1,2},{2,1},{3,0},{4,7},{5,6},{6,5},{7,4},{8,11},{9,10},{10,... | collective-permute-start | bytes 442376 | tf_op jit(solution)/shard_map/ppermute | solution.py:349
  42.5 1.9 %scene.1 = bf16[2,400,256]{2,1,0:T(8,128)(2,1)} custom-call(bf16[6,416,256]{2,1,0:T(8,128)(2,1)S(1)} %splat.1.bev, bf16[4,416,256]{2,1,0:T(8,128)(2,1)S(1)} %get-tuple-element.61.hidden, bf16[2304,256]{1,0:T(8,128)(2,1)S(1)} %copy-done.1), custom_call_target="tpu_custom_call" | custom-call | flops 981467136 | bytes 1000000 | tf_op jit(solution)/shard_map/scene/pallas_call | solution.py:501
  44.4 3.1 %collective-permute-done.9.two = bf16[8,72,128]{2,1,0:T(8,128)(2,1)S(1)} collective-permute-done((bf16[8,72,128]{2,1,0:T(8,128)(2,1)S(1)}, bf16[8,72,128]{2,1,0:T(8,128)(2,1)S(1)}, u32[]{:S(2)}, u32[]{:S(2)}) %collective-permute-start.9) | collective-permute-done | bytes 147488 | tf_op jit(solution)/shard_map/ppermute | solution.py:349
  47.5 2.5 %collective-permute-done.10.three = bf16[8,72,128]{2,1,0:T(8,128)(2,1)S(1)} collective-permute-done((bf16[8,72,128]{2,1,0:T(8,128)(2,1)S(1)}, bf16[8,72,128]{2,1,0:T(8,128)(2,1)S(1)}, u32[]{:S(2)}, u32[]{:S(2)}) %collective-permute-start.10) | collective-permute-done | bytes 147488 | tf_op jit(solution)/shard_map/ppermute | solution.py:349
  50.0 0.1 planes.1
  50.1 0.1 collective-permute-start.11
  50.2 1.8 %collective-permute-start.12 = (bf16[2,72,128]{2,1,0:T(8,128)(2,1)S(1)}, bf16[2,72,128]{2,1,0:T(8,128)(2,1)S(1)}, u32[]{:S(2)}, u32[]{:S(2)}) collective-permute-start(bf16[2,72,128]{2,1,0:T(8,128)(2,1)S(1)} %get-tuple-element.69), channel_id=1, source_target_pairs={{0,8},{1,9},{2,10},{3,11},{4,12},{5,13},{6,14},{7,15},{8,0},{9,1},... | collective-permute-start | bytes 110600 | tf_op jit(solution)/shard_map/ppermute | solution.py:349
  52.0 1.7 %collective-permute-start.13 = (bf16[2,72,128]{2,1,0:T(8,128)(2,1)S(1)}, bf16[2,72,128]{2,1,0:T(8,128)(2,1)S(1)}, u32[]{:S(2)}, u32[]{:S(2)}) collective-permute-start(bf16[2,72,128]{2,1,0:T(8,128)(2,1)S(1)} %get-tuple-element.70), channel_id=1, source_target_pairs={{0,12},{1,13},{2,14},{3,15},{4,8},{5,9},{6,10},{7,11},{8,4},{9,5},... | collective-permute-start | bytes 110600 | tf_op jit(solution)/shard_map/ppermute | solution.py:349
  53.7 0.3 collective-permute-done.12
  54.0 2.8 %collective-permute-done.13 = bf16[2,72,128]{2,1,0:T(8,128)(2,1)S(1)} collective-permute-done((bf16[2,72,128]{2,1,0:T(8,128)(2,1)S(1)}, bf16[2,72,128]{2,1,0:T(8,128)(2,1)S(1)}, u32[]{:S(2)}, u32[]{:S(2)}) %collective-permute-start.13) | collective-permute-done | bytes 36896 | tf_op jit(solution)/shard_map/ppermute | solution.py:349
  56.8 3.9 %collective-permute-start.14 = (bf16[72,128]{1,0:T(8,128)(2,1)S(1)}, bf16[72,128]{1,0:T(8,128)(2,1)S(1)}, u32[]{:S(2)}, u32[]{:S(2)}) collective-permute-start(bf16[72,128]{1,0:T(8,128)(2,1)S(1)} %fusion.1), channel_id=1, source_target_pairs={{0,28},{1,29},{2,30},{3,31},{4,24},{5,25},{6,26},{7,27},{8,20},{9,... | collective-permute-start | bytes 55304 | tf_op jit(solution)/shard_map/ppermute | solution.py:349
  60.7 1.7 %collective-permute-start.19 = (bf16[400,256]{1,0:T(8,128)(2,1)S(1)}, bf16[400,256]{1,0:T(8,128)(2,1)S(1)}, u32[]{:S(2)}, u32[]{:S(2)}) collective-permute-start(bf16[400,256]{1,0:T(8,128)(2,1)S(1)} %get-tuple-element.75), channel_id=1, source_target_pairs={{0,31},{1,2},{2,1},{3,4},{4,3},{5,6},{6,5},{7,8},{8,7},{9,10},{10,... | collective-permute-start | bytes 614408 | tf_op jit(solution)/shard_map/ppermute | solution.py:349
  62.5 2.6 %collective-permute-start.17 = (f32[72,128]{1,0:T(8,128)S(1)}, f32[72,128]{1,0:T(8,128)S(1)}, u32[]{:S(2)}, u32[]{:S(2)}) collective-permute-start(f32[72,128]{1,0:T(8,128)S(1)} %fusion), channel_id=1, source_target_pairs={{0,192},{32,224},{64,128},{96,160},{128,64},{160,96},{192,0},{224,... | collective-permute-start | bytes 110600 | tf_op jit(solution)/shard_map/ppermute | solution.py:349
  65.0 0.5 collective-permute-start.16
  65.6 0.2 collective-permute-start.15
  65.8 2.9 %collective-permute-done.19.second = bf16[400,256]{1,0:T(8,128)(2,1)S(1)} collective-permute-done((bf16[400,256]{1,0:T(8,128)(2,1)S(1)}, bf16[400,256]{1,0:T(8,128)(2,1)S(1)}, u32[]{:S(2)}, u32[]{:S(2)}) %collective-permute-start.19) | collective-permute-done | bytes 204832 | tf_op jit(solution)/shard_map/ppermute | solution.py:349
  68.7 2.0 %derivative.1 = bf16[2,400,256]{2,1,0:T(8,128)(2,1)} custom-call(bf16[2,400,256]{2,1,0:T(8,128)(2,1)S(1)} %bitcast.19, bf16[400,256]{1,0:T(8,128)(2,1)S(1)} %collective-permute-done.18.first, bf16[400,256]{1,0:T(8,128)(2,1)S(1)} %collective-permute-done.19.second, bf16[2304,256]{1,0:T(8,128)(2,1)S(1)} %copy-done.1, f32[2,416,256]{2,1,0:T(8,128)S(1)} %get-tuple-element.76.pre), custom_call_target="tpu_custom_call" | custom-call | flops 981467136 | bytes 1000000 | tf_op jit(solution)/shard_map/derivative/pallas_call | solution.py:528
  70.7 4.2 %collective-permute-start.20 = (f32[72,128]{1,0:T(8,128)S(1)}, f32[72,128]{1,0:T(8,128)S(1)}, u32[]{:S(2)}, u32[]{:S(2)}) collective-permute-start(f32[72,128]{1,0:T(8,128)S(1)} %add_add_fusion.ours), channel_id=1, source_target_pairs={{0,32},{32,0},{64,96},{96,64},{128,160},{160,128},{192,224},{224,1... | collective-permute-start | bytes 110600 | tf_op jit(solution)/shard_map/ppermute | solution.py:349
  74.9 0.9 %collective-permute-done.20.other = f32[72,128]{1,0:T(8,128)S(1)} collective-permute-done((f32[72,128]{1,0:T(8,128)S(1)}, f32[72,128]{1,0:T(8,128)S(1)}, u32[]{:S(2)}, u32[]{:S(2)}) %collective-permute-start.20) | collective-permute-done | bytes 36896 | tf_op jit(solution)/shard_map/ppermute | solution.py:349
  75.8 0.6 gradient.1
  (19 shorter events, 0.1 us)
Async XLA Ops:
  2.2 7.8 %collective-permute-start = (bf16[64,256]{1,0:T(8,128)(2,1)S(1)}, bf16[64,256]{1,0:T(8,128)(2,1)S(1)}, u32[]{:S(2)}, u32[]{:S(2)}) collective-permute-start(bf16[64,256]{1,0:T(8,128)(2,1)S(1)} %pack.1.refs_0_), channel_id=1, source_target_pairs={{0,28},{1,29},{2,30},{3,31},{4,24},{5,25},{6,26},{7,27},{8,20},{9,... | collective-permute-start | bytes 98312 | tf_op jit(solution)/shard_map/ppermute | solution.py:349
  10.1 5.1 %collective-permute-start.1 = (bf16[80,256]{1,0:T(8,128)(2,1)S(1)}, bf16[80,256]{1,0:T(8,128)(2,1)S(1)}, u32[]{:S(2)}, u32[]{:S(2)}) collective-permute-start(bf16[80,256]{1,0:T(8,128)(2,1)S(1)} %get-tuple-element.43), channel_id=1, source_target_pairs={{0,4},{1,5},{2,6},{3,7},{4,0},{5,1},{6,2},{7,3},{8,12},{9,13},{10,... | collective-permute-start | bytes 122888 | tf_op jit(solution)/shard_map/ppermute | solution.py:349
  11.8 4.0 %collective-permute-start.2 = (bf16[80,256]{1,0:T(8,128)(2,1)S(1)}, bf16[80,256]{1,0:T(8,128)(2,1)S(1)}, u32[]{:S(2)}, u32[]{:S(2)}) collective-permute-start(bf16[80,256]{1,0:T(8,128)(2,1)S(1)} %get-tuple-element.44), channel_id=1, source_target_pairs={{0,8},{1,9},{2,10},{3,11},{4,12},{5,13},{6,14},{7,15},{8,0},{9,1},... | collective-permute-start | bytes 122888 | tf_op jit(solution)/shard_map/ppermute | solution.py:349
  12.4 5.1 %collective-permute-start.3 = (bf16[80,256]{1,0:T(8,128)(2,1)S(1)}, bf16[80,256]{1,0:T(8,128)(2,1)S(1)}, u32[]{:S(2)}, u32[]{:S(2)}) collective-permute-start(bf16[80,256]{1,0:T(8,128)(2,1)S(1)} %get-tuple-element.45), channel_id=1, source_target_pairs={{0,12},{1,13},{2,14},{3,15},{4,8},{5,9},{6,10},{7,11},{8,4},{9,5},... | collective-permute-start | bytes 122888 | tf_op jit(solution)/shard_map/ppermute | solution.py:349
  14.0 1.0 %copy-start.2 = (bf16[1,2,400,256]{3,2,1,0:T(8,128)(2,1)S(1)}, bf16[1,2,400,256]{3,2,1,0:T(8,128)(2,1)}, u32[]{:S(2)}) copy-start(bf16[1,2,400,256]{3,2,1,0:T(8,128)(2,1)} %param.13) | copy-start | bytes 1228804
  17.6 5.1 %collective-permute-start.6 = (bf16[288,256]{1,0:T(8,128)(2,1)S(1)}, bf16[288,256]{1,0:T(8,128)(2,1)S(1)}, u32[]{:S(2)}, u32[]{:S(2)}) collective-permute-start(bf16[288,256]{1,0:T(8,128)(2,1)S(1)} %get-tuple-element.53), channel_id=1, source_target_pairs={{0,1},{1,0},{2,3},{3,2},{4,5},{5,4},{6,7},{7,6},{8,9},{9,8},{10,11... | collective-permute-start | bytes 442376 | tf_op jit(solution)/shard_map/ppermute | solution.py:349
  18.9 6.8 %collective-permute-start.4 = (bf16[288,256]{1,0:T(8,128)(2,1)S(1)}, bf16[288,256]{1,0:T(8,128)(2,1)S(1)}, u32[]{:S(2)}, u32[]{:S(2)}) collective-permute-start(bf16[288,256]{1,0:T(8,128)(2,1)S(1)} %get-tuple-element.51), channel_id=1, source_target_pairs={{0,2},{1,3},{2,0},{3,1},{4,6},{5,7},{6,4},{7,5},{8,10},{9,11},{10,... | collective-permute-start | bytes 442376 | tf_op jit(solution)/shard_map/ppermute | solution.py:349
  21.6 5.7 %collective-permute-start.5 = (bf16[288,256]{1,0:T(8,128)(2,1)S(1)}, bf16[288,256]{1,0:T(8,128)(2,1)S(1)}, u32[]{:S(2)}, u32[]{:S(2)}) collective-permute-start(bf16[288,256]{1,0:T(8,128)(2,1)S(1)} %get-tuple-element.52), channel_id=1, source_target_pairs={{0,3},{1,2},{2,1},{3,0},{4,7},{5,6},{6,5},{7,4},{8,11},{9,10},{10,... | collective-permute-start | bytes 442376 | tf_op jit(solution)/shard_map/ppermute | solution.py:349
  23.8 5.6 %copy-start = (bf16[2304,256]{1,0:T(8,128)(2,1)S(1)}, bf16[2304,256]{1,0:T(8,128)(2,1)}, u32[]{:S(2)}) copy-start(bf16[2304,256]{1,0:T(8,128)(2,1)} %weight.3) | copy-start | bytes 3538948
  32.8 9.7 %copy-start.1 = (bf16[2304,256]{1,0:T(8,128)(2,1)S(1)}, bf16[2304,256]{1,0:T(8,128)(2,1)}, u32[]{:S(2)}) copy-start(bf16[2304,256]{1,0:T(8,128)(2,1)} %weight.5) | copy-start | bytes 3538948
  32.8 5.6 %collective-permute-start.7 = (bf16[2304,128]{1,0:T(8,128)(2,1)S(1)}, bf16[2304,128]{1,0:T(8,128)(2,1)S(1)}, u32[]{:S(2)}, u32[]{:S(2)}) collective-permute-start(bf16[2304,128]{1,0:T(8,128)(2,1)S(1)} %get-tuple-element.57), channel_id=1, source_target_pairs={{0,32},{32,0},{64,96},{96,64},{128,160},{160,128},{192,224},{224,1... | collective-permute-start | bytes 1769480 | tf_op jit(solution)/shard_map/ppermute | solution.py:349
  38.5 5.9 %collective-permute-start.8 = (bf16[8,72,128]{2,1,0:T(8,128)(2,1)S(1)}, bf16[8,72,128]{2,1,0:T(8,128)(2,1)S(1)}, u32[]{:S(2)}, u32[]{:S(2)}) collective-permute-start(bf16[8,72,128]{2,1,0:T(8,128)(2,1)S(1)} %get-tuple-element.58), channel_id=1, source_target_pairs={{0,1},{1,0},{2,3},{3,2},{4,5},{5,4},{6,7},{7,6},{8,9},{9,8},{10,11... | collective-permute-start | bytes 442376 | tf_op jit(solution)/shard_map/ppermute | solution.py:349
  38.6 8.8 %collective-permute-start.9 = (bf16[8,72,128]{2,1,0:T(8,128)(2,1)S(1)}, bf16[8,72,128]{2,1,0:T(8,128)(2,1)S(1)}, u32[]{:S(2)}, u32[]{:S(2)}) collective-permute-start(bf16[8,72,128]{2,1,0:T(8,128)(2,1)S(1)} %get-tuple-element.59), channel_id=1, source_target_pairs={{0,2},{1,3},{2,0},{3,1},{4,6},{5,7},{6,4},{7,5},{8,10},{9,11},{10,... | collective-permute-start | bytes 442376 | tf_op jit(solution)/shard_map/ppermute | solution.py:349
  40.7 9.3 %collective-permute-start.10 = (bf16[8,72,128]{2,1,0:T(8,128)(2,1)S(1)}, bf16[8,72,128]{2,1,0:T(8,128)(2,1)S(1)}, u32[]{:S(2)}, u32[]{:S(2)}) collective-permute-start(bf16[8,72,128]{2,1,0:T(8,128)(2,1)S(1)} %get-tuple-element.60), channel_id=1, source_target_pairs={{0,3},{1,2},{2,1},{3,0},{4,7},{5,6},{6,5},{7,4},{8,11},{9,10},{10,... | collective-permute-start | bytes 442376 | tf_op jit(solution)/shard_map/ppermute | solution.py:349
  42.5 26.2 %copy-start.3 = (bf16[1,2,400,256]{3,2,1,0:T(8,128)(2,1)S(1)}, bf16[1,2,400,256]{3,2,1,0:T(8,128)(2,1)}, u32[]{:S(2)}) copy-start(bf16[1,2,400,256]{3,2,1,0:T(8,128)(2,1)} %param.13) | copy-start | bytes 1228804
  50.1 3.6 %collective-permute-start.11 = (bf16[2,72,128]{2,1,0:T(8,128)(2,1)S(1)}, bf16[2,72,128]{2,1,0:T(8,128)(2,1)S(1)}, u32[]{:S(2)}, u32[]{:S(2)}) collective-permute-start(bf16[2,72,128]{2,1,0:T(8,128)(2,1)S(1)} %get-tuple-element.68), channel_id=1, source_target_pairs={{0,4},{1,5},{2,6},{3,7},{4,0},{5,1},{6,2},{7,3},{8,12},{9,13},{10,... | collective-permute-start | bytes 110600 | tf_op jit(solution)/shard_map/ppermute | solution.py:349
  50.2 3.8 %collective-permute-start.12 = (bf16[2,72,128]{2,1,0:T(8,128)(2,1)S(1)}, bf16[2,72,128]{2,1,0:T(8,128)(2,1)S(1)}, u32[]{:S(2)}, u32[]{:S(2)}) collective-permute-start(bf16[2,72,128]{2,1,0:T(8,128)(2,1)S(1)} %get-tuple-element.69), channel_id=1, source_target_pairs={{0,8},{1,9},{2,10},{3,11},{4,12},{5,13},{6,14},{7,15},{8,0},{9,1},... | collective-permute-start | bytes 110600 | tf_op jit(solution)/shard_map/ppermute | solution.py:349
  52.0 4.8 %collective-permute-start.13 = (bf16[2,72,128]{2,1,0:T(8,128)(2,1)S(1)}, bf16[2,72,128]{2,1,0:T(8,128)(2,1)S(1)}, u32[]{:S(2)}, u32[]{:S(2)}) collective-permute-start(bf16[2,72,128]{2,1,0:T(8,128)(2,1)S(1)} %get-tuple-element.70), channel_id=1, source_target_pairs={{0,12},{1,13},{2,14},{3,15},{4,8},{5,9},{6,10},{7,11},{8,4},{9,5},... | collective-permute-start | bytes 110600 | tf_op jit(solution)/shard_map/ppermute | solution.py:349
  56.8 5.6 %collective-permute-start.14 = (bf16[72,128]{1,0:T(8,128)(2,1)S(1)}, bf16[72,128]{1,0:T(8,128)(2,1)S(1)}, u32[]{:S(2)}, u32[]{:S(2)}) collective-permute-start(bf16[72,128]{1,0:T(8,128)(2,1)S(1)} %fusion.1), channel_id=1, source_target_pairs={{0,28},{1,29},{2,30},{3,31},{4,24},{5,25},{6,26},{7,27},{8,20},{9,... | collective-permute-start | bytes 55304 | tf_op jit(solution)/shard_map/ppermute | solution.py:349
  60.7 5.1 %collective-permute-start.18 = (bf16[400,256]{1,0:T(8,128)(2,1)S(1)}, bf16[400,256]{1,0:T(8,128)(2,1)S(1)}, u32[]{:S(2)}, u32[]{:S(2)}) collective-permute-start(bf16[400,256]{1,0:T(8,128)(2,1)S(1)} %get-tuple-element.74), channel_id=1, source_target_pairs={{0,1},{1,0},{2,3},{3,2},{4,5},{5,4},{6,7},{7,6},{8,9},{9,8},{10,11... | collective-permute-start | bytes 614408 | tf_op jit(solution)/shard_map/ppermute | solution.py:349
  60.7 7.9 %collective-permute-start.19 = (bf16[400,256]{1,0:T(8,128)(2,1)S(1)}, bf16[400,256]{1,0:T(8,128)(2,1)S(1)}, u32[]{:S(2)}, u32[]{:S(2)}) collective-permute-start(bf16[400,256]{1,0:T(8,128)(2,1)S(1)} %get-tuple-element.75), channel_id=1, source_target_pairs={{0,31},{1,2},{2,1},{3,4},{4,3},{5,6},{6,5},{7,8},{8,7},{9,10},{10,... | collective-permute-start | bytes 614408 | tf_op jit(solution)/shard_map/ppermute | solution.py:349
  62.5 8.2 %collective-permute-start.17 = (f32[72,128]{1,0:T(8,128)S(1)}, f32[72,128]{1,0:T(8,128)S(1)}, u32[]{:S(2)}, u32[]{:S(2)}) collective-permute-start(f32[72,128]{1,0:T(8,128)S(1)} %fusion), channel_id=1, source_target_pairs={{0,192},{32,224},{64,128},{96,160},{128,64},{160,96},{192,0},{224,... | collective-permute-start | bytes 110600 | tf_op jit(solution)/shard_map/ppermute | solution.py:349
  65.0 5.7 %collective-permute-start.16 = (f32[72,128]{1,0:T(8,128)S(1)}, f32[72,128]{1,0:T(8,128)S(1)}, u32[]{:S(2)}, u32[]{:S(2)}) collective-permute-start(f32[72,128]{1,0:T(8,128)S(1)} %fusion), channel_id=1, source_target_pairs={{0,128},{32,160},{64,192},{96,224},{128,0},{160,32},{192,64},{224,... | collective-permute-start | bytes 110600 | tf_op jit(solution)/shard_map/ppermute | solution.py:349
  65.6 5.1 %collective-permute-start.15 = (f32[72,128]{1,0:T(8,128)S(1)}, f32[72,128]{1,0:T(8,128)S(1)}, u32[]{:S(2)}, u32[]{:S(2)}) collective-permute-start(f32[72,128]{1,0:T(8,128)S(1)} %fusion), channel_id=1, source_target_pairs={{0,64},{32,96},{64,0},{96,32},{128,192},{160,224},{192,128},{224,1... | collective-permute-start | bytes 110600 | tf_op jit(solution)/shard_map/ppermute | solution.py:349
  70.7 5.1 %collective-permute-start.20 = (f32[72,128]{1,0:T(8,128)S(1)}, f32[72,128]{1,0:T(8,128)S(1)}, u32[]{:S(2)}, u32[]{:S(2)}) collective-permute-start(f32[72,128]{1,0:T(8,128)S(1)} %add_add_fusion.ours), channel_id=1, source_target_pairs={{0,32},{32,0},{64,96},{96,64},{128,160},{160,128},{192,224},{224,1... | collective-permute-start | bytes 110600 | tf_op jit(solution)/shard_map/ppermute | solution.py:349

commit v5 on v4

--- a/solution.py
+++ b/solution.py
@@ -198,8 +198,8 @@
         sums[k] = before[k] + splat_row(k, meta, lifted, onehot)
 
 
-def splat_kernel(two, three, before, bev, meta, lifted, onehot):
-    lift([two, three], meta, lifted)
+def splat_kernel(message, before, bev, meta, lifted, onehot):
+    lift([message], meta, lifted)
     for k in range(6):
         normalized(before[k] + splat_row(k, meta, lifted, onehot), bev, k)
 
@@ -231,28 +231,42 @@
     return lax.broadcasted_iota(jnp.int32, shape, 0) < breadth
 
 
-def moved_kernel(breadth, own, shifted, near, far):
+def moved_kernel(breadth, own, kept, given, near, far):
     odd = lax.axis_index("tile") % 2 == 1
     near[...] = jnp.where(odd, own[0], own[1])
     far[...] = jnp.where(odd, own[1], own[0])
-    wide = shifted.shape[1]
+    right_core = lax.axis_index("dp") % 2 == 1
+    wide = kept.shape[1]
     planes = own.shape[2]
+    half = planes // 2
     filler = jnp.zeros((wide - breadth, planes), F32)
     for y in range(2):
         row = jnp.concatenate([own[y].astype(F32), filler], axis=0)
         for b in range(3):
-            shifted[y, :, b * planes : (b + 1) * planes] = turned(row, b - 1).astype(BF16)
-
-
-def hidden_kernel(breadth, bev, weight, shifted, pre, hidden, kept, given):
+            value = turned(row, b - 1).astype(BF16)
+            left, right = value[:, :half], value[:, half:]
+            at = slice(b * half, (b + 1) * half)
+            kept[y, :, at] = jnp.where(right_core, right, left)
+            given[y, :, at] = jnp.where(right_core, left, right)
+
+
+def gradient_terms(columns, cotangent, terms):
+    half = terms.shape[1]
+    planes = columns.shape[1]
+    for a in range(3):
+        term = jnp.dot(columns[a], cotangent[0], preferred_element_type=F32)
+        term = term + jnp.dot(columns[a + 1], cotangent[1], preferred_element_type=F32)
+        for b in range(3):
+            at = slice((a * 3 + b) * planes, (a * 3 + b + 1) * planes)
+            terms[at] = term[:, b * half : (b + 1) * half].astype(terms.dtype)
+
+
+def hidden_kernel(breadth, bev, weight, cotangent, pre, hidden, columns, given):
     wide, planes = bev.shape[1:]
     strip = lax.axis_index("tile")
     last = lax.axis_size("tile") - 1
-    odd = lax.axis_index("dp") % 2 == 1
-    half = planes // 2
     grid = wide_weight(weight, planes)
     mask = inside((wide, planes), breadth)
-    columns = []
     for k in range(4):
         value = conv_row(bev, k + 1, grid)
         if k in (1, 2):
@@ -264,16 +278,8 @@
             keep = jnp.logical_and(mask, strip != last)
         active = jnp.where(keep, value * jax.nn.sigmoid(value), 0.0)
         hidden[k] = active.astype(BF16)
-        columns.append(active.T.astype(BF16))
-    for a in range(3):
-        terms = jnp.dot(columns[a], shifted[0], preferred_element_type=F32)
-        terms = terms + jnp.dot(columns[a + 1], shifted[1], preferred_element_type=F32)
-        for b in range(3):
-            left = terms[:, b * planes : b * planes + half]
-            right = terms[:, b * planes + half : (b + 1) * planes]
-            at = slice((a * 3 + b) * planes, (a * 3 + b + 1) * planes)
-            kept[at] = jnp.where(odd, right, left)
-            given[at] = jnp.where(odd, left, right).astype(BF16)
+        columns[k] = active.T.astype(BF16)
+    gradient_terms(columns, cotangent, given)
 
 
 def scene_kernel(breadth, bev, hidden, weight, scene):
@@ -415,16 +421,16 @@
     )(packed, swap(packed, "tile", mirror))
     line = [line[0]] + [swap(line[k], "tile", line_swap(4 * k)) for k in (1, 2, 3)]
     own = predicted_adjoint[0]
-    shifted, near, far = pl.pallas_call(
+    keep, give, near, far = pl.pallas_call(
         functools.partial(moved_kernel, breadth),
-        out_shape=(held((2, wide, 3 * planes), BF16),) + (held((breadth, planes), BF16),) * 2,
+        out_shape=(held((2, wide, 3 * half), BF16),) * 2 + (held((breadth, planes), BF16),) * 2,
         in_specs=[vmem()],
-        out_specs=(vmem(),) * 3,
+        out_specs=(vmem(),) * 4,
         compiler_params=params(4),
         cost_estimate=pl.CostEstimate(flops=10**6, bytes_accessed=10**6, transcendentals=0),
         name="moved",
     )(own)
-    line, shifted = lax.optimization_barrier((line, shifted))
+    line, keep, give = lax.optimization_barrier((line, keep, give))
     messages = pl.pallas_call(
         strip_kernel,
         out_shape=(held((9 * pixels, planes), BF16),) * 4,
@@ -464,31 +470,51 @@
         cost_estimate=pl.CostEstimate(flops=2 * 6 * breadth * 8 * slots * planes, bytes_accessed=10**6, transcendentals=0),
         name="more",
     )(arrived[0], sums)
+    sums = pl.pallas_call(
+        more_kernel,
+        out_shape=held((6, breadth, planes), F32),
+        in_specs=[vmem()] * 2,
+        out_specs=vmem(),
+        scratch_shapes=splat_scratch(1),
+        compiler_params=params(8),
+        cost_estimate=pl.CostEstimate(flops=2 * 6 * breadth * 8 * slots * planes, bytes_accessed=10**6, transcendentals=0),
+        name="again",
+    )(arrived[1], sums)
     bev = pl.pallas_call(
         splat_kernel,
         out_shape=held((6, wide, planes), BF16),
-        in_specs=[vmem()] * 3,
-        out_specs=vmem(),
-        scratch_shapes=splat_scratch(2),
-        compiler_params=params(12),
+        in_specs=[vmem()] * 2,
+        out_specs=vmem(),
+        scratch_shapes=splat_scratch(1),
+        compiler_params=params(8),
         name="splat",
-    )(arrived[1], arrived[2], sums)
-    pre, hidden, kept, given = pl.pallas_call(
+    )(arrived[2], sums)
+    pre, hidden, columns, given = pl.pallas_call(
         functools.partial(hidden_kernel, breadth),
         out_shape=(
             held((2, wide, planes), F32),
             held((4, wide, planes), BF16),
-            held((taps, half), F32),
+            held((4, planes, wide), BF16),
             held((taps, half), BF16),
         ),
         in_specs=[vmem()] * 3,
         out_specs=(vmem(),) * 4,
         compiler_params=params(10),
         name="hidden",
-    )(bev, initial_plane_filter, shifted)
+    )(bev, initial_plane_filter, give)
+    taken = swap(given, "dp", line_swap(1))
+    kept = pl.pallas_call(
+        gradient_terms,
+        out_shape=held((taps, half), F32),
+        in_specs=[vmem()] * 2,
+        out_specs=vmem(),
+        compiler_params=params(8),
+        cost_estimate=pl.CostEstimate(flops=4 * wide * taps * half, bytes_accessed=10**6, transcendentals=0),
+        name="kept",
+    )(columns, keep)
+    kept, taken = lax.optimization_barrier((kept, taken))
 
     share = taps // strips
-    taken = swap(given, "dp", line_swap(1))
     parts = pl.pallas_call(
         parts_kernel,
         out_shape=tuple(held((strips // 4, share, half), F32 if k == 0 else BF16) for k in range(4)),
@@ -519,12 +545,12 @@
     fetched = [swap(pairs[k], "tile", line_swap(4 * k)) for k in (1, 2, 3)]
     pair = added(pairs[0], *fetched)
     ours = pair[0]
-    theirs = pair[1].astype(BF16)
-    theirs, near, far = lax.optimization_barrier((theirs, near, far))
-    ours = added(ours, swap(theirs, "tile", mirror))
+    theirs, near, far = lax.optimization_barrier((pair[1].astype(BF16), near, far))
     first = swap(near, "tile", line_swap(1))
     second = swap(far, "tile", lambda i: (i - 1 + 2 * (i % 2)) % strips)
-    fetched = [swap(ours, "dp", line_swap(2 * k)) for k in (1, 2, 3)]
+    ours = added(ours, swap(theirs, "tile", mirror))
+    fetched = [swap(ours.astype(BF16), "dp", line_swap(2 * k)) for k in (1, 2, 3)]
+    fetched, first, second = lax.optimization_barrier((fetched, first, second))
     derivative = pl.pallas_call(
         functools.partial(derivative_kernel, breadth),
         out_shape=struct((2, breadth, planes), BF16),
@@ -535,9 +561,8 @@
         cost_estimate=pl.CostEstimate(flops=2 * 2 * wide * taps * planes, bytes_accessed=10**6, transcendentals=10**6),
         name="derivative",
     )(own, first, second, predictor_filter, pre)
-    fetched, derivative = lax.optimization_barrier((fetched, derivative))
     ours = added(ours, *fetched)
-    other = swap(ours, "dp", line_swap(1))
+    other, derivative = lax.optimization_barrier((swap(ours, "dp", line_swap(1)), derivative))
     square_tally = lax.axis_size("dp") * height * strips * breadth
     gradient = pl.pallas_call(
         functools.partial(gradient_kernel, 1.0 / math.sqrt(square_tally)),

time: 76.7 us -> 75.7 us (0.987)
  waiting for transfers between devices: 20.9 us -> 18.2 us
  Pallas kernels: 14.5 us -> 15.5 us
    ppermute x21, waiting for transfers between devices: 20.9 us -> 18.2 us  [swap(): lax.ppermute(values, axis, [(i, partner(i)) for i in range(lax.axis_size(...]
    pallas_call x1 -> x2, Pallas kernels: 1.11 us -> 2.21 us  [on_device(): pl.pallas_call(more_kernel, out_shape=held((6, breadth, planes), F32), in...]
    pallas_call x0 -> x1, Pallas kernels: none -> 0.97 us  [on_device(): pl.pallas_call(gradient_terms, out_shape=held((taps, half), F32), in_spec...]
    pallas_call x1, Pallas kernels: 2.11 us -> 1.28 us  [on_device(): pl.pallas_call(splat_kernel, out_shape=held((6, wide, planes), BF16), in_...]
  transfers between devices with their start and end apart: 21 -> 21, of which waited for: 12 -> 12; matrix products, arithmetic and copies ran while one was open for 0% -> 0% of each run, Pallas kernels for 8% -> 11%
where the time goes in v5:
time: 75.7 us; the launch traced here: 75.4 us
  starting transfers between devices  39.8 us (53%)
  waiting for transfers between devices  18.2 us (24%)
  Pallas kernels  15.5 us (20%)
  local copies, waits for them, and re-layouts  1.02 us (1%)
  between operations  0.81 us (1%)
    ppermute x21, starting transfers between devices, swap(): lax.ppermute(values, axis, [(i, partner(i)) for i in range(lax.axis_size(...  39.8 us
    ppermute x21, waiting for transfers between devices, swap(): lax.ppermute(values, axis, [(i, partner(i)) for i in range(lax.axis_size(...  18.2 us
    pallas_call x1, Pallas kernels, on_device(): pl.pallas_call(functools.partial(hidden_kernel, breadth), out_shape=(held...  3.05 us
    pallas_call x2, Pallas kernels, on_device(): pl.pallas_call(more_kernel, out_shape=held((6, breadth, planes), F32), in...  2.21 us
    pallas_call x1, Pallas kernels, on_device(): pl.pallas_call(functools.partial(derivative_kernel, breadth), out_shape=s...  2.01 us
    pallas_call x1, Pallas kernels, on_device(): pl.pallas_call(functools.partial(scene_kernel, breadth), out_shape=struct...  1.92 us
    pallas_call x1, Pallas kernels, on_device(): pl.pallas_call(pack_kernel, out_shape=held((places, planes), BF16), in_sp...  1.52 us
  transfers between devices with their start and end apart: 21, of which 12 were waited for; matrix products, arithmetic and copies ran while one was open for 0% of the time, Pallas kernels for 11%

profile of v5, /device:TPU:1, one launch (start us, length us, event | category | flops | bytes accessed | tf_op | source)
XLA Modules:
  0.0 75.4 jit_solution(12193511097678306466)
XLA Ops:
  0.6 1.5 %pack.1.refs_0_ = bf16[64,256]{1,0:T(8,128)(2,1)S(1)} custom-call(bf16[32,256]{1,0:T(8,128)(2,1)} %bitcast.25, bf16[32,64]{1,0:T(8,128)(2,1)} %bitcast.28, s32[32,64]{1,0:T(8,128)} %bitcast.26, s32[32,64]{1,0:T(8,128)} %bitcast.27, s32[1,32]{1,0:T(1,128)} %bitcast.29), custom_call_target="tpu_custom_call" | custom-call | tf_op jit(solution)/shard_map/pack/pallas_call | solution.py:392
  2.2 6.5 %collective-permute-start = (bf16[64,256]{1,0:T(8,128)(2,1)S(1)}, bf16[64,256]{1,0:T(8,128)(2,1)S(1)}, u32[]{:S(2)}, u32[]{:S(2)}) collective-permute-start(bf16[64,256]{1,0:T(8,128)(2,1)S(1)} %pack.1.refs_0_), channel_id=1, source_target_pairs={{0,28},{1,29},{2,30},{3,31},{4,24},{5,25},{6,26},{7,27},{8,20},{9,... | collective-permute-start | bytes 98312 | tf_op jit(solution)/shard_map/ppermute | solution.py:355
  8.7 1.3 %collective-permute-done.refs_1_ = bf16[64,256]{1,0:T(8,128)(2,1)S(1)} collective-permute-done((bf16[64,256]{1,0:T(8,128)(2,1)S(1)}, bf16[64,256]{1,0:T(8,128)(2,1)S(1)}, u32[]{:S(2)}, u32[]{:S(2)}) %collective-permute-start) | collective-permute-done | bytes 32800 | tf_op jit(solution)/shard_map/ppermute | solution.py:355
  10.0 0.2 line.1
  10.1 1.7 %collective-permute-start.1 = (bf16[80,256]{1,0:T(8,128)(2,1)S(1)}, bf16[80,256]{1,0:T(8,128)(2,1)S(1)}, u32[]{:S(2)}, u32[]{:S(2)}) collective-permute-start(bf16[80,256]{1,0:T(8,128)(2,1)S(1)} %get-tuple-element.50), channel_id=1, source_target_pairs={{0,4},{1,5},{2,6},{3,7},{4,0},{5,1},{6,2},{7,3},{8,12},{9,13},{10,... | collective-permute-start | bytes 122888 | tf_op jit(solution)/shard_map/ppermute | solution.py:355
  11.8 0.5 collective-permute-start.2
  12.4 1.6 %collective-permute-start.3 = (bf16[80,256]{1,0:T(8,128)(2,1)S(1)}, bf16[80,256]{1,0:T(8,128)(2,1)S(1)}, u32[]{:S(2)}, u32[]{:S(2)}) collective-permute-start(bf16[80,256]{1,0:T(8,128)(2,1)S(1)} %get-tuple-element.52), channel_id=1, source_target_pairs={{0,12},{1,13},{2,14},{3,15},{4,8},{5,9},{6,10},{7,11},{8,4},{9,5},... | collective-permute-start | bytes 122888 | tf_op jit(solution)/shard_map/ppermute | solution.py:355
  14.0 1.0 %copy-done.2 = bf16[1,2,400,256]{3,2,1,0:T(8,128)(2,1)S(1)} copy-done((bf16[1,2,400,256]{3,2,1,0:T(8,128)(2,1)S(1)}, bf16[1,2,400,256]{3,2,1,0:T(8,128)(2,1)}, u32[]{:S(2)}) %copy-start.2) | copy-done | bytes 409624
  15.0 0.4 moved.1
  15.4 0.4 collective-permute-done.2.refs_2_
  15.9 1.6 %collective-permute-done.3.refs_3_ = bf16[80,256]{1,0:T(8,128)(2,1)S(1)} collective-permute-done((bf16[80,256]{1,0:T(8,128)(2,1)S(1)}, bf16[80,256]{1,0:T(8,128)(2,1)S(1)}, u32[]{:S(2)}, u32[]{:S(2)}) %collective-permute-start.3) | collective-permute-done | bytes 40992 | tf_op jit(solution)/shard_map/ppermute | solution.py:355
  17.5 0.1 strip.1
  17.6 1.4 %collective-permute-start.6 = (bf16[288,256]{1,0:T(8,128)(2,1)S(1)}, bf16[288,256]{1,0:T(8,128)(2,1)S(1)}, u32[]{:S(2)}, u32[]{:S(2)}) collective-permute-start(bf16[288,256]{1,0:T(8,128)(2,1)S(1)} %get-tuple-element.61), channel_id=1, source_target_pairs={{0,1},{1,0},{2,3},{3,2},{4,5},{5,4},{6,7},{7,6},{8,9},{9,8},{10,11... | collective-permute-start | bytes 442376 | tf_op jit(solution)/shard_map/ppermute | solution.py:355
  18.9 2.6 %collective-permute-start.5 = (bf16[288,256]{1,0:T(8,128)(2,1)S(1)}, bf16[288,256]{1,0:T(8,128)(2,1)S(1)}, u32[]{:S(2)}, u32[]{:S(2)}) collective-permute-start(bf16[288,256]{1,0:T(8,128)(2,1)S(1)} %get-tuple-element.60), channel_id=1, source_target_pairs={{0,2},{1,3},{2,0},{3,1},{4,6},{5,7},{6,4},{7,5},{8,10},{9,11},{10,... | collective-permute-start | bytes 442376 | tf_op jit(solution)/shard_map/ppermute | solution.py:355
  21.6 1.1 %plane.1.before = f32[6,400,256]{2,1,0:T(8,128)S(1)} custom-call(bf16[288,256]{1,0:T(8,128)(2,1)S(1)} %get-tuple-element.62.message), custom_call_target="tpu_custom_call" | custom-call | flops 629145600 | bytes 1000000 | tf_op jit(solution)/shard_map/plane/pallas_call | solution.py:453
  22.7 1.1 %more.1.before = f32[6,400,256]{2,1,0:T(8,128)S(1)} custom-call(bf16[288,256]{1,0:T(8,128)(2,1)S(1)} %collective-permute-done.6.message, f32[6,400,256]{2,1,0:T(8,128)S(1)} %plane.1.before), custom_call_target="tpu_custom_call" | custom-call | flops 629145600 | bytes 1000000 | tf_op jit(solution)/shard_map/more/pallas_call | solution.py:463
  23.8 1.9 %collective-permute-done.5.message = bf16[288,256]{1,0:T(8,128)(2,1)S(1)} collective-permute-done((bf16[288,256]{1,0:T(8,128)(2,1)S(1)}, bf16[288,256]{1,0:T(8,128)(2,1)S(1)}, u32[]{:S(2)}, u32[]{:S(2)}) %collective-permute-start.5) | collective-permute-done | bytes 147488 | tf_op jit(solution)/shard_map/ppermute | solution.py:355
  25.7 1.1 %again.1.before = f32[6,400,256]{2,1,0:T(8,128)S(1)} custom-call(bf16[288,256]{1,0:T(8,128)(2,1)S(1)} %collective-permute-done.5.message, f32[6,400,256]{2,1,0:T(8,128)S(1)} %more.1.before), custom_call_target="tpu_custom_call" | custom-call | flops 629145600 | bytes 1000000 | tf_op jit(solution)/shard_map/again/pallas_call | solution.py:473
  26.8 0.0 copy-start
  26.9 0.4 collective-permute-done.4.message
  27.3 1.3 %splat.1.bev = bf16[6,416,256]{2,1,0:T(8,128)(2,1)S(1)} custom-call(bf16[288,256]{1,0:T(8,128)(2,1)S(1)} %collective-permute-done.4.message, f32[6,400,256]{2,1,0:T(8,128)S(1)} %again.1.before), custom_call_target="tpu_custom_call" | custom-call | tf_op jit(solution)/shard_map/splat/pallas_call | solution.py:483
  28.5 3.0 %hidden.1 = (f32[2,416,256]{2,1,0:T(8,128)S(1)}, bf16[4,416,256]{2,1,0:T(8,128)(2,1)S(1)}, bf16[4,256,416]{2,1,0:T(8,128)(2,1)S(1)}, bf16[2304,128]{1,0:T(8,128)(2,1)S(1)}) custom-call(bf16[6,416,256]{2,1,0:T(8,128)(2,1)S(1)} %splat.1.bev, bf16[2304,256]{1,0:T(8,128)(2,1)S(1)} %copy-done, bf16[2,416,384]{2,1,0:T(8,128)(2,1)S(1)} %get-tuple-element.63.cotangent), custom_call_target="tpu_custom_call" | custom-call | tf_op jit(solution)/shard_map/hidden/pallas_call | solution.py:492
  31.6 4.1 %collective-permute-start.7 = (bf16[2304,128]{1,0:T(8,128)(2,1)S(1)}, bf16[2304,128]{1,0:T(8,128)(2,1)S(1)}, u32[]{:S(2)}, u32[]{:S(2)}) collective-permute-start(bf16[2304,128]{1,0:T(8,128)(2,1)S(1)} %get-tuple-element.66), channel_id=1, source_target_pairs={{0,32},{32,0},{64,96},{96,64},{128,160},{160,128},{192,224},{224,1... | collective-permute-start | bytes 1769480 | tf_op jit(solution)/shard_map/ppermute | solution.py:355
  35.7 1.0 %kept.1 = f32[2304,128]{1,0:T(8,128)S(1)} custom-call(bf16[4,256,416]{2,1,0:T(8,128)(2,1)S(1)} %get-tuple-element.64.columns, bf16[2,416,384]{2,1,0:T(8,128)(2,1)S(1)} %get-tuple-element.65.cotangent), custom_call_target="tpu_custom_call" | custom-call | flops 490733568 | bytes 1000000 | tf_op jit(solution)/shard_map/kept/pallas_call | solution.py:506
  36.7 0.6 collective-permute-done.7
  37.4 0.1 parts.1
  37.5 0.1 collective-permute-start.8
  37.6 2.1 %collective-permute-start.9 = (bf16[8,72,128]{2,1,0:T(8,128)(2,1)S(1)}, bf16[8,72,128]{2,1,0:T(8,128)(2,1)S(1)}, u32[]{:S(2)}, u32[]{:S(2)}) collective-permute-start(bf16[8,72,128]{2,1,0:T(8,128)(2,1)S(1)} %get-tuple-element.70), channel_id=1, source_target_pairs={{0,2},{1,3},{2,0},{3,1},{4,6},{5,7},{6,4},{7,5},{8,10},{9,11},{10,... | collective-permute-start | bytes 442376 | tf_op jit(solution)/shard_map/ppermute | solution.py:355
  39.7 1.8 %collective-permute-start.10 = (bf16[8,72,128]{2,1,0:T(8,128)(2,1)S(1)}, bf16[8,72,128]{2,1,0:T(8,128)(2,1)S(1)}, u32[]{:S(2)}, u32[]{:S(2)}) collective-permute-start(bf16[8,72,128]{2,1,0:T(8,128)(2,1)S(1)} %get-tuple-element.71), channel_id=1, source_target_pairs={{0,3},{1,2},{2,1},{3,0},{4,7},{5,6},{6,5},{7,4},{8,11},{9,10},{10,... | collective-permute-start | bytes 442376 | tf_op jit(solution)/shard_map/ppermute | solution.py:355
  41.5 1.9 %scene.1 = bf16[2,400,256]{2,1,0:T(8,128)(2,1)} custom-call(bf16[6,416,256]{2,1,0:T(8,128)(2,1)S(1)} %splat.1.bev, bf16[4,416,256]{2,1,0:T(8,128)(2,1)S(1)} %get-tuple-element.72.hidden, bf16[2304,256]{1,0:T(8,128)(2,1)S(1)} %copy-done.1), custom_call_target="tpu_custom_call" | custom-call | flops 981467136 | bytes 1000000 | tf_op jit(solution)/shard_map/scene/pallas_call | solution.py:527
  43.4 3.1 %collective-permute-done.9.two = bf16[8,72,128]{2,1,0:T(8,128)(2,1)S(1)} collective-permute-done((bf16[8,72,128]{2,1,0:T(8,128)(2,1)S(1)}, bf16[8,72,128]{2,1,0:T(8,128)(2,1)S(1)}, u32[]{:S(2)}, u32[]{:S(2)}) %collective-permute-start.9) | collective-permute-done | bytes 147488 | tf_op jit(solution)/shard_map/ppermute | solution.py:355
  46.5 2.5 %collective-permute-done.10.three = bf16[8,72,128]{2,1,0:T(8,128)(2,1)S(1)} collective-permute-done((bf16[8,72,128]{2,1,0:T(8,128)(2,1)S(1)}, bf16[8,72,128]{2,1,0:T(8,128)(2,1)S(1)}, u32[]{:S(2)}, u32[]{:S(2)}) %collective-permute-start.10) | collective-permute-done | bytes 147488 | tf_op jit(solution)/shard_map/ppermute | solution.py:355
  48.9 0.1 planes.1
  49.0 0.1 collective-permute-start.11
  49.1 1.8 %collective-permute-start.12 = (bf16[2,72,128]{2,1,0:T(8,128)(2,1)S(1)}, bf16[2,72,128]{2,1,0:T(8,128)(2,1)S(1)}, u32[]{:S(2)}, u32[]{:S(2)}) collective-permute-start(bf16[2,72,128]{2,1,0:T(8,128)(2,1)S(1)} %get-tuple-element.80), channel_id=1, source_target_pairs={{0,8},{1,9},{2,10},{3,11},{4,12},{5,13},{6,14},{7,15},{8,0},{9,1},... | collective-permute-start | bytes 110600 | tf_op jit(solution)/shard_map/ppermute | solution.py:355
  50.9 1.7 %collective-permute-start.13 = (bf16[2,72,128]{2,1,0:T(8,128)(2,1)S(1)}, bf16[2,72,128]{2,1,0:T(8,128)(2,1)S(1)}, u32[]{:S(2)}, u32[]{:S(2)}) collective-permute-start(bf16[2,72,128]{2,1,0:T(8,128)(2,1)S(1)} %get-tuple-element.81), channel_id=1, source_target_pairs={{0,12},{1,13},{2,14},{3,15},{4,8},{5,9},{6,10},{7,11},{8,4},{9,5},... | collective-permute-start | bytes 110600 | tf_op jit(solution)/shard_map/ppermute | solution.py:355
  52.7 0.3 collective-permute-done.12
  52.9 2.7 %collective-permute-done.13 = bf16[2,72,128]{2,1,0:T(8,128)(2,1)S(1)} collective-permute-done((bf16[2,72,128]{2,1,0:T(8,128)(2,1)S(1)}, bf16[2,72,128]{2,1,0:T(8,128)(2,1)S(1)}, u32[]{:S(2)}, u32[]{:S(2)}) %collective-permute-start.13) | collective-permute-done | bytes 36896 | tf_op jit(solution)/shard_map/ppermute | solution.py:355
  55.7 4.0 %collective-permute-start.14 = (bf16[72,128]{1,0:T(8,128)(2,1)S(1)}, bf16[72,128]{1,0:T(8,128)(2,1)S(1)}, u32[]{:S(2)}, u32[]{:S(2)}) collective-permute-start(bf16[72,128]{1,0:T(8,128)(2,1)S(1)} %fusion.2), channel_id=1, source_target_pairs={{0,28},{1,29},{2,30},{3,31},{4,24},{5,25},{6,26},{7,27},{8,20},{9,... | collective-permute-start | bytes 55304 | tf_op jit(solution)/shard_map/ppermute | solution.py:355
  59.7 1.7 %collective-permute-start.19 = (bf16[400,256]{1,0:T(8,128)(2,1)S(1)}, bf16[400,256]{1,0:T(8,128)(2,1)S(1)}, u32[]{:S(2)}, u32[]{:S(2)}) collective-permute-start(bf16[400,256]{1,0:T(8,128)(2,1)S(1)} %get-tuple-element.86), channel_id=1, source_target_pairs={{0,31},{1,2},{2,1},{3,4},{4,3},{5,6},{6,5},{7,8},{8,7},{9,10},{10,... | collective-permute-start | bytes 614408 | tf_op jit(solution)/shard_map/ppermute | solution.py:355
  61.4 2.6 %collective-permute-start.17 = (bf16[72,128]{1,0:T(8,128)(2,1)S(1)}, bf16[72,128]{1,0:T(8,128)(2,1)S(1)}, u32[]{:S(2)}, u32[]{:S(2)}) collective-permute-start(bf16[72,128]{1,0:T(8,128)(2,1)S(1)} %fusion.1), channel_id=1, source_target_pairs={{0,192},{32,224},{64,128},{96,160},{128,64},{160,96},{192,0},{224,... | collective-permute-start | bytes 55304 | tf_op jit(solution)/shard_map/ppermute | solution.py:355
  64.0 0.5 collective-permute-start.16
  64.5 0.3 collective-permute-start.15
  64.8 0.6 collective-permute-done.17
  65.3 2.8 %collective-permute-done.16 = bf16[72,128]{1,0:T(8,128)(2,1)S(1)} collective-permute-done((bf16[72,128]{1,0:T(8,128)(2,1)S(1)}, bf16[72,128]{1,0:T(8,128)(2,1)S(1)}, u32[]{:S(2)}, u32[]{:S(2)}) %collective-permute-start.16) | collective-permute-done | bytes 18464 | tf_op jit(solution)/shard_map/ppermute | solution.py:355
  68.2 4.6 %collective-permute-start.20 = (f32[72,128]{1,0:T(8,128)S(1)}, f32[72,128]{1,0:T(8,128)S(1)}, u32[]{:S(2)}, u32[]{:S(2)}) collective-permute-start(f32[72,128]{1,0:T(8,128)S(1)} %convert_add_fusion.1.ours), channel_id=1, source_target_pairs={{0,32},{32,0},{64,96},{96,64},{128,160},{160,128},{192,224},{224,1... | collective-permute-start | bytes 110600 | tf_op jit(solution)/shard_map/ppermute | solution.py:355
  72.7 2.0 %derivative.1 = bf16[2,400,256]{2,1,0:T(8,128)(2,1)} custom-call(bf16[2,400,256]{2,1,0:T(8,128)(2,1)S(1)} %bitcast.23, bf16[400,256]{1,0:T(8,128)(2,1)S(1)} %collective-permute-done.18.first, bf16[400,256]{1,0:T(8,128)(2,1)S(1)} %collective-permute-done.19.second, bf16[2304,256]{1,0:T(8,128)(2,1)S(1)} %copy-done.1, f32[2,416,256]{2,1,0:T(8,128)S(1)} %get-tuple-element.92.pre), custom_call_target="tpu_custom_call" | custom-call | flops 981467136 | bytes 1000000 | tf_op jit(solution)/shard_map/derivative/pallas_call | solution.py:554
  74.8 0.6 gradient.1
  (21 shorter events, 0.1 us)
Async XLA Ops:
  2.2 7.8 %collective-permute-start = (bf16[64,256]{1,0:T(8,128)(2,1)S(1)}, bf16[64,256]{1,0:T(8,128)(2,1)S(1)}, u32[]{:S(2)}, u32[]{:S(2)}) collective-permute-start(bf16[64,256]{1,0:T(8,128)(2,1)S(1)} %pack.1.refs_0_), channel_id=1, source_target_pairs={{0,28},{1,29},{2,30},{3,31},{4,24},{5,25},{6,26},{7,27},{8,20},{9,... | collective-permute-start | bytes 98312 | tf_op jit(solution)/shard_map/ppermute | solution.py:355
  10.1 5.3 %collective-permute-start.1 = (bf16[80,256]{1,0:T(8,128)(2,1)S(1)}, bf16[80,256]{1,0:T(8,128)(2,1)S(1)}, u32[]{:S(2)}, u32[]{:S(2)}) collective-permute-start(bf16[80,256]{1,0:T(8,128)(2,1)S(1)} %get-tuple-element.50), channel_id=1, source_target_pairs={{0,4},{1,5},{2,6},{3,7},{4,0},{5,1},{6,2},{7,3},{8,12},{9,13},{10,... | collective-permute-start | bytes 122888 | tf_op jit(solution)/shard_map/ppermute | solution.py:355
  11.8 4.0 %collective-permute-start.2 = (bf16[80,256]{1,0:T(8,128)(2,1)S(1)}, bf16[80,256]{1,0:T(8,128)(2,1)S(1)}, u32[]{:S(2)}, u32[]{:S(2)}) collective-permute-start(bf16[80,256]{1,0:T(8,128)(2,1)S(1)} %get-tuple-element.51), channel_id=1, source_target_pairs={{0,8},{1,9},{2,10},{3,11},{4,12},{5,13},{6,14},{7,15},{8,0},{9,1},... | collective-permute-start | bytes 122888 | tf_op jit(solution)/shard_map/ppermute | solution.py:355
  12.4 5.1 %collective-permute-start.3 = (bf16[80,256]{1,0:T(8,128)(2,1)S(1)}, bf16[80,256]{1,0:T(8,128)(2,1)S(1)}, u32[]{:S(2)}, u32[]{:S(2)}) collective-permute-start(bf16[80,256]{1,0:T(8,128)(2,1)S(1)} %get-tuple-element.52), channel_id=1, source_target_pairs={{0,12},{1,13},{2,14},{3,15},{4,8},{5,9},{6,10},{7,11},{8,4},{9,5},... | collective-permute-start | bytes 122888 | tf_op jit(solution)/shard_map/ppermute | solution.py:355
  14.0 1.0 %copy-start.2 = (bf16[1,2,400,256]{3,2,1,0:T(8,128)(2,1)S(1)}, bf16[1,2,400,256]{3,2,1,0:T(8,128)(2,1)}, u32[]{:S(2)}) copy-start(bf16[1,2,400,256]{3,2,1,0:T(8,128)(2,1)} %param.13) | copy-start | bytes 1228804
  17.6 5.1 %collective-permute-start.6 = (bf16[288,256]{1,0:T(8,128)(2,1)S(1)}, bf16[288,256]{1,0:T(8,128)(2,1)S(1)}, u32[]{:S(2)}, u32[]{:S(2)}) collective-permute-start(bf16[288,256]{1,0:T(8,128)(2,1)S(1)} %get-tuple-element.61), channel_id=1, source_target_pairs={{0,1},{1,0},{2,3},{3,2},{4,5},{5,4},{6,7},{7,6},{8,9},{9,8},{10,11... | collective-permute-start | bytes 442376 | tf_op jit(solution)/shard_map/ppermute | solution.py:355
  18.9 6.8 %collective-permute-start.5 = (bf16[288,256]{1,0:T(8,128)(2,1)S(1)}, bf16[288,256]{1,0:T(8,128)(2,1)S(1)}, u32[]{:S(2)}, u32[]{:S(2)}) collective-permute-start(bf16[288,256]{1,0:T(8,128)(2,1)S(1)} %get-tuple-element.60), channel_id=1, source_target_pairs={{0,2},{1,3},{2,0},{3,1},{4,6},{5,7},{6,4},{7,5},{8,10},{9,11},{10,... | collective-permute-start | bytes 442376 | tf_op jit(solution)/shard_map/ppermute | solution.py:355
  21.6 5.7 %collective-permute-start.4 = (bf16[288,256]{1,0:T(8,128)(2,1)S(1)}, bf16[288,256]{1,0:T(8,128)(2,1)S(1)}, u32[]{:S(2)}, u32[]{:S(2)}) collective-permute-start(bf16[288,256]{1,0:T(8,128)(2,1)S(1)} %get-tuple-element.59), channel_id=1, source_target_pairs={{0,3},{1,2},{2,1},{3,0},{4,7},{5,6},{6,5},{7,4},{8,11},{9,10},{10,... | collective-permute-start | bytes 442376 | tf_op jit(solution)/shard_map/ppermute | solution.py:355
  26.8 1.7 %copy-start = (bf16[2304,256]{1,0:T(8,128)(2,1)S(1)}, bf16[2304,256]{1,0:T(8,128)(2,1)}, u32[]{:S(2)}) copy-start(bf16[2304,256]{1,0:T(8,128)(2,1)} %weight.3) | copy-start | bytes 3538948
  31.6 5.8 %collective-permute-start.7 = (bf16[2304,128]{1,0:T(8,128)(2,1)S(1)}, bf16[2304,128]{1,0:T(8,128)(2,1)S(1)}, u32[]{:S(2)}, u32[]{:S(2)}) collective-permute-start(bf16[2304,128]{1,0:T(8,128)(2,1)S(1)} %get-tuple-element.66), channel_id=1, source_target_pairs={{0,32},{32,0},{64,96},{96,64},{128,160},{160,128},{192,224},{224,1... | collective-permute-start | bytes 1769480 | tf_op jit(solution)/shard_map/ppermute | solution.py:355
  36.7 4.7 %copy-start.1 = (bf16[2304,256]{1,0:T(8,128)(2,1)S(1)}, bf16[2304,256]{1,0:T(8,128)(2,1)}, u32[]{:S(2)}) copy-start(bf16[2304,256]{1,0:T(8,128)(2,1)} %weight.5) | copy-start | bytes 3538948
  37.5 5.9 %collective-permute-start.8 = (bf16[8,72,128]{2,1,0:T(8,128)(2,1)S(1)}, bf16[8,72,128]{2,1,0:T(8,128)(2,1)S(1)}, u32[]{:S(2)}, u32[]{:S(2)}) collective-permute-start(bf16[8,72,128]{2,1,0:T(8,128)(2,1)S(1)} %get-tuple-element.69), channel_id=1, source_target_pairs={{0,1},{1,0},{2,3},{3,2},{4,5},{5,4},{6,7},{7,6},{8,9},{9,8},{10,11... | collective-permute-start | bytes 442376 | tf_op jit(solution)/shard_map/ppermute | solution.py:355
  37.6 8.9 %collective-permute-start.9 = (bf16[8,72,128]{2,1,0:T(8,128)(2,1)S(1)}, bf16[8,72,128]{2,1,0:T(8,128)(2,1)S(1)}, u32[]{:S(2)}, u32[]{:S(2)}) collective-permute-start(bf16[8,72,128]{2,1,0:T(8,128)(2,1)S(1)} %get-tuple-element.70), channel_id=1, source_target_pairs={{0,2},{1,3},{2,0},{3,1},{4,6},{5,7},{6,4},{7,5},{8,10},{9,11},{10,... | collective-permute-start | bytes 442376 | tf_op jit(solution)/shard_map/ppermute | solution.py:355
  39.7 9.3 %collective-permute-start.10 = (bf16[8,72,128]{2,1,0:T(8,128)(2,1)S(1)}, bf16[8,72,128]{2,1,0:T(8,128)(2,1)S(1)}, u32[]{:S(2)}, u32[]{:S(2)}) collective-permute-start(bf16[8,72,128]{2,1,0:T(8,128)(2,1)S(1)} %get-tuple-element.71), channel_id=1, source_target_pairs={{0,3},{1,2},{2,1},{3,0},{4,7},{5,6},{6,5},{7,4},{8,11},{9,10},{10,... | collective-permute-start | bytes 442376 | tf_op jit(solution)/shard_map/ppermute | solution.py:355
  41.5 31.3 %copy-start.3 = (bf16[1,2,400,256]{3,2,1,0:T(8,128)(2,1)S(1)}, bf16[1,2,400,256]{3,2,1,0:T(8,128)(2,1)}, u32[]{:S(2)}) copy-start(bf16[1,2,400,256]{3,2,1,0:T(8,128)(2,1)} %param.13) | copy-start | bytes 1228804
  49.0 3.6 %collective-permute-start.11 = (bf16[2,72,128]{2,1,0:T(8,128)(2,1)S(1)}, bf16[2,72,128]{2,1,0:T(8,128)(2,1)S(1)}, u32[]{:S(2)}, u32[]{:S(2)}) collective-permute-start(bf16[2,72,128]{2,1,0:T(8,128)(2,1)S(1)} %get-tuple-element.79), channel_id=1, source_target_pairs={{0,4},{1,5},{2,6},{3,7},{4,0},{5,1},{6,2},{7,3},{8,12},{9,13},{10,... | collective-permute-start | bytes 110600 | tf_op jit(solution)/shard_map/ppermute | solution.py:355
  49.1 3.8 %collective-permute-start.12 = (bf16[2,72,128]{2,1,0:T(8,128)(2,1)S(1)}, bf16[2,72,128]{2,1,0:T(8,128)(2,1)S(1)}, u32[]{:S(2)}, u32[]{:S(2)}) collective-permute-start(bf16[2,72,128]{2,1,0:T(8,128)(2,1)S(1)} %get-tuple-element.80), channel_id=1, source_target_pairs={{0,8},{1,9},{2,10},{3,11},{4,12},{5,13},{6,14},{7,15},{8,0},{9,1},... | collective-permute-start | bytes 110600 | tf_op jit(solution)/shard_map/ppermute | solution.py:355
  50.9 4.7 %collective-permute-start.13 = (bf16[2,72,128]{2,1,0:T(8,128)(2,1)S(1)}, bf16[2,72,128]{2,1,0:T(8,128)(2,1)S(1)}, u32[]{:S(2)}, u32[]{:S(2)}) collective-permute-start(bf16[2,72,128]{2,1,0:T(8,128)(2,1)S(1)} %get-tuple-element.81), channel_id=1, source_target_pairs={{0,12},{1,13},{2,14},{3,15},{4,8},{5,9},{6,10},{7,11},{8,4},{9,5},... | collective-permute-start | bytes 110600 | tf_op jit(solution)/shard_map/ppermute | solution.py:355
  55.7 5.7 %collective-permute-start.14 = (bf16[72,128]{1,0:T(8,128)(2,1)S(1)}, bf16[72,128]{1,0:T(8,128)(2,1)S(1)}, u32[]{:S(2)}, u32[]{:S(2)}) collective-permute-start(bf16[72,128]{1,0:T(8,128)(2,1)S(1)} %fusion.2), channel_id=1, source_target_pairs={{0,28},{1,29},{2,30},{3,31},{4,24},{5,25},{6,26},{7,27},{8,20},{9,... | collective-permute-start | bytes 55304 | tf_op jit(solution)/shard_map/ppermute | solution.py:355
  59.7 8.4 %collective-permute-start.18 = (bf16[400,256]{1,0:T(8,128)(2,1)S(1)}, bf16[400,256]{1,0:T(8,128)(2,1)S(1)}, u32[]{:S(2)}, u32[]{:S(2)}) collective-permute-start(bf16[400,256]{1,0:T(8,128)(2,1)S(1)} %get-tuple-element.85), channel_id=1, source_target_pairs={{0,1},{1,0},{2,3},{3,2},{4,5},{5,4},{6,7},{7,6},{8,9},{9,8},{10,11... | collective-permute-start | bytes 614408 | tf_op jit(solution)/shard_map/ppermute | solution.py:355
  59.7 8.4 %collective-permute-start.19 = (bf16[400,256]{1,0:T(8,128)(2,1)S(1)}, bf16[400,256]{1,0:T(8,128)(2,1)S(1)}, u32[]{:S(2)}, u32[]{:S(2)}) collective-permute-start(bf16[400,256]{1,0:T(8,128)(2,1)S(1)} %get-tuple-element.86), channel_id=1, source_target_pairs={{0,31},{1,2},{2,1},{3,4},{4,3},{5,6},{6,5},{7,8},{8,7},{9,10},{10,... | collective-permute-start | bytes 614408 | tf_op jit(solution)/shard_map/ppermute | solution.py:355
  61.4 3.9 %collective-permute-start.17 = (bf16[72,128]{1,0:T(8,128)(2,1)S(1)}, bf16[72,128]{1,0:T(8,128)(2,1)S(1)}, u32[]{:S(2)}, u32[]{:S(2)}) collective-permute-start(bf16[72,128]{1,0:T(8,128)(2,1)S(1)} %fusion.1), channel_id=1, source_target_pairs={{0,192},{32,224},{64,128},{96,160},{128,64},{160,96},{192,0},{224,... | collective-permute-start | bytes 55304 | tf_op jit(solution)/shard_map/ppermute | solution.py:355
  64.0 4.1 %collective-permute-start.16 = (bf16[72,128]{1,0:T(8,128)(2,1)S(1)}, bf16[72,128]{1,0:T(8,128)(2,1)S(1)}, u32[]{:S(2)}, u32[]{:S(2)}) collective-permute-start(bf16[72,128]{1,0:T(8,128)(2,1)S(1)} %fusion.1), channel_id=1, source_target_pairs={{0,128},{32,160},{64,192},{96,224},{128,0},{160,32},{192,64},{224,... | collective-permute-start | bytes 55304 | tf_op jit(solution)/shard_map/ppermute | solution.py:355
  64.5 3.6 %collective-permute-start.15 = (bf16[72,128]{1,0:T(8,128)(2,1)S(1)}, bf16[72,128]{1,0:T(8,128)(2,1)S(1)}, u32[]{:S(2)}, u32[]{:S(2)}) collective-permute-start(bf16[72,128]{1,0:T(8,128)(2,1)S(1)} %fusion.1), channel_id=1, source_target_pairs={{0,64},{32,96},{64,0},{96,32},{128,192},{160,224},{192,128},{224,1... | collective-permute-start | bytes 55304 | tf_op jit(solution)/shard_map/ppermute | solution.py:355
  68.2 6.6 %collective-permute-start.20 = (f32[72,128]{1,0:T(8,128)S(1)}, f32[72,128]{1,0:T(8,128)S(1)}, u32[]{:S(2)}, u32[]{:S(2)}) collective-permute-start(f32[72,128]{1,0:T(8,128)S(1)} %convert_add_fusion.1.ours), channel_id=1, source_target_pairs={{0,32},{32,0},{64,96},{96,64},{128,160},{160,128},{192,224},{224,1... | collective-permute-start | bytes 110600 | tf_op jit(solution)/shard_map/ppermute | solution.py:355

commit v6 on v5

--- a/solution.py
+++ b/solution.py
@@ -289,42 +289,59 @@
         scene[y] = (bev[y + 2, :breadth].astype(F32) + value[:breadth]).astype(BF16)
 
 
-def derivative_kernel(breadth, own, first, second, weight, pre, derivative, field):
+def flipped_taps(weight, planes, rows):
+    return jnp.concatenate(
+        [
+            jnp.concatenate(
+                [weight[(a * 3 + b) * planes : (a * 3 + b + 1) * planes] for a in rows], axis=1
+            )
+            for b in (2, 1, 0)
+        ],
+        axis=0,
+    )
+
+
+def back_products(stacked, flipped):
+    return lax.dot_general(
+        stacked, flipped, (((1,), (1,)), ((), ())), preferred_element_type=F32
+    )
+
+
+def joined(product, planes):
+    return (
+        product[:, planes : 2 * planes]
+        + turned(product[:, :planes], 1)
+        + turned(product[:, 2 * planes :], -1)
+    )
+
+
+def inner_kernel(breadth, own, weight, back, field):
+    wide, planes = back.shape[1:]
+    for k in range(2):
+        field[k, :breadth] = own[k]
+        field[k, breadth:] = jnp.zeros((wide - breadth, planes), BF16)
+    stacked = jnp.concatenate([field[0], field[1]], axis=1)
+    back[0] = joined(back_products(stacked, flipped_taps(weight, planes, (1, 0))), planes)
+    back[1] = joined(back_products(stacked, flipped_taps(weight, planes, (2, 1))), planes)
+
+
+def derivative_kernel(breadth, first, second, back, weight, pre, derivative, field):
     wide, planes = pre.shape[1:]
     strip = lax.axis_index("tile")
     odd = strip % 2 == 1
-    blank = jnp.zeros((wide - breadth, planes), BF16)
     zero = jnp.zeros((breadth, planes), BF16)
     above = jnp.where(odd, first[...], jnp.where(strip == 0, zero, second[...]))
     below = jnp.where(
         odd, jnp.where(strip == lax.axis_size("tile") - 1, zero, second[...]), first[...]
     )
-    for k, row in enumerate((above, own[0], own[1], below)):
-        field[k, :breadth] = row
-        field[k, breadth:] = blank
-    flipped = jnp.concatenate(
-        [
-            jnp.concatenate(
-                [weight[(a * 3 + b) * planes : (a * 3 + b + 1) * planes] for a in (2, 1, 0)], axis=1
-            )
-            for b in (2, 1, 0)
-        ],
-        axis=0,
-    )
-    for y in range(2):
-        stacked = jnp.concatenate([field[y], field[y + 1], field[y + 2]], axis=1)
-        product = lax.dot_general(
-            stacked, flipped, (((1,), (1,)), ((), ())), preferred_element_type=F32
-        )
-        back = (
-            product[:, planes : 2 * planes]
-            + turned(product[:, :planes], 1)
-            + turned(product[:, 2 * planes :], -1)
-        )
+    for y, (row, a) in enumerate(((above, 2), (below, 0))):
+        field[y, :breadth] = row
+        field[y, breadth:] = jnp.zeros((wide - breadth, planes), BF16)
+        rest = joined(back_products(field[y], flipped_taps(weight, planes, (a,))), planes)
         value = pre[y, :breadth]
         sigma = jax.nn.sigmoid(value)
         slope = sigma * (1.0 + value * (1.0 - sigma))
-        derivative[y] = (back[:breadth] * slope).astype(BF16)
+        derivative[y] = ((back[y, :breadth] + rest[:breadth]) * slope).astype(BF16)
 
 
 def parts_kernel(kept, taken, *parts):
@@ -419,7 +436,7 @@
         compiler_params=params(4),
         name="line",
     )(packed, swap(packed, "tile", mirror))
-    line = [line[0]] + [swap(line[k], "tile", line_swap(4 * k)) for k in (1, 2, 3)]
+    line = [line[0]] + [swap(line[k], "tile", line_swap(4 * k)) for k in (3, 2, 1)]
     own = predicted_adjoint[0]
     keep, give, near, far = pl.pallas_call(
         functools.partial(moved_kernel, breadth),
@@ -440,7 +457,7 @@
         compiler_params=params(4),
         name="strip",
     )(*line)
-    arrived = [swap(messages[k], "tile", line_swap(k)) for k in (1, 2, 3)]
+    arrived = [swap(messages[k], "tile", line_swap(k)) for k in (3, 2, 1)]
 
     def splat_scratch(count):
         total = count * 8 * slots
@@ -523,7 +540,7 @@
         compiler_params=params(2),
         name="parts",
     )(kept.reshape(strips, share, half), taken.reshape(strips, share, half))
-    fetched = [swap(parts[k], "tile", line_swap(k)) for k in (1, 2, 3)]
+    fetched = [swap(parts[k], "tile", line_swap(k)) for k in (3, 2, 1)]
     scene = pl.pallas_call(
         functools.partial(scene_kernel, breadth),
         out_shape=struct((2, breadth, planes), BF16),
@@ -533,7 +550,17 @@
         cost_estimate=pl.CostEstimate(flops=2 * 2 * wide * taps * planes, bytes_accessed=10**6, transcendentals=0),
         name="scene",
     )(bev, hidden, predictor_filter)
-    fetched, scene = lax.optimization_barrier((fetched, scene))
+    back = pl.pallas_call(
+        functools.partial(inner_kernel, breadth),
+        out_shape=held((2, wide, planes), F32),
+        in_specs=[vmem()] * 2,
+        out_specs=vmem(),
+        scratch_shapes=[pltpu.VMEM((2, wide, planes), BF16)],
+        compiler_params=params(8),
+        cost_estimate=pl.CostEstimate(flops=4 * wide * taps * planes // 3 * 2, bytes_accessed=10**6, transcendentals=0),
+        name="inner",
+    )(own, predictor_filter)
+    fetched, scene, back = lax.optimization_barrier((fetched, scene, back))
     pairs = pl.pallas_call(
         planes_kernel,
         out_shape=tuple(held((2, share, half), F32 if k == 0 else BF16) for k in range(4)),
@@ -542,25 +569,25 @@
         compiler_params=params(2),
         name="planes",
     )(parts[0], *fetched)
-    fetched = [swap(pairs[k], "tile", line_swap(4 * k)) for k in (1, 2, 3)]
+    fetched = [swap(pairs[k], "tile", line_swap(4 * k)) for k in (3, 2, 1)]
     pair = added(pairs[0], *fetched)
     ours = pair[0]
     theirs, near, far = lax.optimization_barrier((pair[1].astype(BF16), near, far))
     first = swap(near, "tile", line_swap(1))
     second = swap(far, "tile", lambda i: (i - 1 + 2 * (i % 2)) % strips)
     ours = added(ours, swap(theirs, "tile", mirror))
-    fetched = [swap(ours.astype(BF16), "dp", line_swap(2 * k)) for k in (1, 2, 3)]
+    fetched = [swap(ours.astype(BF16), "dp", line_swap(2 * k)) for k in (3, 2, 1)]
     fetched, first, second = lax.optimization_barrier((fetched, first, second))
     derivative = pl.pallas_call(
         functools.partial(derivative_kernel, breadth),
         out_shape=struct((2, breadth, planes), BF16),
         in_specs=[vmem()] * 5,
         out_specs=vmem(),
-        scratch_shapes=[pltpu.VMEM((4, wide, planes), BF16)],
-        compiler_params=params(8),
-        cost_estimate=pl.CostEstimate(flops=2 * 2 * wide * taps * planes, bytes_accessed=10**6, transcendentals=10**6),
+        scratch_shapes=[pltpu.VMEM((2, wide, planes), BF16)],
+        compiler_params=params(8),
+        cost_estimate=pl.CostEstimate(flops=4 * wide * taps * planes // 3, bytes_accessed=10**6, transcendentals=10**6),
         name="derivative",
-    )(own, first, second, predictor_filter, pre)
+    )(first, second, back, predictor_filter, pre)
     ours = added(ours, *fetched)
     other, derivative = lax.optimization_barrier((swap(ours, "dp", line_swap(1)), derivative))
     square_tally = lax.axis_size("dp") * height * strips * breadth

time: 75.7 us -> 73.1 us (0.966)
  waiting for transfers between devices: 18.2 us -> 15.7 us
    ppermute x21, waiting for transfers between devices: 18.2 us -> 15.7 us  [swap(): lax.ppermute(values, axis, [(i, partner(i)) for i in range(lax.axis_size(...]
    pallas_call x0 -> x1, Pallas kernels: none -> 0.86 us  [on_device(): pl.pallas_call(functools.partial(inner_kernel, breadth), out_shape=held((...]
  transfers between devices with their start and end apart: 21 -> 21, of which waited for: 12 -> 13; matrix products, arithmetic and copies ran while one was open for 0% -> 0% of each run, Pallas kernels for 11% -> 12%
where the time goes in v6:
time: 73.1 us; the launch traced here: 72.9 us
  starting transfers between devices  39.5 us (54%)
  Pallas kernels  15.8 us (22%)
  waiting for transfers between devices  15.7 us (21%)
  local copies, waits for them, and re-layouts  1.02 us (1%)
  between operations  0.8 us (1%)
    ppermute x21, starting transfers between devices, swap(): lax.ppermute(values, axis, [(i, partner(i)) for i in range(lax.axis_size(...  39.5 us
    ppermute x21, waiting for transfers between devices, swap(): lax.ppermute(values, axis, [(i, partner(i)) for i in range(lax.axis_size(...  15.7 us
    pallas_call x1, Pallas kernels, on_device(): pl.pallas_call(functools.partial(hidden_kernel, breadth), out_shape=(held...  3.05 us
    pallas_call x2, Pallas kernels, on_device(): pl.pallas_call(more_kernel, out_shape=held((6, breadth, planes), F32), in...  2.21 us
    pallas_call x1, Pallas kernels, on_device(): pl.pallas_call(functools.partial(scene_kernel, breadth), out_shape=struct...  1.92 us
    pallas_call x1, Pallas kernels, on_device(): pl.pallas_call(pack_kernel, out_shape=held((places, planes), BF16), in_sp...  1.52 us
  transfers between devices with their start and end apart: 21, of which 13 were waited for; matrix products, arithmetic and copies ran while one was open for 0% of the time, Pallas kernels for 12%

profile of v6, /device:TPU:1, one launch (start us, length us, event | category | flops | bytes accessed | tf_op | source)
XLA Modules:
  0.0 72.9 jit_solution(12130483723728288624)
XLA Ops:
  0.6 1.5 %pack.1.refs_0_ = bf16[64,256]{1,0:T(8,128)(2,1)S(1)} custom-call(bf16[32,256]{1,0:T(8,128)(2,1)} %bitcast.26, bf16[32,64]{1,0:T(8,128)(2,1)} %bitcast.29, s32[32,64]{1,0:T(8,128)} %bitcast.27, s32[32,64]{1,0:T(8,128)} %bitcast.28, s32[1,32]{1,0:T(1,128)} %bitcast.30), custom_call_target="tpu_custom_call" | custom-call | tf_op jit(solution)/shard_map/pack/pallas_call | solution.py:409
  2.2 6.5 %collective-permute-start = (bf16[64,256]{1,0:T(8,128)(2,1)S(1)}, bf16[64,256]{1,0:T(8,128)(2,1)S(1)}, u32[]{:S(2)}, u32[]{:S(2)}) collective-permute-start(bf16[64,256]{1,0:T(8,128)(2,1)S(1)} %pack.1.refs_0_), channel_id=1, source_target_pairs={{0,28},{1,29},{2,30},{3,31},{4,24},{5,25},{6,26},{7,27},{8,20},{9,... | collective-permute-start | bytes 98312 | tf_op jit(solution)/shard_map/ppermute | solution.py:372
  8.7 1.3 %collective-permute-done.refs_1_ = bf16[64,256]{1,0:T(8,128)(2,1)S(1)} collective-permute-done((bf16[64,256]{1,0:T(8,128)(2,1)S(1)}, bf16[64,256]{1,0:T(8,128)(2,1)S(1)}, u32[]{:S(2)}, u32[]{:S(2)}) %collective-permute-start) | collective-permute-done | bytes 32800 | tf_op jit(solution)/shard_map/ppermute | solution.py:372
  10.0 0.2 line.1
  10.1 1.7 %collective-permute-start.1 = (bf16[80,256]{1,0:T(8,128)(2,1)S(1)}, bf16[80,256]{1,0:T(8,128)(2,1)S(1)}, u32[]{:S(2)}, u32[]{:S(2)}) collective-permute-start(bf16[80,256]{1,0:T(8,128)(2,1)S(1)} %get-tuple-element.51), channel_id=1, source_target_pairs={{0,12},{1,13},{2,14},{3,15},{4,8},{5,9},{6,10},{7,11},{8,4},{9,5},... | collective-permute-start | bytes 122888 | tf_op jit(solution)/shard_map/ppermute | solution.py:372
  11.8 1.2 %collective-permute-start.2 = (bf16[80,256]{1,0:T(8,128)(2,1)S(1)}, bf16[80,256]{1,0:T(8,128)(2,1)S(1)}, u32[]{:S(2)}, u32[]{:S(2)}) collective-permute-start(bf16[80,256]{1,0:T(8,128)(2,1)S(1)} %get-tuple-element.52), channel_id=1, source_target_pairs={{0,8},{1,9},{2,10},{3,11},{4,12},{5,13},{6,14},{7,15},{8,0},{9,1},... | collective-permute-start | bytes 122888 | tf_op jit(solution)/shard_map/ppermute | solution.py:372
  13.0 0.7 %collective-permute-start.3 = (bf16[80,256]{1,0:T(8,128)(2,1)S(1)}, bf16[80,256]{1,0:T(8,128)(2,1)S(1)}, u32[]{:S(2)}, u32[]{:S(2)}) collective-permute-start(bf16[80,256]{1,0:T(8,128)(2,1)S(1)} %get-tuple-element.53), channel_id=1, source_target_pairs={{0,4},{1,5},{2,6},{3,7},{4,0},{5,1},{6,2},{7,3},{8,12},{9,13},{10,... | collective-permute-start | bytes 122888 | tf_op jit(solution)/shard_map/ppermute | solution.py:372
  13.8 1.0 %copy-done.1 = bf16[1,2,400,256]{3,2,1,0:T(8,128)(2,1)S(1)} copy-done((bf16[1,2,400,256]{3,2,1,0:T(8,128)(2,1)S(1)}, bf16[1,2,400,256]{3,2,1,0:T(8,128)(2,1)}, u32[]{:S(2)}) %copy-start.1) | copy-done | bytes 409624
  14.8 0.4 moved.1
  15.2 0.4 collective-permute-done.2.refs_2_
  15.6 0.4 collective-permute-done.3.refs_3_
  16.1 2.8 %collective-permute-start.6 = (bf16[288,256]{1,0:T(8,128)(2,1)S(1)}, bf16[288,256]{1,0:T(8,128)(2,1)S(1)}, u32[]{:S(2)}, u32[]{:S(2)}) collective-permute-start(bf16[288,256]{1,0:T(8,128)(2,1)S(1)} %get-tuple-element.62), channel_id=1, source_target_pairs={{0,3},{1,2},{2,1},{3,0},{4,7},{5,6},{6,5},{7,4},{8,11},{9,10},{10,... | collective-permute-start | bytes 442376 | tf_op jit(solution)/shard_map/ppermute | solution.py:372
  18.9 0.3 collective-permute-start.5
  19.3 0.3 collective-permute-start.4
  19.6 1.1 %plane.1.before = f32[6,400,256]{2,1,0:T(8,128)S(1)} custom-call(bf16[288,256]{1,0:T(8,128)(2,1)S(1)} %get-tuple-element.63.message), custom_call_target="tpu_custom_call" | custom-call | flops 629145600 | bytes 1000000 | tf_op jit(solution)/shard_map/plane/pallas_call | solution.py:470
  20.7 1.9 %collective-permute-done.6.message = bf16[288,256]{1,0:T(8,128)(2,1)S(1)} collective-permute-done((bf16[288,256]{1,0:T(8,128)(2,1)S(1)}, bf16[288,256]{1,0:T(8,128)(2,1)S(1)}, u32[]{:S(2)}, u32[]{:S(2)}) %collective-permute-start.6) | collective-permute-done | bytes 147488 | tf_op jit(solution)/shard_map/ppermute | solution.py:372
  22.6 1.1 %more.1.before = f32[6,400,256]{2,1,0:T(8,128)S(1)} custom-call(bf16[288,256]{1,0:T(8,128)(2,1)S(1)} %collective-permute-done.6.message, f32[6,400,256]{2,1,0:T(8,128)S(1)} %plane.1.before), custom_call_target="tpu_custom_call" | custom-call | flops 629145600 | bytes 1000000 | tf_op jit(solution)/shard_map/more/pallas_call | solution.py:480
  23.7 0.8 %collective-permute-done.5.message = bf16[288,256]{1,0:T(8,128)(2,1)S(1)} collective-permute-done((bf16[288,256]{1,0:T(8,128)(2,1)S(1)}, bf16[288,256]{1,0:T(8,128)(2,1)S(1)}, u32[]{:S(2)}, u32[]{:S(2)}) %collective-permute-start.5) | collective-permute-done | bytes 147488 | tf_op jit(solution)/shard_map/ppermute | solution.py:372
  24.5 1.1 %again.1.before = f32[6,400,256]{2,1,0:T(8,128)S(1)} custom-call(bf16[288,256]{1,0:T(8,128)(2,1)S(1)} %collective-permute-done.5.message, f32[6,400,256]{2,1,0:T(8,128)S(1)} %more.1.before), custom_call_target="tpu_custom_call" | custom-call | flops 629145600 | bytes 1000000 | tf_op jit(solution)/shard_map/again/pallas_call | solution.py:490
  25.7 1.3 %splat.1.bev = bf16[6,416,256]{2,1,0:T(8,128)(2,1)S(1)} custom-call(bf16[288,256]{1,0:T(8,128)(2,1)S(1)} %collective-permute-done.4.message, f32[6,400,256]{2,1,0:T(8,128)S(1)} %again.1.before), custom_call_target="tpu_custom_call" | custom-call | tf_op jit(solution)/shard_map/splat/pallas_call | solution.py:500
  27.0 3.0 %hidden.1 = (f32[2,416,256]{2,1,0:T(8,128)S(1)}, bf16[4,416,256]{2,1,0:T(8,128)(2,1)S(1)}, bf16[4,256,416]{2,1,0:T(8,128)(2,1)S(1)}, bf16[2304,128]{1,0:T(8,128)(2,1)S(1)}) custom-call(bf16[6,416,256]{2,1,0:T(8,128)(2,1)S(1)} %splat.1.bev, bf16[2304,256]{1,0:T(8,128)(2,1)S(1)} %copy-done.3, bf16[2,416,384]{2,1,0:T(8,128)(2,1)S(1)} %get-tuple-element.64.cotangent), custom_call_target="tpu_custom_call" | custom-call | tf_op jit(solution)/shard_map/hidden/pallas_call | solution.py:509
  30.0 4.7 %collective-permute-start.7 = (bf16[2304,128]{1,0:T(8,128)(2,1)S(1)}, bf16[2304,128]{1,0:T(8,128)(2,1)S(1)}, u32[]{:S(2)}, u32[]{:S(2)}) collective-permute-start(bf16[2304,128]{1,0:T(8,128)(2,1)S(1)} %get-tuple-element.67), channel_id=1, source_target_pairs={{0,32},{32,0},{64,96},{96,64},{128,160},{160,128},{192,224},{224,1... | collective-permute-start | bytes 1769480 | tf_op jit(solution)/shard_map/ppermute | solution.py:372
  34.7 1.0 %kept.1 = f32[2304,128]{1,0:T(8,128)S(1)} custom-call(bf16[4,256,416]{2,1,0:T(8,128)(2,1)S(1)} %get-tuple-element.65.columns, bf16[2,416,384]{2,1,0:T(8,128)(2,1)S(1)} %get-tuple-element.66.cotangent), custom_call_target="tpu_custom_call" | custom-call | flops 490733568 | bytes 1000000 | tf_op jit(solution)/shard_map/kept/pallas_call | solution.py:523
  35.7 0.6 collective-permute-done.7
  36.3 0.1 parts.1
  36.5 2.2 %collective-permute-start.8 = (bf16[8,72,128]{2,1,0:T(8,128)(2,1)S(1)}, bf16[8,72,128]{2,1,0:T(8,128)(2,1)S(1)}, u32[]{:S(2)}, u32[]{:S(2)}) collective-permute-start(bf16[8,72,128]{2,1,0:T(8,128)(2,1)S(1)} %get-tuple-element.70), channel_id=1, source_target_pairs={{0,3},{1,2},{2,1},{3,0},{4,7},{5,6},{6,5},{7,4},{8,11},{9,10},{10,... | collective-permute-start | bytes 442376 | tf_op jit(solution)/shard_map/ppermute | solution.py:372
  38.7 1.1 %collective-permute-start.10 = (bf16[8,72,128]{2,1,0:T(8,128)(2,1)S(1)}, bf16[8,72,128]{2,1,0:T(8,128)(2,1)S(1)}, u32[]{:S(2)}, u32[]{:S(2)}) collective-permute-start(bf16[8,72,128]{2,1,0:T(8,128)(2,1)S(1)} %get-tuple-element.72), channel_id=1, source_target_pairs={{0,1},{1,0},{2,3},{3,2},{4,5},{5,4},{6,7},{7,6},{8,9},{9,8},{10,11... | collective-permute-start | bytes 442376 | tf_op jit(solution)/shard_map/ppermute | solution.py:372
  39.8 0.9 %inner.1.back = f32[2,416,256]{2,1,0:T(8,128)S(1)} custom-call(bf16[2,400,256]{2,1,0:T(8,128)(2,1)S(1)} %bitcast.22, bf16[2304,256]{1,0:T(8,128)(2,1)S(1)} %copy-done), custom_call_target="tpu_custom_call" | custom-call | flops 654311424 | bytes 1000000 | tf_op jit(solution)/shard_map/inner/pallas_call | solution.py:553
  40.7 1.9 %scene.1 = bf16[2,400,256]{2,1,0:T(8,128)(2,1)} custom-call(bf16[6,416,256]{2,1,0:T(8,128)(2,1)S(1)} %splat.1.bev, bf16[4,416,256]{2,1,0:T(8,128)(2,1)S(1)} %get-tuple-element.73.hidden, bf16[2304,256]{1,0:T(8,128)(2,1)S(1)} %copy-done), custom_call_target="tpu_custom_call" | custom-call | flops 981467136 | bytes 1000000 | tf_op jit(solution)/shard_map/scene/pallas_call | solution.py:544
  42.6 2.0 %collective-permute-done.8.one = bf16[8,72,128]{2,1,0:T(8,128)(2,1)S(1)} collective-permute-done((bf16[8,72,128]{2,1,0:T(8,128)(2,1)S(1)}, bf16[8,72,128]{2,1,0:T(8,128)(2,1)S(1)}, u32[]{:S(2)}, u32[]{:S(2)}) %collective-permute-start.8) | collective-permute-done | bytes 147488 | tf_op jit(solution)/shard_map/ppermute | solution.py:372
  44.6 0.4 collective-permute-done.9.two
  45.0 1.3 %collective-permute-done.10.three = bf16[8,72,128]{2,1,0:T(8,128)(2,1)S(1)} collective-permute-done((bf16[8,72,128]{2,1,0:T(8,128)(2,1)S(1)}, bf16[8,72,128]{2,1,0:T(8,128)(2,1)S(1)}, u32[]{:S(2)}, u32[]{:S(2)}) %collective-permute-start.10) | collective-permute-done | bytes 147488 | tf_op jit(solution)/shard_map/ppermute | solution.py:372
  46.4 0.8 %collective-permute-start.13 = (bf16[2,72,128]{2,1,0:T(8,128)(2,1)S(1)}, bf16[2,72,128]{2,1,0:T(8,128)(2,1)S(1)}, u32[]{:S(2)}, u32[]{:S(2)}) collective-permute-start(bf16[2,72,128]{2,1,0:T(8,128)(2,1)S(1)} %get-tuple-element.82), channel_id=1, source_target_pairs={{0,4},{1,5},{2,6},{3,7},{4,0},{5,1},{6,2},{7,3},{8,12},{9,13},{10,... | collective-permute-start | bytes 110600 | tf_op jit(solution)/shard_map/ppermute | solution.py:372
  47.3 1.3 %collective-permute-start.12 = (bf16[2,72,128]{2,1,0:T(8,128)(2,1)S(1)}, bf16[2,72,128]{2,1,0:T(8,128)(2,1)S(1)}, u32[]{:S(2)}, u32[]{:S(2)}) collective-permute-start(bf16[2,72,128]{2,1,0:T(8,128)(2,1)S(1)} %get-tuple-element.81), channel_id=1, source_target_pairs={{0,8},{1,9},{2,10},{3,11},{4,12},{5,13},{6,14},{7,15},{8,0},{9,1},... | collective-permute-start | bytes 110600 | tf_op jit(solution)/shard_map/ppermute | solution.py:372
  48.5 1.5 %collective-permute-start.11 = (bf16[2,72,128]{2,1,0:T(8,128)(2,1)S(1)}, bf16[2,72,128]{2,1,0:T(8,128)(2,1)S(1)}, u32[]{:S(2)}, u32[]{:S(2)}) collective-permute-start(bf16[2,72,128]{2,1,0:T(8,128)(2,1)S(1)} %get-tuple-element.80), channel_id=1, source_target_pairs={{0,12},{1,13},{2,14},{3,15},{4,8},{5,9},{6,10},{7,11},{8,4},{9,5},... | collective-permute-start | bytes 110600 | tf_op jit(solution)/shard_map/ppermute | solution.py:372
  50.1 0.9 %collective-permute-done.12 = bf16[2,72,128]{2,1,0:T(8,128)(2,1)S(1)} collective-permute-done((bf16[2,72,128]{2,1,0:T(8,128)(2,1)S(1)}, bf16[2,72,128]{2,1,0:T(8,128)(2,1)S(1)}, u32[]{:S(2)}, u32[]{:S(2)}) %collective-permute-start.12) | collective-permute-done | bytes 36896 | tf_op jit(solution)/shard_map/ppermute | solution.py:372
  51.0 2.2 %collective-permute-done.11 = bf16[2,72,128]{2,1,0:T(8,128)(2,1)S(1)} collective-permute-done((bf16[2,72,128]{2,1,0:T(8,128)(2,1)S(1)}, bf16[2,72,128]{2,1,0:T(8,128)(2,1)S(1)}, u32[]{:S(2)}, u32[]{:S(2)}) %collective-permute-start.11) | collective-permute-done | bytes 36896 | tf_op jit(solution)/shard_map/ppermute | solution.py:372
  53.2 3.8 %collective-permute-start.14 = (bf16[72,128]{1,0:T(8,128)(2,1)S(1)}, bf16[72,128]{1,0:T(8,128)(2,1)S(1)}, u32[]{:S(2)}, u32[]{:S(2)}) collective-permute-start(bf16[72,128]{1,0:T(8,128)(2,1)S(1)} %fusion.2), channel_id=1, source_target_pairs={{0,28},{1,29},{2,30},{3,31},{4,24},{5,25},{6,26},{7,27},{8,20},{9,... | collective-permute-start | bytes 55304 | tf_op jit(solution)/shard_map/ppermute | solution.py:372
  57.0 0.7 collective-permute-start.18
  57.7 1.4 %collective-permute-start.19 = (bf16[400,256]{1,0:T(8,128)(2,1)S(1)}, bf16[400,256]{1,0:T(8,128)(2,1)S(1)}, u32[]{:S(2)}, u32[]{:S(2)}) collective-permute-start(bf16[400,256]{1,0:T(8,128)(2,1)S(1)} %get-tuple-element.87), channel_id=1, source_target_pairs={{0,31},{1,2},{2,1},{3,4},{4,3},{5,6},{6,5},{7,8},{8,7},{9,10},{10,... | collective-permute-start | bytes 614408 | tf_op jit(solution)/shard_map/ppermute | solution.py:372
  59.2 2.6 %collective-permute-start.15 = (bf16[72,128]{1,0:T(8,128)(2,1)S(1)}, bf16[72,128]{1,0:T(8,128)(2,1)S(1)}, u32[]{:S(2)}, u32[]{:S(2)}) collective-permute-start(bf16[72,128]{1,0:T(8,128)(2,1)S(1)} %fusion.1), channel_id=1, source_target_pairs={{0,192},{32,224},{64,128},{96,160},{128,64},{160,96},{192,0},{224,... | collective-permute-start | bytes 55304 | tf_op jit(solution)/shard_map/ppermute | solution.py:372
  61.7 0.5 collective-permute-start.16
  62.3 0.2 collective-permute-start.17
  62.5 0.6 collective-permute-done.15
  63.1 2.8 %collective-permute-done.16 = bf16[72,128]{1,0:T(8,128)(2,1)S(1)} collective-permute-done((bf16[72,128]{1,0:T(8,128)(2,1)S(1)}, bf16[72,128]{1,0:T(8,128)(2,1)S(1)}, u32[]{:S(2)}, u32[]{:S(2)}) %collective-permute-start.16) | collective-permute-done | bytes 18464 | tf_op jit(solution)/shard_map/ppermute | solution.py:372
  65.9 4.9 %collective-permute-start.20 = (f32[72,128]{1,0:T(8,128)S(1)}, f32[72,128]{1,0:T(8,128)S(1)}, u32[]{:S(2)}, u32[]{:S(2)}) collective-permute-start(f32[72,128]{1,0:T(8,128)S(1)} %convert_add_fusion.1.ours), channel_id=1, source_target_pairs={{0,32},{32,0},{64,96},{96,64},{128,160},{160,128},{192,224},{224,1... | collective-permute-start | bytes 110600 | tf_op jit(solution)/shard_map/ppermute | solution.py:372
  70.8 1.4 %derivative.1 = bf16[2,400,256]{2,1,0:T(8,128)(2,1)} custom-call(bf16[400,256]{1,0:T(8,128)(2,1)S(1)} %collective-permute-done.18.first, bf16[400,256]{1,0:T(8,128)(2,1)S(1)} %collective-permute-done.19.second, f32[2,416,256]{2,1,0:T(8,128)S(1)} %inner.1.back, bf16[2304,256]{1,0:T(8,128)(2,1)S(1)} %copy-done, f32[2,416,256]{2,1,0:T(8,128)S(1)} %get-tuple-element.94.pre), custom_call_target="tpu_custom_call" | custom-call | flops 327155712 | bytes 1000000 | tf_op jit(solution)/shard_map/derivative/pallas_call | solution.py:581
  72.2 0.6 gradient.1
  (22 shorter events, 0.3 us)
Async XLA Ops:
  2.2 7.8 %collective-permute-start = (bf16[64,256]{1,0:T(8,128)(2,1)S(1)}, bf16[64,256]{1,0:T(8,128)(2,1)S(1)}, u32[]{:S(2)}, u32[]{:S(2)}) collective-permute-start(bf16[64,256]{1,0:T(8,128)(2,1)S(1)} %pack.1.refs_0_), channel_id=1, source_target_pairs={{0,28},{1,29},{2,30},{3,31},{4,24},{5,25},{6,26},{7,27},{8,20},{9,... | collective-permute-start | bytes 98312 | tf_op jit(solution)/shard_map/ppermute | solution.py:372
  10.1 5.0 %collective-permute-start.1 = (bf16[80,256]{1,0:T(8,128)(2,1)S(1)}, bf16[80,256]{1,0:T(8,128)(2,1)S(1)}, u32[]{:S(2)}, u32[]{:S(2)}) collective-permute-start(bf16[80,256]{1,0:T(8,128)(2,1)S(1)} %get-tuple-element.51), channel_id=1, source_target_pairs={{0,12},{1,13},{2,14},{3,15},{4,8},{5,9},{6,10},{7,11},{8,4},{9,5},... | collective-permute-start | bytes 122888 | tf_op jit(solution)/shard_map/ppermute | solution.py:372
  11.8 3.8 %collective-permute-start.2 = (bf16[80,256]{1,0:T(8,128)(2,1)S(1)}, bf16[80,256]{1,0:T(8,128)(2,1)S(1)}, u32[]{:S(2)}, u32[]{:S(2)}) collective-permute-start(bf16[80,256]{1,0:T(8,128)(2,1)S(1)} %get-tuple-element.52), channel_id=1, source_target_pairs={{0,8},{1,9},{2,10},{3,11},{4,12},{5,13},{6,14},{7,15},{8,0},{9,1},... | collective-permute-start | bytes 122888 | tf_op jit(solution)/shard_map/ppermute | solution.py:372
  13.0 3.0 %collective-permute-start.3 = (bf16[80,256]{1,0:T(8,128)(2,1)S(1)}, bf16[80,256]{1,0:T(8,128)(2,1)S(1)}, u32[]{:S(2)}, u32[]{:S(2)}) collective-permute-start(bf16[80,256]{1,0:T(8,128)(2,1)S(1)} %get-tuple-element.53), channel_id=1, source_target_pairs={{0,4},{1,5},{2,6},{3,7},{4,0},{5,1},{6,2},{7,3},{8,12},{9,13},{10,... | collective-permute-start | bytes 122888 | tf_op jit(solution)/shard_map/ppermute | solution.py:372
  13.8 1.0 %copy-start.1 = (bf16[1,2,400,256]{3,2,1,0:T(8,128)(2,1)S(1)}, bf16[1,2,400,256]{3,2,1,0:T(8,128)(2,1)}, u32[]{:S(2)}) copy-start(bf16[1,2,400,256]{3,2,1,0:T(8,128)(2,1)} %param.13) | copy-start | bytes 1228804
  16.1 6.5 %collective-permute-start.6 = (bf16[288,256]{1,0:T(8,128)(2,1)S(1)}, bf16[288,256]{1,0:T(8,128)(2,1)S(1)}, u32[]{:S(2)}, u32[]{:S(2)}) collective-permute-start(bf16[288,256]{1,0:T(8,128)(2,1)S(1)} %get-tuple-element.62), channel_id=1, source_target_pairs={{0,3},{1,2},{2,1},{3,0},{4,7},{5,6},{6,5},{7,4},{8,11},{9,10},{10,... | collective-permute-start | bytes 442376 | tf_op jit(solution)/shard_map/ppermute | solution.py:372
  18.9 5.6 %collective-permute-start.5 = (bf16[288,256]{1,0:T(8,128)(2,1)S(1)}, bf16[288,256]{1,0:T(8,128)(2,1)S(1)}, u32[]{:S(2)}, u32[]{:S(2)}) collective-permute-start(bf16[288,256]{1,0:T(8,128)(2,1)S(1)} %get-tuple-element.61), channel_id=1, source_target_pairs={{0,2},{1,3},{2,0},{3,1},{4,6},{5,7},{6,4},{7,5},{8,10},{9,11},{10,... | collective-permute-start | bytes 442376 | tf_op jit(solution)/shard_map/ppermute | solution.py:372
  19.3 6.4 %collective-permute-start.4 = (bf16[288,256]{1,0:T(8,128)(2,1)S(1)}, bf16[288,256]{1,0:T(8,128)(2,1)S(1)}, u32[]{:S(2)}, u32[]{:S(2)}) collective-permute-start(bf16[288,256]{1,0:T(8,128)(2,1)S(1)} %get-tuple-element.60), channel_id=1, source_target_pairs={{0,1},{1,0},{2,3},{3,2},{4,5},{5,4},{6,7},{7,6},{8,9},{9,8},{10,11... | collective-permute-start | bytes 442376 | tf_op jit(solution)/shard_map/ppermute | solution.py:372
  25.7 1.3 %copy-start.3 = (bf16[2304,256]{1,0:T(8,128)(2,1)S(1)}, bf16[2304,256]{1,0:T(8,128)(2,1)}, u32[]{:S(2)}) copy-start(bf16[2304,256]{1,0:T(8,128)(2,1)} %weight.4) | copy-start | bytes 3538948
  30.0 6.3 %collective-permute-start.7 = (bf16[2304,128]{1,0:T(8,128)(2,1)S(1)}, bf16[2304,128]{1,0:T(8,128)(2,1)S(1)}, u32[]{:S(2)}, u32[]{:S(2)}) collective-permute-start(bf16[2304,128]{1,0:T(8,128)(2,1)S(1)} %get-tuple-element.67), channel_id=1, source_target_pairs={{0,32},{32,0},{64,96},{96,64},{128,160},{160,128},{192,224},{224,1... | collective-permute-start | bytes 1769480 | tf_op jit(solution)/shard_map/ppermute | solution.py:372
  35.7 4.1 %copy-start = (bf16[2304,256]{1,0:T(8,128)(2,1)S(1)}, bf16[2304,256]{1,0:T(8,128)(2,1)}, u32[]{:S(2)}) copy-start(bf16[2304,256]{1,0:T(8,128)(2,1)} %weight.7) | copy-start | bytes 3538948
  35.7 4.1 %copy-start.2 = (bf16[1,2,400,256]{3,2,1,0:T(8,128)(2,1)S(1)}, bf16[1,2,400,256]{3,2,1,0:T(8,128)(2,1)}, u32[]{:S(2)}) copy-start(bf16[1,2,400,256]{3,2,1,0:T(8,128)(2,1)} %param.13) | copy-start | bytes 1228804
  36.5 8.1 %collective-permute-start.8 = (bf16[8,72,128]{2,1,0:T(8,128)(2,1)S(1)}, bf16[8,72,128]{2,1,0:T(8,128)(2,1)S(1)}, u32[]{:S(2)}, u32[]{:S(2)}) collective-permute-start(bf16[8,72,128]{2,1,0:T(8,128)(2,1)S(1)} %get-tuple-element.70), channel_id=1, source_target_pairs={{0,3},{1,2},{2,1},{3,0},{4,7},{5,6},{6,5},{7,4},{8,11},{9,10},{10,... | collective-permute-start | bytes 442376 | tf_op jit(solution)/shard_map/ppermute | solution.py:372
  38.7 6.3 %collective-permute-start.9 = (bf16[8,72,128]{2,1,0:T(8,128)(2,1)S(1)}, bf16[8,72,128]{2,1,0:T(8,128)(2,1)S(1)}, u32[]{:S(2)}, u32[]{:S(2)}) collective-permute-start(bf16[8,72,128]{2,1,0:T(8,128)(2,1)S(1)} %get-tuple-element.71), channel_id=1, source_target_pairs={{0,2},{1,3},{2,0},{3,1},{4,6},{5,7},{6,4},{7,5},{8,10},{9,11},{10,... | collective-permute-start | bytes 442376 | tf_op jit(solution)/shard_map/ppermute | solution.py:372
  38.7 7.6 %collective-permute-start.10 = (bf16[8,72,128]{2,1,0:T(8,128)(2,1)S(1)}, bf16[8,72,128]{2,1,0:T(8,128)(2,1)S(1)}, u32[]{:S(2)}, u32[]{:S(2)}) collective-permute-start(bf16[8,72,128]{2,1,0:T(8,128)(2,1)S(1)} %get-tuple-element.72), channel_id=1, source_target_pairs={{0,1},{1,0},{2,3},{3,2},{4,5},{5,4},{6,7},{7,6},{8,9},{9,8},{10,11... | collective-permute-start | bytes 442376 | tf_op jit(solution)/shard_map/ppermute | solution.py:372
  46.4 3.6 %collective-permute-start.13 = (bf16[2,72,128]{2,1,0:T(8,128)(2,1)S(1)}, bf16[2,72,128]{2,1,0:T(8,128)(2,1)S(1)}, u32[]{:S(2)}, u32[]{:S(2)}) collective-permute-start(bf16[2,72,128]{2,1,0:T(8,128)(2,1)S(1)} %get-tuple-element.82), channel_id=1, source_target_pairs={{0,4},{1,5},{2,6},{3,7},{4,0},{5,1},{6,2},{7,3},{8,12},{9,13},{10,... | collective-permute-start | bytes 110600 | tf_op jit(solution)/shard_map/ppermute | solution.py:372
  47.3 3.7 %collective-permute-start.12 = (bf16[2,72,128]{2,1,0:T(8,128)(2,1)S(1)}, bf16[2,72,128]{2,1,0:T(8,128)(2,1)S(1)}, u32[]{:S(2)}, u32[]{:S(2)}) collective-permute-start(bf16[2,72,128]{2,1,0:T(8,128)(2,1)S(1)} %get-tuple-element.81), channel_id=1, source_target_pairs={{0,8},{1,9},{2,10},{3,11},{4,12},{5,13},{6,14},{7,15},{8,0},{9,1},... | collective-permute-start | bytes 110600 | tf_op jit(solution)/shard_map/ppermute | solution.py:372
  48.5 4.6 %collective-permute-start.11 = (bf16[2,72,128]{2,1,0:T(8,128)(2,1)S(1)}, bf16[2,72,128]{2,1,0:T(8,128)(2,1)S(1)}, u32[]{:S(2)}, u32[]{:S(2)}) collective-permute-start(bf16[2,72,128]{2,1,0:T(8,128)(2,1)S(1)} %get-tuple-element.80), channel_id=1, source_target_pairs={{0,12},{1,13},{2,14},{3,15},{4,8},{5,9},{6,10},{7,11},{8,4},{9,5},... | collective-permute-start | bytes 110600 | tf_op jit(solution)/shard_map/ppermute | solution.py:372
  53.2 6.0 %collective-permute-start.14 = (bf16[72,128]{1,0:T(8,128)(2,1)S(1)}, bf16[72,128]{1,0:T(8,128)(2,1)S(1)}, u32[]{:S(2)}, u32[]{:S(2)}) collective-permute-start(bf16[72,128]{1,0:T(8,128)(2,1)S(1)} %fusion.2), channel_id=1, source_target_pairs={{0,28},{1,29},{2,30},{3,31},{4,24},{5,25},{6,26},{7,27},{8,20},{9,... | collective-permute-start | bytes 55304 | tf_op jit(solution)/shard_map/ppermute | solution.py:372
  57.0 8.8 %collective-permute-start.18 = (bf16[400,256]{1,0:T(8,128)(2,1)S(1)}, bf16[400,256]{1,0:T(8,128)(2,1)S(1)}, u32[]{:S(2)}, u32[]{:S(2)}) collective-permute-start(bf16[400,256]{1,0:T(8,128)(2,1)S(1)} %get-tuple-element.86), channel_id=1, source_target_pairs={{0,1},{1,0},{2,3},{3,2},{4,5},{5,4},{6,7},{7,6},{8,9},{9,8},{10,11... | collective-permute-start | bytes 614408 | tf_op jit(solution)/shard_map/ppermute | solution.py:372
  57.7 8.1 %collective-permute-start.19 = (bf16[400,256]{1,0:T(8,128)(2,1)S(1)}, bf16[400,256]{1,0:T(8,128)(2,1)S(1)}, u32[]{:S(2)}, u32[]{:S(2)}) collective-permute-start(bf16[400,256]{1,0:T(8,128)(2,1)S(1)} %get-tuple-element.87), channel_id=1, source_target_pairs={{0,31},{1,2},{2,1},{3,4},{4,3},{5,6},{6,5},{7,8},{8,7},{9,10},{10,... | collective-permute-start | bytes 614408 | tf_op jit(solution)/shard_map/ppermute | solution.py:372
  59.2 3.9 %collective-permute-start.15 = (bf16[72,128]{1,0:T(8,128)(2,1)S(1)}, bf16[72,128]{1,0:T(8,128)(2,1)S(1)}, u32[]{:S(2)}, u32[]{:S(2)}) collective-permute-start(bf16[72,128]{1,0:T(8,128)(2,1)S(1)} %fusion.1), channel_id=1, source_target_pairs={{0,192},{32,224},{64,128},{96,160},{128,64},{160,96},{192,0},{224,... | collective-permute-start | bytes 55304 | tf_op jit(solution)/shard_map/ppermute | solution.py:372
  61.7 4.1 %collective-permute-start.16 = (bf16[72,128]{1,0:T(8,128)(2,1)S(1)}, bf16[72,128]{1,0:T(8,128)(2,1)S(1)}, u32[]{:S(2)}, u32[]{:S(2)}) collective-permute-start(bf16[72,128]{1,0:T(8,128)(2,1)S(1)} %fusion.1), channel_id=1, source_target_pairs={{0,128},{32,160},{64,192},{96,224},{128,0},{160,32},{192,64},{224,... | collective-permute-start | bytes 55304 | tf_op jit(solution)/shard_map/ppermute | solution.py:372
  62.3 3.6 %collective-permute-start.17 = (bf16[72,128]{1,0:T(8,128)(2,1)S(1)}, bf16[72,128]{1,0:T(8,128)(2,1)S(1)}, u32[]{:S(2)}, u32[]{:S(2)}) collective-permute-start(bf16[72,128]{1,0:T(8,128)(2,1)S(1)} %fusion.1), channel_id=1, source_target_pairs={{0,64},{32,96},{64,0},{96,32},{128,192},{160,224},{192,128},{224,1... | collective-permute-start | bytes 55304 | tf_op jit(solution)/shard_map/ppermute | solution.py:372
  65.9 6.3 %collective-permute-start.20 = (f32[72,128]{1,0:T(8,128)S(1)}, f32[72,128]{1,0:T(8,128)S(1)}, u32[]{:S(2)}, u32[]{:S(2)}) collective-permute-start(f32[72,128]{1,0:T(8,128)S(1)} %convert_add_fusion.1.ours), channel_id=1, source_target_pairs={{0,32},{32,0},{64,96},{96,64},{128,160},{160,128},{192,224},{224,1... | collective-permute-start | bytes 110600 | tf_op jit(solution)/shard_map/ppermute | solution.py:372

commit v7 on v6

--- a/solution.py
+++ b/solution.py
@@ -457,7 +457,7 @@
         compiler_params=params(4),
         name="strip",
     )(*line)
-    arrived = [swap(messages[k], "tile", line_swap(k)) for k in (3, 2, 1)]
+    arrived = [swap(messages[k], "tile", line_swap(k)) for k in (2, 1, 3)]
 
     def splat_scratch(count):
         total = count * 8 * slots
@@ -540,7 +540,7 @@
         compiler_params=params(2),
         name="parts",
     )(kept.reshape(strips, share, half), taken.reshape(strips, share, half))
-    fetched = [swap(parts[k], "tile", line_swap(k)) for k in (3, 2, 1)]
+    fetched = [swap(parts[k], "tile", line_swap(k)) for k in (2, 3, 1)]
     scene = pl.pallas_call(
         functools.partial(scene_kernel, breadth),
         out_shape=struct((2, breadth, planes), BF16),
@@ -569,7 +569,7 @@
         compiler_params=params(2),
         name="planes",
     )(parts[0], *fetched)
-    fetched = [swap(pairs[k], "tile", line_swap(4 * k)) for k in (3, 2, 1)]
+    fetched = [swap(pairs[k], "tile", line_swap(4 * k)) for k in (1, 2, 3)]
     pair = added(pairs[0], *fetched)
     ours = pair[0]
     theirs, near, far = lax.optimization_barrier((pair[1].astype(BF16), near, far))

time: 73.1 us -> 70.8 us (0.969)
  starting transfers between devices: 39.5 us -> 35.8 us
  waiting for transfers between devices: 15.7 us -> 16.9 us
    ppermute x21, starting transfers between devices: 39.5 us -> 35.8 us  [swap(): lax.ppermute(values, axis, [(i, partner(i)) for i in range(lax.axis_size(...]
    ppermute x21, waiting for transfers between devices: 15.7 us -> 16.9 us  [swap(): lax.ppermute(values, axis, [(i, partner(i)) for i in range(lax.axis_size(...]
  transfers between devices with their start and end apart: 21 -> 21, of which waited for: 13 -> 14; matrix products, arithmetic and copies ran while one was open for 0% -> 0% of each run, Pallas kernels for 12% -> 13%
where the time goes in v7:
time: 70.8 us; the launch traced here: 70.4 us
  starting transfers between devices  35.8 us (51%)
  waiting for transfers between devices  16.9 us (24%)
  Pallas kernels  15.8 us (22%)
  local copies, waits for them, and re-layouts  1.02 us (1%)
  between operations  0.8 us (1%)
    ppermute x21, starting transfers between devices, swap(): lax.ppermute(values, axis, [(i, partner(i)) for i in range(lax.axis_size(...  35.8 us
    ppermute x21, waiting for transfers between devices, swap(): lax.ppermute(values, axis, [(i, partner(i)) for i in range(lax.axis_size(...  16.9 us
    pallas_call x1, Pallas kernels, on_device(): pl.pallas_call(functools.partial(hidden_kernel, breadth), out_shape=(held...  3.05 us
    pallas_call x2, Pallas kernels, on_device(): pl.pallas_call(more_kernel, out_shape=held((6, breadth, planes), F32), in...  2.21 us
    pallas_call x1, Pallas kernels, on_device(): pl.pallas_call(functools.partial(scene_kernel, breadth), out_shape=struct...  1.92 us
    pallas_call x1, Pallas kernels, on_device(): pl.pallas_call(pack_kernel, out_shape=held((places, planes), BF16), in_sp...  1.52 us
    pallas_call x1, Pallas kernels, on_device(): pl.pallas_call(functools.partial(derivative_kernel, breadth), out_shape=s...  1.42 us
  transfers between devices with their start and end apart: 21, of which 14 were waited for; matrix products, arithmetic and copies ran while one was open for 0% of the time, Pallas kernels for 13%

profile of v7, /device:TPU:1, one launch (start us, length us, event | category | flops | bytes accessed | tf_op | source)
XLA Modules:
  0.0 70.4 jit_solution(2396885713377841117)
XLA Ops:
  0.6 1.5 %pack.1.refs_0_ = bf16[64,256]{1,0:T(8,128)(2,1)S(1)} custom-call(bf16[32,256]{1,0:T(8,128)(2,1)} %bitcast.26, bf16[32,64]{1,0:T(8,128)(2,1)} %bitcast.29, s32[32,64]{1,0:T(8,128)} %bitcast.27, s32[32,64]{1,0:T(8,128)} %bitcast.28, s32[1,32]{1,0:T(1,128)} %bitcast.30), custom_call_target="tpu_custom_call" | custom-call | tf_op jit(solution)/shard_map/pack/pallas_call | solution.py:409
  2.2 6.5 %collective-permute-start = (bf16[64,256]{1,0:T(8,128)(2,1)S(1)}, bf16[64,256]{1,0:T(8,128)(2,1)S(1)}, u32[]{:S(2)}, u32[]{:S(2)}) collective-permute-start(bf16[64,256]{1,0:T(8,128)(2,1)S(1)} %pack.1.refs_0_), channel_id=1, source_target_pairs={{0,28},{1,29},{2,30},{3,31},{4,24},{5,25},{6,26},{7,27},{8,20},{9,... | collective-permute-start | bytes 98312 | tf_op jit(solution)/shard_map/ppermute | solution.py:372
  8.7 1.3 %collective-permute-done.refs_1_ = bf16[64,256]{1,0:T(8,128)(2,1)S(1)} collective-permute-done((bf16[64,256]{1,0:T(8,128)(2,1)S(1)}, bf16[64,256]{1,0:T(8,128)(2,1)S(1)}, u32[]{:S(2)}, u32[]{:S(2)}) %collective-permute-start) | collective-permute-done | bytes 32800 | tf_op jit(solution)/shard_map/ppermute | solution.py:372
  10.0 0.2 line.1
  10.1 1.7 %collective-permute-start.1 = (bf16[80,256]{1,0:T(8,128)(2,1)S(1)}, bf16[80,256]{1,0:T(8,128)(2,1)S(1)}, u32[]{:S(2)}, u32[]{:S(2)}) collective-permute-start(bf16[80,256]{1,0:T(8,128)(2,1)S(1)} %get-tuple-element.51), channel_id=1, source_target_pairs={{0,12},{1,13},{2,14},{3,15},{4,8},{5,9},{6,10},{7,11},{8,4},{9,5},... | collective-permute-start | bytes 122888 | tf_op jit(solution)/shard_map/ppermute | solution.py:372
  11.8 1.2 %collective-permute-start.2 = (bf16[80,256]{1,0:T(8,128)(2,1)S(1)}, bf16[80,256]{1,0:T(8,128)(2,1)S(1)}, u32[]{:S(2)}, u32[]{:S(2)}) collective-permute-start(bf16[80,256]{1,0:T(8,128)(2,1)S(1)} %get-tuple-element.52), channel_id=1, source_target_pairs={{0,8},{1,9},{2,10},{3,11},{4,12},{5,13},{6,14},{7,15},{8,0},{9,1},... | collective-permute-start | bytes 122888 | tf_op jit(solution)/shard_map/ppermute | solution.py:372
  13.0 0.7 %collective-permute-start.3 = (bf16[80,256]{1,0:T(8,128)(2,1)S(1)}, bf16[80,256]{1,0:T(8,128)(2,1)S(1)}, u32[]{:S(2)}, u32[]{:S(2)}) collective-permute-start(bf16[80,256]{1,0:T(8,128)(2,1)S(1)} %get-tuple-element.53), channel_id=1, source_target_pairs={{0,4},{1,5},{2,6},{3,7},{4,0},{5,1},{6,2},{7,3},{8,12},{9,13},{10,... | collective-permute-start | bytes 122888 | tf_op jit(solution)/shard_map/ppermute | solution.py:372
  13.8 1.0 %copy-done.1 = bf16[1,2,400,256]{3,2,1,0:T(8,128)(2,1)S(1)} copy-done((bf16[1,2,400,256]{3,2,1,0:T(8,128)(2,1)S(1)}, bf16[1,2,400,256]{3,2,1,0:T(8,128)(2,1)}, u32[]{:S(2)}) %copy-start.1) | copy-done | bytes 409624
  14.8 0.4 moved.1
  15.2 0.4 collective-permute-done.2.refs_2_
  15.6 0.4 collective-permute-done.3.refs_3_
  16.1 3.0 %collective-permute-start.6 = (bf16[288,256]{1,0:T(8,128)(2,1)S(1)}, bf16[288,256]{1,0:T(8,128)(2,1)S(1)}, u32[]{:S(2)}, u32[]{:S(2)}) collective-permute-start(bf16[288,256]{1,0:T(8,128)(2,1)S(1)} %get-tuple-element.62), channel_id=1, source_target_pairs={{0,2},{1,3},{2,0},{3,1},{4,6},{5,7},{6,4},{7,5},{8,10},{9,11},{10,... | collective-permute-start | bytes 442376 | tf_op jit(solution)/shard_map/ppermute | solution.py:372
  19.1 0.4 collective-permute-start.5
  19.5 0.4 collective-permute-start.4
  19.9 1.1 %plane.1.before = f32[6,400,256]{2,1,0:T(8,128)S(1)} custom-call(bf16[288,256]{1,0:T(8,128)(2,1)S(1)} %get-tuple-element.63.message), custom_call_target="tpu_custom_call" | custom-call | flops 629145600 | bytes 1000000 | tf_op jit(solution)/shard_map/plane/pallas_call | solution.py:470
  21.0 0.7 collective-permute-done.6.message
  21.7 1.1 %more.1.before = f32[6,400,256]{2,1,0:T(8,128)S(1)} custom-call(bf16[288,256]{1,0:T(8,128)(2,1)S(1)} %collective-permute-done.6.message, f32[6,400,256]{2,1,0:T(8,128)S(1)} %plane.1.before), custom_call_target="tpu_custom_call" | custom-call | flops 629145600 | bytes 1000000 | tf_op jit(solution)/shard_map/more/pallas_call | solution.py:480
  22.8 0.8 %collective-permute-done.5.message = bf16[288,256]{1,0:T(8,128)(2,1)S(1)} collective-permute-done((bf16[288,256]{1,0:T(8,128)(2,1)S(1)}, bf16[288,256]{1,0:T(8,128)(2,1)S(1)}, u32[]{:S(2)}, u32[]{:S(2)}) %collective-permute-start.5) | collective-permute-done | bytes 147488 | tf_op jit(solution)/shard_map/ppermute | solution.py:372
  23.6 1.1 %again.1.before = f32[6,400,256]{2,1,0:T(8,128)S(1)} custom-call(bf16[288,256]{1,0:T(8,128)(2,1)S(1)} %collective-permute-done.5.message, f32[6,400,256]{2,1,0:T(8,128)S(1)} %more.1.before), custom_call_target="tpu_custom_call" | custom-call | flops 629145600 | bytes 1000000 | tf_op jit(solution)/shard_map/again/pallas_call | solution.py:490
  24.7 1.6 %collective-permute-done.4.message = bf16[288,256]{1,0:T(8,128)(2,1)S(1)} collective-permute-done((bf16[288,256]{1,0:T(8,128)(2,1)S(1)}, bf16[288,256]{1,0:T(8,128)(2,1)S(1)}, u32[]{:S(2)}, u32[]{:S(2)}) %collective-permute-start.4) | collective-permute-done | bytes 147488 | tf_op jit(solution)/shard_map/ppermute | solution.py:372
  26.3 1.3 %splat.1.bev = bf16[6,416,256]{2,1,0:T(8,128)(2,1)S(1)} custom-call(bf16[288,256]{1,0:T(8,128)(2,1)S(1)} %collective-permute-done.4.message, f32[6,400,256]{2,1,0:T(8,128)S(1)} %again.1.before), custom_call_target="tpu_custom_call" | custom-call | tf_op jit(solution)/shard_map/splat/pallas_call | solution.py:500
  27.6 3.0 %hidden.1 = (f32[2,416,256]{2,1,0:T(8,128)S(1)}, bf16[4,416,256]{2,1,0:T(8,128)(2,1)S(1)}, bf16[4,256,416]{2,1,0:T(8,128)(2,1)S(1)}, bf16[2304,128]{1,0:T(8,128)(2,1)S(1)}) custom-call(bf16[6,416,256]{2,1,0:T(8,128)(2,1)S(1)} %splat.1.bev, bf16[2304,256]{1,0:T(8,128)(2,1)S(1)} %copy-done.3, bf16[2,416,384]{2,1,0:T(8,128)(2,1)S(1)} %get-tuple-element.64.cotangent), custom_call_target="tpu_custom_call" | custom-call | tf_op jit(solution)/shard_map/hidden/pallas_call | solution.py:509
  30.6 3.5 %collective-permute-start.7 = (bf16[2304,128]{1,0:T(8,128)(2,1)S(1)}, bf16[2304,128]{1,0:T(8,128)(2,1)S(1)}, u32[]{:S(2)}, u32[]{:S(2)}) collective-permute-start(bf16[2304,128]{1,0:T(8,128)(2,1)S(1)} %get-tuple-element.67), channel_id=1, source_target_pairs={{0,32},{32,0},{64,96},{96,64},{128,160},{160,128},{192,224},{224,1... | collective-permute-start | bytes 1769480 | tf_op jit(solution)/shard_map/ppermute | solution.py:372
  34.1 1.0 %kept.1 = f32[2304,128]{1,0:T(8,128)S(1)} custom-call(bf16[4,256,416]{2,1,0:T(8,128)(2,1)S(1)} %get-tuple-element.65.columns, bf16[2,416,384]{2,1,0:T(8,128)(2,1)S(1)} %get-tuple-element.66.cotangent), custom_call_target="tpu_custom_call" | custom-call | flops 490733568 | bytes 1000000 | tf_op jit(solution)/shard_map/kept/pallas_call | solution.py:523
  35.1 0.6 collective-permute-done.7
  35.9 1.7 %collective-permute-start.8 = (bf16[8,72,128]{2,1,0:T(8,128)(2,1)S(1)}, bf16[8,72,128]{2,1,0:T(8,128)(2,1)S(1)}, u32[]{:S(2)}, u32[]{:S(2)}) collective-permute-start(bf16[8,72,128]{2,1,0:T(8,128)(2,1)S(1)} %get-tuple-element.70), channel_id=1, source_target_pairs={{0,2},{1,3},{2,0},{3,1},{4,6},{5,7},{6,4},{7,5},{8,10},{9,11},{10,... | collective-permute-start | bytes 442376 | tf_op jit(solution)/shard_map/ppermute | solution.py:372
  37.6 1.3 %collective-permute-start.9 = (bf16[8,72,128]{2,1,0:T(8,128)(2,1)S(1)}, bf16[8,72,128]{2,1,0:T(8,128)(2,1)S(1)}, u32[]{:S(2)}, u32[]{:S(2)}) collective-permute-start(bf16[8,72,128]{2,1,0:T(8,128)(2,1)S(1)} %get-tuple-element.71), channel_id=1, source_target_pairs={{0,3},{1,2},{2,1},{3,0},{4,7},{5,6},{6,5},{7,4},{8,11},{9,10},{10,... | collective-permute-start | bytes 442376 | tf_op jit(solution)/shard_map/ppermute | solution.py:372
  38.9 0.9 %inner.1.back = f32[2,416,256]{2,1,0:T(8,128)S(1)} custom-call(bf16[2,400,256]{2,1,0:T(8,128)(2,1)S(1)} %bitcast.22, bf16[2304,256]{1,0:T(8,128)(2,1)S(1)} %copy-done), custom_call_target="tpu_custom_call" | custom-call | flops 654311424 | bytes 1000000 | tf_op jit(solution)/shard_map/inner/pallas_call | solution.py:553
  39.8 1.9 %scene.1 = bf16[2,400,256]{2,1,0:T(8,128)(2,1)} custom-call(bf16[6,416,256]{2,1,0:T(8,128)(2,1)S(1)} %splat.1.bev, bf16[4,416,256]{2,1,0:T(8,128)(2,1)S(1)} %get-tuple-element.73.hidden, bf16[2304,256]{1,0:T(8,128)(2,1)S(1)} %copy-done), custom_call_target="tpu_custom_call" | custom-call | flops 981467136 | bytes 1000000 | tf_op jit(solution)/shard_map/scene/pallas_call | solution.py:544
  41.7 0.8 %collective-permute-done.8.one = bf16[8,72,128]{2,1,0:T(8,128)(2,1)S(1)} collective-permute-done((bf16[8,72,128]{2,1,0:T(8,128)(2,1)S(1)}, bf16[8,72,128]{2,1,0:T(8,128)(2,1)S(1)}, u32[]{:S(2)}, u32[]{:S(2)}) %collective-permute-start.8) | collective-permute-done | bytes 147488 | tf_op jit(solution)/shard_map/ppermute | solution.py:372
  42.6 3.9 %collective-permute-done.9.two = bf16[8,72,128]{2,1,0:T(8,128)(2,1)S(1)} collective-permute-done((bf16[8,72,128]{2,1,0:T(8,128)(2,1)S(1)}, bf16[8,72,128]{2,1,0:T(8,128)(2,1)S(1)}, u32[]{:S(2)}, u32[]{:S(2)}) %collective-permute-start.9) | collective-permute-done | bytes 147488 | tf_op jit(solution)/shard_map/ppermute | solution.py:372
  46.5 1.8 %collective-permute-start.13 = (bf16[2,72,128]{2,1,0:T(8,128)(2,1)S(1)}, bf16[2,72,128]{2,1,0:T(8,128)(2,1)S(1)}, u32[]{:S(2)}, u32[]{:S(2)}) collective-permute-start(bf16[2,72,128]{2,1,0:T(8,128)(2,1)S(1)} %get-tuple-element.82), channel_id=1, source_target_pairs={{0,12},{1,13},{2,14},{3,15},{4,8},{5,9},{6,10},{7,11},{8,4},{9,5},... | collective-permute-start | bytes 110600 | tf_op jit(solution)/shard_map/ppermute | solution.py:372
  48.3 0.2 collective-permute-start.12
  48.5 1.6 %collective-permute-start.11 = (bf16[2,72,128]{2,1,0:T(8,128)(2,1)S(1)}, bf16[2,72,128]{2,1,0:T(8,128)(2,1)S(1)}, u32[]{:S(2)}, u32[]{:S(2)}) collective-permute-start(bf16[2,72,128]{2,1,0:T(8,128)(2,1)S(1)} %get-tuple-element.80), channel_id=1, source_target_pairs={{0,4},{1,5},{2,6},{3,7},{4,0},{5,1},{6,2},{7,3},{8,12},{9,13},{10,... | collective-permute-start | bytes 110600 | tf_op jit(solution)/shard_map/ppermute | solution.py:372
  50.2 1.1 %collective-permute-done.13 = bf16[2,72,128]{2,1,0:T(8,128)(2,1)S(1)} collective-permute-done((bf16[2,72,128]{2,1,0:T(8,128)(2,1)S(1)}, bf16[2,72,128]{2,1,0:T(8,128)(2,1)S(1)}, u32[]{:S(2)}, u32[]{:S(2)}) %collective-permute-start.13) | collective-permute-done | bytes 36896 | tf_op jit(solution)/shard_map/ppermute | solution.py:372
  51.2 1.6 %collective-permute-done.12 = bf16[2,72,128]{2,1,0:T(8,128)(2,1)S(1)} collective-permute-done((bf16[2,72,128]{2,1,0:T(8,128)(2,1)S(1)}, bf16[2,72,128]{2,1,0:T(8,128)(2,1)S(1)}, u32[]{:S(2)}, u32[]{:S(2)}) %collective-permute-start.12) | collective-permute-done | bytes 36896 | tf_op jit(solution)/shard_map/ppermute | solution.py:372
  52.9 3.9 %collective-permute-start.14 = (bf16[72,128]{1,0:T(8,128)(2,1)S(1)}, bf16[72,128]{1,0:T(8,128)(2,1)S(1)}, u32[]{:S(2)}, u32[]{:S(2)}) collective-permute-start(bf16[72,128]{1,0:T(8,128)(2,1)S(1)} %fusion.2), channel_id=1, source_target_pairs={{0,28},{1,29},{2,30},{3,31},{4,24},{5,25},{6,26},{7,27},{8,20},{9,... | collective-permute-start | bytes 55304 | tf_op jit(solution)/shard_map/ppermute | solution.py:372
  56.8 0.5 collective-permute-start.18
  57.3 0.9 %collective-permute-start.19 = (bf16[400,256]{1,0:T(8,128)(2,1)S(1)}, bf16[400,256]{1,0:T(8,128)(2,1)S(1)}, u32[]{:S(2)}, u32[]{:S(2)}) collective-permute-start(bf16[400,256]{1,0:T(8,128)(2,1)S(1)} %get-tuple-element.87), channel_id=1, source_target_pairs={{0,31},{1,2},{2,1},{3,4},{4,3},{5,6},{6,5},{7,8},{8,7},{9,10},{10,... | collective-permute-start | bytes 614408 | tf_op jit(solution)/shard_map/ppermute | solution.py:372
  58.2 2.6 %collective-permute-start.15 = (bf16[72,128]{1,0:T(8,128)(2,1)S(1)}, bf16[72,128]{1,0:T(8,128)(2,1)S(1)}, u32[]{:S(2)}, u32[]{:S(2)}) collective-permute-start(bf16[72,128]{1,0:T(8,128)(2,1)S(1)} %fusion.1), channel_id=1, source_target_pairs={{0,192},{32,224},{64,128},{96,160},{128,64},{160,96},{192,0},{224,... | collective-permute-start | bytes 55304 | tf_op jit(solution)/shard_map/ppermute | solution.py:372
  60.8 0.5 collective-permute-start.16
  61.3 0.3 collective-permute-start.17
  61.5 0.6 collective-permute-done.15
  62.1 2.8 %collective-permute-done.16 = bf16[72,128]{1,0:T(8,128)(2,1)S(1)} collective-permute-done((bf16[72,128]{1,0:T(8,128)(2,1)S(1)}, bf16[72,128]{1,0:T(8,128)(2,1)S(1)}, u32[]{:S(2)}, u32[]{:S(2)}) %collective-permute-start.16) | collective-permute-done | bytes 18464 | tf_op jit(solution)/shard_map/ppermute | solution.py:372
  64.9 0.4 collective-permute-done.19.second
  65.3 3.0 %collective-permute-start.20 = (f32[72,128]{1,0:T(8,128)S(1)}, f32[72,128]{1,0:T(8,128)S(1)}, u32[]{:S(2)}, u32[]{:S(2)}) collective-permute-start(f32[72,128]{1,0:T(8,128)S(1)} %convert_add_fusion.1.ours), channel_id=1, source_target_pairs={{0,32},{32,0},{64,96},{96,64},{128,160},{160,128},{192,224},{224,1... | collective-permute-start | bytes 110600 | tf_op jit(solution)/shard_map/ppermute | solution.py:372
  68.3 1.4 %derivative.1 = bf16[2,400,256]{2,1,0:T(8,128)(2,1)} custom-call(bf16[400,256]{1,0:T(8,128)(2,1)S(1)} %collective-permute-done.18.first, bf16[400,256]{1,0:T(8,128)(2,1)S(1)} %collective-permute-done.19.second, f32[2,416,256]{2,1,0:T(8,128)S(1)} %inner.1.back, bf16[2304,256]{1,0:T(8,128)(2,1)S(1)} %copy-done, f32[2,416,256]{2,1,0:T(8,128)S(1)} %get-tuple-element.94.pre), custom_call_target="tpu_custom_call" | custom-call | flops 327155712 | bytes 1000000 | tf_op jit(solution)/shard_map/derivative/pallas_call | solution.py:581
  69.7 0.6 gradient.1
  (22 shorter events, 0.4 us)
Async XLA Ops:
  2.2 7.8 %collective-permute-start = (bf16[64,256]{1,0:T(8,128)(2,1)S(1)}, bf16[64,256]{1,0:T(8,128)(2,1)S(1)}, u32[]{:S(2)}, u32[]{:S(2)}) collective-permute-start(bf16[64,256]{1,0:T(8,128)(2,1)S(1)} %pack.1.refs_0_), channel_id=1, source_target_pairs={{0,28},{1,29},{2,30},{3,31},{4,24},{5,25},{6,26},{7,27},{8,20},{9,... | collective-permute-start | bytes 98312 | tf_op jit(solution)/shard_map/ppermute | solution.py:372
  10.1 5.0 %collective-permute-start.1 = (bf16[80,256]{1,0:T(8,128)(2,1)S(1)}, bf16[80,256]{1,0:T(8,128)(2,1)S(1)}, u32[]{:S(2)}, u32[]{:S(2)}) collective-permute-start(bf16[80,256]{1,0:T(8,128)(2,1)S(1)} %get-tuple-element.51), channel_id=1, source_target_pairs={{0,12},{1,13},{2,14},{3,15},{4,8},{5,9},{6,10},{7,11},{8,4},{9,5},... | collective-permute-start | bytes 122888 | tf_op jit(solution)/shard_map/ppermute | solution.py:372
  11.8 3.8 %collective-permute-start.2 = (bf16[80,256]{1,0:T(8,128)(2,1)S(1)}, bf16[80,256]{1,0:T(8,128)(2,1)S(1)}, u32[]{:S(2)}, u32[]{:S(2)}) collective-permute-start(bf16[80,256]{1,0:T(8,128)(2,1)S(1)} %get-tuple-element.52), channel_id=1, source_target_pairs={{0,8},{1,9},{2,10},{3,11},{4,12},{5,13},{6,14},{7,15},{8,0},{9,1},... | collective-permute-start | bytes 122888 | tf_op jit(solution)/shard_map/ppermute | solution.py:372
  13.0 3.0 %collective-permute-start.3 = (bf16[80,256]{1,0:T(8,128)(2,1)S(1)}, bf16[80,256]{1,0:T(8,128)(2,1)S(1)}, u32[]{:S(2)}, u32[]{:S(2)}) collective-permute-start(bf16[80,256]{1,0:T(8,128)(2,1)S(1)} %get-tuple-element.53), channel_id=1, source_target_pairs={{0,4},{1,5},{2,6},{3,7},{4,0},{5,1},{6,2},{7,3},{8,12},{9,13},{10,... | collective-permute-start | bytes 122888 | tf_op jit(solution)/shard_map/ppermute | solution.py:372
  13.8 1.0 %copy-start.1 = (bf16[1,2,400,256]{3,2,1,0:T(8,128)(2,1)S(1)}, bf16[1,2,400,256]{3,2,1,0:T(8,128)(2,1)}, u32[]{:S(2)}) copy-start(bf16[1,2,400,256]{3,2,1,0:T(8,128)(2,1)} %param.13) | copy-start | bytes 1228804
  16.1 5.6 %collective-permute-start.6 = (bf16[288,256]{1,0:T(8,128)(2,1)S(1)}, bf16[288,256]{1,0:T(8,128)(2,1)S(1)}, u32[]{:S(2)}, u32[]{:S(2)}) collective-permute-start(bf16[288,256]{1,0:T(8,128)(2,1)S(1)} %get-tuple-element.62), channel_id=1, source_target_pairs={{0,2},{1,3},{2,0},{3,1},{4,6},{5,7},{6,4},{7,5},{8,10},{9,11},{10,... | collective-permute-start | bytes 442376 | tf_op jit(solution)/shard_map/ppermute | solution.py:372
  19.1 4.5 %collective-permute-start.5 = (bf16[288,256]{1,0:T(8,128)(2,1)S(1)}, bf16[288,256]{1,0:T(8,128)(2,1)S(1)}, u32[]{:S(2)}, u32[]{:S(2)}) collective-permute-start(bf16[288,256]{1,0:T(8,128)(2,1)S(1)} %get-tuple-element.61), channel_id=1, source_target_pairs={{0,1},{1,0},{2,3},{3,2},{4,5},{5,4},{6,7},{7,6},{8,9},{9,8},{10,11... | collective-permute-start | bytes 442376 | tf_op jit(solution)/shard_map/ppermute | solution.py:372
  19.5 6.8 %collective-permute-start.4 = (bf16[288,256]{1,0:T(8,128)(2,1)S(1)}, bf16[288,256]{1,0:T(8,128)(2,1)S(1)}, u32[]{:S(2)}, u32[]{:S(2)}) collective-permute-start(bf16[288,256]{1,0:T(8,128)(2,1)S(1)} %get-tuple-element.60), channel_id=1, source_target_pairs={{0,3},{1,2},{2,1},{3,0},{4,7},{5,6},{6,5},{7,4},{8,11},{9,10},{10,... | collective-permute-start | bytes 442376 | tf_op jit(solution)/shard_map/ppermute | solution.py:372
  24.7 2.8 %copy-start.3 = (bf16[2304,256]{1,0:T(8,128)(2,1)S(1)}, bf16[2304,256]{1,0:T(8,128)(2,1)}, u32[]{:S(2)}) copy-start(bf16[2304,256]{1,0:T(8,128)(2,1)} %weight.4) | copy-start | bytes 3538948
  30.6 5.1 %collective-permute-start.7 = (bf16[2304,128]{1,0:T(8,128)(2,1)S(1)}, bf16[2304,128]{1,0:T(8,128)(2,1)S(1)}, u32[]{:S(2)}, u32[]{:S(2)}) collective-permute-start(bf16[2304,128]{1,0:T(8,128)(2,1)S(1)} %get-tuple-element.67), channel_id=1, source_target_pairs={{0,32},{32,0},{64,96},{96,64},{128,160},{160,128},{192,224},{224,1... | collective-permute-start | bytes 1769480 | tf_op jit(solution)/shard_map/ppermute | solution.py:372
  35.1 3.8 %copy-start = (bf16[2304,256]{1,0:T(8,128)(2,1)S(1)}, bf16[2304,256]{1,0:T(8,128)(2,1)}, u32[]{:S(2)}) copy-start(bf16[2304,256]{1,0:T(8,128)(2,1)} %weight.7) | copy-start | bytes 3538948
  35.1 3.8 %copy-start.2 = (bf16[1,2,400,256]{3,2,1,0:T(8,128)(2,1)S(1)}, bf16[1,2,400,256]{3,2,1,0:T(8,128)(2,1)}, u32[]{:S(2)}) copy-start(bf16[1,2,400,256]{3,2,1,0:T(8,128)(2,1)} %param.13) | copy-start | bytes 1228804
  35.9 6.7 %collective-permute-start.8 = (bf16[8,72,128]{2,1,0:T(8,128)(2,1)S(1)}, bf16[8,72,128]{2,1,0:T(8,128)(2,1)S(1)}, u32[]{:S(2)}, u32[]{:S(2)}) collective-permute-start(bf16[8,72,128]{2,1,0:T(8,128)(2,1)S(1)} %get-tuple-element.70), channel_id=1, source_target_pairs={{0,2},{1,3},{2,0},{3,1},{4,6},{5,7},{6,4},{7,5},{8,10},{9,11},{10,... | collective-permute-start | bytes 442376 | tf_op jit(solution)/shard_map/ppermute | solution.py:372
  37.6 8.8 %collective-permute-start.9 = (bf16[8,72,128]{2,1,0:T(8,128)(2,1)S(1)}, bf16[8,72,128]{2,1,0:T(8,128)(2,1)S(1)}, u32[]{:S(2)}, u32[]{:S(2)}) collective-permute-start(bf16[8,72,128]{2,1,0:T(8,128)(2,1)S(1)} %get-tuple-element.71), channel_id=1, source_target_pairs={{0,3},{1,2},{2,1},{3,0},{4,7},{5,6},{6,5},{7,4},{8,11},{9,10},{10,... | collective-permute-start | bytes 442376 | tf_op jit(solution)/shard_map/ppermute | solution.py:372
  38.9 7.5 %collective-permute-start.10 = (bf16[8,72,128]{2,1,0:T(8,128)(2,1)S(1)}, bf16[8,72,128]{2,1,0:T(8,128)(2,1)S(1)}, u32[]{:S(2)}, u32[]{:S(2)}) collective-permute-start(bf16[8,72,128]{2,1,0:T(8,128)(2,1)S(1)} %get-tuple-element.72), channel_id=1, source_target_pairs={{0,1},{1,0},{2,3},{3,2},{4,5},{5,4},{6,7},{7,6},{8,9},{9,8},{10,11... | collective-permute-start | bytes 442376 | tf_op jit(solution)/shard_map/ppermute | solution.py:372
  46.5 4.7 %collective-permute-start.13 = (bf16[2,72,128]{2,1,0:T(8,128)(2,1)S(1)}, bf16[2,72,128]{2,1,0:T(8,128)(2,1)S(1)}, u32[]{:S(2)}, u32[]{:S(2)}) collective-permute-start(bf16[2,72,128]{2,1,0:T(8,128)(2,1)S(1)} %get-tuple-element.82), channel_id=1, source_target_pairs={{0,12},{1,13},{2,14},{3,15},{4,8},{5,9},{6,10},{7,11},{8,4},{9,5},... | collective-permute-start | bytes 110600 | tf_op jit(solution)/shard_map/ppermute | solution.py:372
  48.3 4.5 %collective-permute-start.12 = (bf16[2,72,128]{2,1,0:T(8,128)(2,1)S(1)}, bf16[2,72,128]{2,1,0:T(8,128)(2,1)S(1)}, u32[]{:S(2)}, u32[]{:S(2)}) collective-permute-start(bf16[2,72,128]{2,1,0:T(8,128)(2,1)S(1)} %get-tuple-element.81), channel_id=1, source_target_pairs={{0,8},{1,9},{2,10},{3,11},{4,12},{5,13},{6,14},{7,15},{8,0},{9,1},... | collective-permute-start | bytes 110600 | tf_op jit(solution)/shard_map/ppermute | solution.py:372
  48.5 4.3 %collective-permute-start.11 = (bf16[2,72,128]{2,1,0:T(8,128)(2,1)S(1)}, bf16[2,72,128]{2,1,0:T(8,128)(2,1)S(1)}, u32[]{:S(2)}, u32[]{:S(2)}) collective-permute-start(bf16[2,72,128]{2,1,0:T(8,128)(2,1)S(1)} %get-tuple-element.80), channel_id=1, source_target_pairs={{0,4},{1,5},{2,6},{3,7},{4,0},{5,1},{6,2},{7,3},{8,12},{9,13},{10,... | collective-permute-start | bytes 110600 | tf_op jit(solution)/shard_map/ppermute | solution.py:372
  52.9 5.3 %collective-permute-start.14 = (bf16[72,128]{1,0:T(8,128)(2,1)S(1)}, bf16[72,128]{1,0:T(8,128)(2,1)S(1)}, u32[]{:S(2)}, u32[]{:S(2)}) collective-permute-start(bf16[72,128]{1,0:T(8,128)(2,1)S(1)} %fusion.2), channel_id=1, source_target_pairs={{0,28},{1,29},{2,30},{3,31},{4,24},{5,25},{6,26},{7,27},{8,20},{9,... | collective-permute-start | bytes 55304 | tf_op jit(solution)/shard_map/ppermute | solution.py:372
  56.8 8.1 %collective-permute-start.18 = (bf16[400,256]{1,0:T(8,128)(2,1)S(1)}, bf16[400,256]{1,0:T(8,128)(2,1)S(1)}, u32[]{:S(2)}, u32[]{:S(2)}) collective-permute-start(bf16[400,256]{1,0:T(8,128)(2,1)S(1)} %get-tuple-element.86), channel_id=1, source_target_pairs={{0,1},{1,0},{2,3},{3,2},{4,5},{5,4},{6,7},{7,6},{8,9},{9,8},{10,11... | collective-permute-start | bytes 614408 | tf_op jit(solution)/shard_map/ppermute | solution.py:372
  57.3 7.9 %collective-permute-start.19 = (bf16[400,256]{1,0:T(8,128)(2,1)S(1)}, bf16[400,256]{1,0:T(8,128)(2,1)S(1)}, u32[]{:S(2)}, u32[]{:S(2)}) collective-permute-start(bf16[400,256]{1,0:T(8,128)(2,1)S(1)} %get-tuple-element.87), channel_id=1, source_target_pairs={{0,31},{1,2},{2,1},{3,4},{4,3},{5,6},{6,5},{7,8},{8,7},{9,10},{10,... | collective-permute-start | bytes 614408 | tf_op jit(solution)/shard_map/ppermute | solution.py:372
  58.2 3.9 %collective-permute-start.15 = (bf16[72,128]{1,0:T(8,128)(2,1)S(1)}, bf16[72,128]{1,0:T(8,128)(2,1)S(1)}, u32[]{:S(2)}, u32[]{:S(2)}) collective-permute-start(bf16[72,128]{1,0:T(8,128)(2,1)S(1)} %fusion.1), channel_id=1, source_target_pairs={{0,192},{32,224},{64,128},{96,160},{128,64},{160,96},{192,0},{224,... | collective-permute-start | bytes 55304 | tf_op jit(solution)/shard_map/ppermute | solution.py:372
  60.8 4.1 %collective-permute-start.16 = (bf16[72,128]{1,0:T(8,128)(2,1)S(1)}, bf16[72,128]{1,0:T(8,128)(2,1)S(1)}, u32[]{:S(2)}, u32[]{:S(2)}) collective-permute-start(bf16[72,128]{1,0:T(8,128)(2,1)S(1)} %fusion.1), channel_id=1, source_target_pairs={{0,128},{32,160},{64,192},{96,224},{128,0},{160,32},{192,64},{224,... | collective-permute-start | bytes 55304 | tf_op jit(solution)/shard_map/ppermute | solution.py:372
  61.3 3.6 %collective-permute-start.17 = (bf16[72,128]{1,0:T(8,128)(2,1)S(1)}, bf16[72,128]{1,0:T(8,128)(2,1)S(1)}, u32[]{:S(2)}, u32[]{:S(2)}) collective-permute-start(bf16[72,128]{1,0:T(8,128)(2,1)S(1)} %fusion.1), channel_id=1, source_target_pairs={{0,64},{32,96},{64,0},{96,32},{128,192},{160,224},{192,128},{224,1... | collective-permute-start | bytes 55304 | tf_op jit(solution)/shard_map/ppermute | solution.py:372
  65.3 4.4 %collective-permute-start.20 = (f32[72,128]{1,0:T(8,128)S(1)}, f32[72,128]{1,0:T(8,128)S(1)}, u32[]{:S(2)}, u32[]{:S(2)}) collective-permute-start(f32[72,128]{1,0:T(8,128)S(1)} %convert_add_fusion.1.ours), channel_id=1, source_target_pairs={{0,32},{32,0},{64,96},{96,64},{128,160},{160,128},{192,224},{224,1... | collective-permute-start | bytes 110600 | tf_op jit(solution)/shard_map/ppermute | solution.py:372

commit v8 on v7

--- a/solution.py
+++ b/solution.py
@@ -48,7 +48,7 @@
     ]
     for copy in copies:
         copy.start()
-    for copy in copies:
+    for copy in copies[:-1]:
         copy.wait()
     pixels, bins = scores.shape
     strips, slots = points.shape
@@ -80,6 +80,7 @@
     weights = jnp.where(low, coarse, pltpu.roll(weight - coarse, slots, 1))
     codes = jnp.where(low, upper, pltpu.roll(under, slots, 1))
     packed[pixels:] = jnp.concatenate([weights, codes], axis=1).astype(BF16)
+    copies[-1].wait()
 
 
 def line_kernel(*refs):
@@ -315,7 +316,7 @@
     )
 
 
-def inner_kernel(breadth, own, weight, back, field):
+def inner_kernel(breadth, own, weight, pre, back, slope, field):
     wide, planes = back.shape[1:]
     for k in range(2):
         field[k, :breadth] = own[k]
@@ -323,10 +324,14 @@
     stacked = jnp.concatenate([field[0], field[1]], axis=1)
     back[0] = joined(back_products(stacked, flipped_taps(weight, planes, (1, 0))), planes)
     back[1] = joined(back_products(stacked, flipped_taps(weight, planes, (2, 1))), planes)
-
-
-def derivative_kernel(breadth, first, second, back, weight, pre, derivative, field):
-    wide, planes = pre.shape[1:]
+    for y in range(2):
+        value = pre[y]
+        sigma = jax.nn.sigmoid(value)
+        slope[y] = sigma * (1.0 + value * (1.0 - sigma))
+
+
+def derivative_kernel(breadth, first, second, back, weight, slope, derivative, field):
+    wide, planes = slope.shape[1:]
     strip = lax.axis_index("tile")
     odd = strip % 2 == 1
     zero = jnp.zeros((breadth, planes), BF16)
@@ -338,10 +343,7 @@
         field[y, :breadth] = row
         field[y, breadth:] = jnp.zeros((wide - breadth, planes), BF16)
         rest = joined(back_products(field[y], flipped_taps(weight, planes, (a,))), planes)
-        value = pre[y, :breadth]
-        sigma = jax.nn.sigmoid(value)
-        slope = sigma * (1.0 + value * (1.0 - sigma))
-        derivative[y] = ((back[y, :breadth] + rest[:breadth]) * slope).astype(BF16)
+        derivative[y] = ((back[y, :breadth] + rest[:breadth]) * slope[y, :breadth]).astype(BF16)
 
 
 def parts_kernel(kept, taken, *parts):
@@ -550,17 +552,17 @@
         cost_estimate=pl.CostEstimate(flops=2 * 2 * wide * taps * planes, bytes_accessed=10**6, transcendentals=0),
         name="scene",
     )(bev, hidden, predictor_filter)
-    back = pl.pallas_call(
+    back, slope = pl.pallas_call(
         functools.partial(inner_kernel, breadth),
-        out_shape=held((2, wide, planes), F32),
-        in_specs=[vmem()] * 2,
-        out_specs=vmem(),
+        out_shape=(held((2, wide, planes), F32),) * 2,
+        in_specs=[vmem()] * 3,
+        out_specs=(vmem(),) * 2,
         scratch_shapes=[pltpu.VMEM((2, wide, planes), BF16)],
         compiler_params=params(8),
         cost_estimate=pl.CostEstimate(flops=4 * wide * taps * planes // 3 * 2, bytes_accessed=10**6, transcendentals=0),
         name="inner",
-    )(own, predictor_filter)
-    fetched, scene, back = lax.optimization_barrier((fetched, scene, back))
+    )(own, predictor_filter, pre)
+    fetched, scene, back, slope = lax.optimization_barrier((fetched, scene, back, slope))
     pairs = pl.pallas_call(
         planes_kernel,
         out_shape=tuple(held((2, share, half), F32 if k == 0 else BF16) for k in range(4)),
@@ -587,7 +589,7 @@
         compiler_params=params(8),
         cost_estimate=pl.CostEstimate(flops=4 * wide * taps * planes // 3, bytes_accessed=10**6, transcendentals=10**6),
         name="derivative",
-    )(first, second, back, predictor_filter, pre)
+    )(first, second, back, predictor_filter, slope)
     ours = added(ours, *fetched)
     other, derivative = lax.optimization_barrier((swap(ours, "dp", line_swap(1)), derivative))
     square_tally = lax.axis_size("dp") * height * strips * breadth

time: 70.8 us -> 72.9 us (1.030)
  starting transfers between devices: 35.8 us -> 38 us
    ppermute x21, starting transfers between devices: 35.8 us -> 38 us  [swap(): lax.ppermute(values, axis, [(i, partner(i)) for i in range(lax.axis_size(...]
  transfers between devices with their start and end apart: 21 -> 21, of which waited for: 14 -> 13; matrix products, arithmetic and copies ran while one was open for 0% -> 0% of each run, Pallas kernels for 13% -> 12%
where the time goes in v8:
time: 72.9 us; the launch traced here: 72.8 us
  starting transfers between devices  38 us (52%)
  waiting for transfers between devices  17.1 us (23%)
  Pallas kernels  15.8 us (22%)
  local copies, waits for them, and re-layouts  1.02 us (1%)
  between operations  0.8 us (1%)
    ppermute x21, starting transfers between devices, swap(): lax.ppermute(values, axis, [(i, partner(i)) for i in range(lax.axis_size(...  38 us
    ppermute x21, waiting for transfers between devices, swap(): lax.ppermute(values, axis, [(i, partner(i)) for i in range(lax.axis_size(...  17.1 us
    pallas_call x1, Pallas kernels, on_device(): pl.pallas_call(functools.partial(hidden_kernel, breadth), out_shape=(held...  3.05 us
    pallas_call x2, Pallas kernels, on_device(): pl.pallas_call(more_kernel, out_shape=held((6, breadth, planes), F32), in...  2.2 us
    pallas_call x1, Pallas kernels, on_device(): pl.pallas_call(functools.partial(scene_kernel, breadth), out_shape=struct...  1.92 us
    pallas_call x1, Pallas kernels, on_device(): pl.pallas_call(pack_kernel, out_shape=held((places, planes), BF16), in_sp...  1.49 us
  transfers between devices with their start and end apart: 21, of which 13 were waited for; matrix products, arithmetic and copies ran while one was open for 0% of the time, Pallas kernels for 12%

profile of v8, /device:TPU:1, one launch (start us, length us, event | category | flops | bytes accessed | tf_op | source)
XLA Modules:
  0.0 72.8 jit_solution(4951675419269256148)
XLA Ops:
  0.6 1.5 %pack.1.refs_0_ = bf16[64,256]{1,0:T(8,128)(2,1)S(1)} custom-call(bf16[32,256]{1,0:T(8,128)(2,1)} %bitcast.26, bf16[32,64]{1,0:T(8,128)(2,1)} %bitcast.29, s32[32,64]{1,0:T(8,128)} %bitcast.27, s32[32,64]{1,0:T(8,128)} %bitcast.28, s32[1,32]{1,0:T(1,128)} %bitcast.30), custom_call_target="tpu_custom_call" | custom-call | tf_op jit(solution)/shard_map/pack/pallas_call | solution.py:411
  2.1 6.5 %collective-permute-start = (bf16[64,256]{1,0:T(8,128)(2,1)S(1)}, bf16[64,256]{1,0:T(8,128)(2,1)S(1)}, u32[]{:S(2)}, u32[]{:S(2)}) collective-permute-start(bf16[64,256]{1,0:T(8,128)(2,1)S(1)} %pack.1.refs_0_), channel_id=1, source_target_pairs={{0,28},{1,29},{2,30},{3,31},{4,24},{5,25},{6,26},{7,27},{8,20},{9,... | collective-permute-start | bytes 98312 | tf_op jit(solution)/shard_map/ppermute | solution.py:374
  8.6 1.3 %collective-permute-done.refs_1_ = bf16[64,256]{1,0:T(8,128)(2,1)S(1)} collective-permute-done((bf16[64,256]{1,0:T(8,128)(2,1)S(1)}, bf16[64,256]{1,0:T(8,128)(2,1)S(1)}, u32[]{:S(2)}, u32[]{:S(2)}) %collective-permute-start) | collective-permute-done | bytes 32800 | tf_op jit(solution)/shard_map/ppermute | solution.py:374
  9.9 0.2 line.1
  10.1 1.7 %collective-permute-start.1 = (bf16[80,256]{1,0:T(8,128)(2,1)S(1)}, bf16[80,256]{1,0:T(8,128)(2,1)S(1)}, u32[]{:S(2)}, u32[]{:S(2)}) collective-permute-start(bf16[80,256]{1,0:T(8,128)(2,1)S(1)} %get-tuple-element.54), channel_id=1, source_target_pairs={{0,12},{1,13},{2,14},{3,15},{4,8},{5,9},{6,10},{7,11},{8,4},{9,5},... | collective-permute-start | bytes 122888 | tf_op jit(solution)/shard_map/ppermute | solution.py:374
  11.8 1.2 %collective-permute-start.2 = (bf16[80,256]{1,0:T(8,128)(2,1)S(1)}, bf16[80,256]{1,0:T(8,128)(2,1)S(1)}, u32[]{:S(2)}, u32[]{:S(2)}) collective-permute-start(bf16[80,256]{1,0:T(8,128)(2,1)S(1)} %get-tuple-element.55), channel_id=1, source_target_pairs={{0,8},{1,9},{2,10},{3,11},{4,12},{5,13},{6,14},{7,15},{8,0},{9,1},... | collective-permute-start | bytes 122888 | tf_op jit(solution)/shard_map/ppermute | solution.py:374
  13.0 0.7 %collective-permute-start.3 = (bf16[80,256]{1,0:T(8,128)(2,1)S(1)}, bf16[80,256]{1,0:T(8,128)(2,1)S(1)}, u32[]{:S(2)}, u32[]{:S(2)}) collective-permute-start(bf16[80,256]{1,0:T(8,128)(2,1)S(1)} %get-tuple-element.56), channel_id=1, source_target_pairs={{0,4},{1,5},{2,6},{3,7},{4,0},{5,1},{6,2},{7,3},{8,12},{9,13},{10,... | collective-permute-start | bytes 122888 | tf_op jit(solution)/shard_map/ppermute | solution.py:374
  13.7 1.0 %copy-done.1 = bf16[1,2,400,256]{3,2,1,0:T(8,128)(2,1)S(1)} copy-done((bf16[1,2,400,256]{3,2,1,0:T(8,128)(2,1)S(1)}, bf16[1,2,400,256]{3,2,1,0:T(8,128)(2,1)}, u32[]{:S(2)}) %copy-start.1) | copy-done | bytes 409624
  14.7 0.4 moved.1
  15.1 0.4 collective-permute-done.2.refs_2_
  15.6 0.4 collective-permute-done.3.refs_3_
  16.1 3.0 %collective-permute-start.6 = (bf16[288,256]{1,0:T(8,128)(2,1)S(1)}, bf16[288,256]{1,0:T(8,128)(2,1)S(1)}, u32[]{:S(2)}, u32[]{:S(2)}) collective-permute-start(bf16[288,256]{1,0:T(8,128)(2,1)S(1)} %get-tuple-element.65), channel_id=1, source_target_pairs={{0,2},{1,3},{2,0},{3,1},{4,6},{5,7},{6,4},{7,5},{8,10},{9,11},{10,... | collective-permute-start | bytes 442376 | tf_op jit(solution)/shard_map/ppermute | solution.py:374
  19.1 0.4 collective-permute-start.5
  19.5 0.4 collective-permute-start.4
  19.9 1.1 %plane.1.before = f32[6,400,256]{2,1,0:T(8,128)S(1)} custom-call(bf16[288,256]{1,0:T(8,128)(2,1)S(1)} %get-tuple-element.66.message), custom_call_target="tpu_custom_call" | custom-call | flops 629145600 | bytes 1000000 | tf_op jit(solution)/shard_map/plane/pallas_call | solution.py:472
  21.0 0.7 collective-permute-done.6.message
  21.7 1.1 %more.1.before = f32[6,400,256]{2,1,0:T(8,128)S(1)} custom-call(bf16[288,256]{1,0:T(8,128)(2,1)S(1)} %collective-permute-done.6.message, f32[6,400,256]{2,1,0:T(8,128)S(1)} %plane.1.before), custom_call_target="tpu_custom_call" | custom-call | flops 629145600 | bytes 1000000 | tf_op jit(solution)/shard_map/more/pallas_call | solution.py:482
  22.8 0.8 %collective-permute-done.5.message = bf16[288,256]{1,0:T(8,128)(2,1)S(1)} collective-permute-done((bf16[288,256]{1,0:T(8,128)(2,1)S(1)}, bf16[288,256]{1,0:T(8,128)(2,1)S(1)}, u32[]{:S(2)}, u32[]{:S(2)}) %collective-permute-start.5) | collective-permute-done | bytes 147488 | tf_op jit(solution)/shard_map/ppermute | solution.py:374
  23.6 1.1 %again.1.before = f32[6,400,256]{2,1,0:T(8,128)S(1)} custom-call(bf16[288,256]{1,0:T(8,128)(2,1)S(1)} %collective-permute-done.5.message, f32[6,400,256]{2,1,0:T(8,128)S(1)} %more.1.before), custom_call_target="tpu_custom_call" | custom-call | flops 629145600 | bytes 1000000 | tf_op jit(solution)/shard_map/again/pallas_call | solution.py:492
  24.7 1.6 %collective-permute-done.4.message = bf16[288,256]{1,0:T(8,128)(2,1)S(1)} collective-permute-done((bf16[288,256]{1,0:T(8,128)(2,1)S(1)}, bf16[288,256]{1,0:T(8,128)(2,1)S(1)}, u32[]{:S(2)}, u32[]{:S(2)}) %collective-permute-start.4) | collective-permute-done | bytes 147488 | tf_op jit(solution)/shard_map/ppermute | solution.py:374
  26.3 1.3 %splat.1.bev = bf16[6,416,256]{2,1,0:T(8,128)(2,1)S(1)} custom-call(bf16[288,256]{1,0:T(8,128)(2,1)S(1)} %collective-permute-done.4.message, f32[6,400,256]{2,1,0:T(8,128)S(1)} %again.1.before), custom_call_target="tpu_custom_call" | custom-call | tf_op jit(solution)/shard_map/splat/pallas_call | solution.py:502
  27.5 3.0 %hidden.1 = (f32[2,416,256]{2,1,0:T(8,128)S(1)}, bf16[4,416,256]{2,1,0:T(8,128)(2,1)S(1)}, bf16[4,256,416]{2,1,0:T(8,128)(2,1)S(1)}, bf16[2304,128]{1,0:T(8,128)(2,1)S(1)}) custom-call(bf16[6,416,256]{2,1,0:T(8,128)(2,1)S(1)} %splat.1.bev, bf16[2304,256]{1,0:T(8,128)(2,1)S(1)} %copy-done.3, bf16[2,416,384]{2,1,0:T(8,128)(2,1)S(1)} %get-tuple-element.67.cotangent), custom_call_target="tpu_custom_call" | custom-call | tf_op jit(solution)/shard_map/hidden/pallas_call | solution.py:511
  30.6 3.5 %collective-permute-start.7 = (bf16[2304,128]{1,0:T(8,128)(2,1)S(1)}, bf16[2304,128]{1,0:T(8,128)(2,1)S(1)}, u32[]{:S(2)}, u32[]{:S(2)}) collective-permute-start(bf16[2304,128]{1,0:T(8,128)(2,1)S(1)} %get-tuple-element.70), channel_id=1, source_target_pairs={{0,32},{32,0},{64,96},{96,64},{128,160},{160,128},{192,224},{224,1... | collective-permute-start | bytes 1769480 | tf_op jit(solution)/shard_map/ppermute | solution.py:374
  34.1 1.0 %kept.1 = f32[2304,128]{1,0:T(8,128)S(1)} custom-call(bf16[4,256,416]{2,1,0:T(8,128)(2,1)S(1)} %get-tuple-element.68.columns, bf16[2,416,384]{2,1,0:T(8,128)(2,1)S(1)} %get-tuple-element.69.cotangent), custom_call_target="tpu_custom_call" | custom-call | flops 490733568 | bytes 1000000 | tf_op jit(solution)/shard_map/kept/pallas_call | solution.py:525
  35.1 0.6 collective-permute-done.7
  35.7 0.1 parts.1
  35.9 1.7 %collective-permute-start.8 = (bf16[8,72,128]{2,1,0:T(8,128)(2,1)S(1)}, bf16[8,72,128]{2,1,0:T(8,128)(2,1)S(1)}, u32[]{:S(2)}, u32[]{:S(2)}) collective-permute-start(bf16[8,72,128]{2,1,0:T(8,128)(2,1)S(1)} %get-tuple-element.73), channel_id=1, source_target_pairs={{0,2},{1,3},{2,0},{3,1},{4,6},{5,7},{6,4},{7,5},{8,10},{9,11},{10,... | collective-permute-start | bytes 442376 | tf_op jit(solution)/shard_map/ppermute | solution.py:374
  37.6 1.3 %collective-permute-start.9 = (bf16[8,72,128]{2,1,0:T(8,128)(2,1)S(1)}, bf16[8,72,128]{2,1,0:T(8,128)(2,1)S(1)}, u32[]{:S(2)}, u32[]{:S(2)}) collective-permute-start(bf16[8,72,128]{2,1,0:T(8,128)(2,1)S(1)} %get-tuple-element.74), channel_id=1, source_target_pairs={{0,3},{1,2},{2,1},{3,0},{4,7},{5,6},{6,5},{7,4},{8,11},{9,10},{10,... | collective-permute-start | bytes 442376 | tf_op jit(solution)/shard_map/ppermute | solution.py:374
  38.9 1.1 %inner.1 = (f32[2,416,256]{2,1,0:T(8,128)S(1)}, f32[2,416,256]{2,1,0:T(8,128)S(1)}) custom-call(bf16[2,400,256]{2,1,0:T(8,128)(2,1)S(1)} %bitcast.22, bf16[2304,256]{1,0:T(8,128)(2,1)S(1)} %copy-done, f32[2,416,256]{2,1,0:T(8,128)S(1)} %get-tuple-element.77.pre), custom_call_target="tpu_custom_call" | custom-call | flops 654311424 | bytes 1000000 | tf_op jit(solution)/shard_map/inner/pallas_call | solution.py:555
  40.0 1.9 %scene.1 = bf16[2,400,256]{2,1,0:T(8,128)(2,1)} custom-call(bf16[6,416,256]{2,1,0:T(8,128)(2,1)S(1)} %splat.1.bev, bf16[4,416,256]{2,1,0:T(8,128)(2,1)S(1)} %get-tuple-element.76.hidden, bf16[2304,256]{1,0:T(8,128)(2,1)S(1)} %copy-done), custom_call_target="tpu_custom_call" | custom-call | flops 981467136 | bytes 1000000 | tf_op jit(solution)/shard_map/scene/pallas_call | solution.py:546
  41.9 0.6 collective-permute-done.8.one
  42.5 3.9 %collective-permute-done.9.two = bf16[8,72,128]{2,1,0:T(8,128)(2,1)S(1)} collective-permute-done((bf16[8,72,128]{2,1,0:T(8,128)(2,1)S(1)}, bf16[8,72,128]{2,1,0:T(8,128)(2,1)S(1)}, u32[]{:S(2)}, u32[]{:S(2)}) %collective-permute-start.9) | collective-permute-done | bytes 147488 | tf_op jit(solution)/shard_map/ppermute | solution.py:374
  46.5 0.8 %collective-permute-start.11 = (bf16[2,72,128]{2,1,0:T(8,128)(2,1)S(1)}, bf16[2,72,128]{2,1,0:T(8,128)(2,1)S(1)}, u32[]{:S(2)}, u32[]{:S(2)}) collective-permute-start(bf16[2,72,128]{2,1,0:T(8,128)(2,1)S(1)} %get-tuple-element.86), channel_id=1, source_target_pairs={{0,4},{1,5},{2,6},{3,7},{4,0},{5,1},{6,2},{7,3},{8,12},{9,13},{10,... | collective-permute-start | bytes 110600 | tf_op jit(solution)/shard_map/ppermute | solution.py:374
  47.3 1.3 %collective-permute-start.12 = (bf16[2,72,128]{2,1,0:T(8,128)(2,1)S(1)}, bf16[2,72,128]{2,1,0:T(8,128)(2,1)S(1)}, u32[]{:S(2)}, u32[]{:S(2)}) collective-permute-start(bf16[2,72,128]{2,1,0:T(8,128)(2,1)S(1)} %get-tuple-element.87), channel_id=1, source_target_pairs={{0,8},{1,9},{2,10},{3,11},{4,12},{5,13},{6,14},{7,15},{8,0},{9,1},... | collective-permute-start | bytes 110600 | tf_op jit(solution)/shard_map/ppermute | solution.py:374
  48.6 1.6 %collective-permute-start.13 = (bf16[2,72,128]{2,1,0:T(8,128)(2,1)S(1)}, bf16[2,72,128]{2,1,0:T(8,128)(2,1)S(1)}, u32[]{:S(2)}, u32[]{:S(2)}) collective-permute-start(bf16[2,72,128]{2,1,0:T(8,128)(2,1)S(1)} %get-tuple-element.88), channel_id=1, source_target_pairs={{0,12},{1,13},{2,14},{3,15},{4,8},{5,9},{6,10},{7,11},{8,4},{9,5},... | collective-permute-start | bytes 110600 | tf_op jit(solution)/shard_map/ppermute | solution.py:374
  50.1 0.9 %collective-permute-done.12 = bf16[2,72,128]{2,1,0:T(8,128)(2,1)S(1)} collective-permute-done((bf16[2,72,128]{2,1,0:T(8,128)(2,1)S(1)}, bf16[2,72,128]{2,1,0:T(8,128)(2,1)S(1)}, u32[]{:S(2)}, u32[]{:S(2)}) %collective-permute-start.12) | collective-permute-done | bytes 36896 | tf_op jit(solution)/shard_map/ppermute | solution.py:374
  51.0 2.2 %collective-permute-done.13 = bf16[2,72,128]{2,1,0:T(8,128)(2,1)S(1)} collective-permute-done((bf16[2,72,128]{2,1,0:T(8,128)(2,1)S(1)}, bf16[2,72,128]{2,1,0:T(8,128)(2,1)S(1)}, u32[]{:S(2)}, u32[]{:S(2)}) %collective-permute-start.13) | collective-permute-done | bytes 36896 | tf_op jit(solution)/shard_map/ppermute | solution.py:374
  53.2 3.9 %collective-permute-start.14 = (bf16[72,128]{1,0:T(8,128)(2,1)S(1)}, bf16[72,128]{1,0:T(8,128)(2,1)S(1)}, u32[]{:S(2)}, u32[]{:S(2)}) collective-permute-start(bf16[72,128]{1,0:T(8,128)(2,1)S(1)} %fusion.2), channel_id=1, source_target_pairs={{0,28},{1,29},{2,30},{3,31},{4,24},{5,25},{6,26},{7,27},{8,20},{9,... | collective-permute-start | bytes 55304 | tf_op jit(solution)/shard_map/ppermute | solution.py:374
  57.1 0.5 collective-permute-start.18
  57.7 1.1 %collective-permute-start.19 = (bf16[400,256]{1,0:T(8,128)(2,1)S(1)}, bf16[400,256]{1,0:T(8,128)(2,1)S(1)}, u32[]{:S(2)}, u32[]{:S(2)}) collective-permute-start(bf16[400,256]{1,0:T(8,128)(2,1)S(1)} %get-tuple-element.93), channel_id=1, source_target_pairs={{0,31},{1,2},{2,1},{3,4},{4,3},{5,6},{6,5},{7,8},{8,7},{9,10},{10,... | collective-permute-start | bytes 614408 | tf_op jit(solution)/shard_map/ppermute | solution.py:374
  58.8 1.3 %collective-permute-start.17 = (bf16[72,128]{1,0:T(8,128)(2,1)S(1)}, bf16[72,128]{1,0:T(8,128)(2,1)S(1)}, u32[]{:S(2)}, u32[]{:S(2)}) collective-permute-start(bf16[72,128]{1,0:T(8,128)(2,1)S(1)} %fusion.1), channel_id=1, source_target_pairs={{0,64},{32,96},{64,0},{96,32},{128,192},{160,224},{192,128},{224,1... | collective-permute-start | bytes 55304 | tf_op jit(solution)/shard_map/ppermute | solution.py:374
  60.1 2.5 %collective-permute-start.16 = (bf16[72,128]{1,0:T(8,128)(2,1)S(1)}, bf16[72,128]{1,0:T(8,128)(2,1)S(1)}, u32[]{:S(2)}, u32[]{:S(2)}) collective-permute-start(bf16[72,128]{1,0:T(8,128)(2,1)S(1)} %fusion.1), channel_id=1, source_target_pairs={{0,128},{32,160},{64,192},{96,224},{128,0},{160,32},{192,64},{224,... | collective-permute-start | bytes 55304 | tf_op jit(solution)/shard_map/ppermute | solution.py:374
  62.6 0.2 collective-permute-start.15
  62.7 1.5 %collective-permute-done.16 = bf16[72,128]{1,0:T(8,128)(2,1)S(1)} collective-permute-done((bf16[72,128]{1,0:T(8,128)(2,1)S(1)}, bf16[72,128]{1,0:T(8,128)(2,1)S(1)}, u32[]{:S(2)}, u32[]{:S(2)}) %collective-permute-start.16) | collective-permute-done | bytes 18464 | tf_op jit(solution)/shard_map/ppermute | solution.py:374
  64.2 2.2 %collective-permute-done.15 = bf16[72,128]{1,0:T(8,128)(2,1)S(1)} collective-permute-done((bf16[72,128]{1,0:T(8,128)(2,1)S(1)}, bf16[72,128]{1,0:T(8,128)(2,1)S(1)}, u32[]{:S(2)}, u32[]{:S(2)}) %collective-permute-start.15) | collective-permute-done | bytes 18464 | tf_op jit(solution)/shard_map/ppermute | solution.py:374
  66.4 4.4 %collective-permute-start.20 = (f32[72,128]{1,0:T(8,128)S(1)}, f32[72,128]{1,0:T(8,128)S(1)}, u32[]{:S(2)}, u32[]{:S(2)}) collective-permute-start(f32[72,128]{1,0:T(8,128)S(1)} %convert_add_fusion.1.ours), channel_id=1, source_target_pairs={{0,32},{32,0},{64,96},{96,64},{128,160},{160,128},{192,224},{224,1... | collective-permute-start | bytes 110600 | tf_op jit(solution)/shard_map/ppermute | solution.py:374
  70.8 1.3 %derivative.1 = bf16[2,400,256]{2,1,0:T(8,128)(2,1)} custom-call(bf16[400,256]{1,0:T(8,128)(2,1)S(1)} %collective-permute-done.18.first, bf16[400,256]{1,0:T(8,128)(2,1)S(1)} %collective-permute-done.19.second, f32[2,416,256]{2,1,0:T(8,128)S(1)} %get-tuple-element.99.back, bf16[2304,256]{1,0:T(8,128)(2,1)S(1)} %copy-done, ...), custom_call_target="tpu_custom_call" | custom-call | flops 327155712 | bytes 1000000 | tf_op jit(solution)/shard_map/derivative/pallas_call | solution.py:583
  72.1 0.6 gradient.1
  (22 shorter events, 0.3 us)
Async XLA Ops:
  2.1 7.8 %collective-permute-start = (bf16[64,256]{1,0:T(8,128)(2,1)S(1)}, bf16[64,256]{1,0:T(8,128)(2,1)S(1)}, u32[]{:S(2)}, u32[]{:S(2)}) collective-permute-start(bf16[64,256]{1,0:T(8,128)(2,1)S(1)} %pack.1.refs_0_), channel_id=1, source_target_pairs={{0,28},{1,29},{2,30},{3,31},{4,24},{5,25},{6,26},{7,27},{8,20},{9,... | collective-permute-start | bytes 98312 | tf_op jit(solution)/shard_map/ppermute | solution.py:374
  10.1 5.0 %collective-permute-start.1 = (bf16[80,256]{1,0:T(8,128)(2,1)S(1)}, bf16[80,256]{1,0:T(8,128)(2,1)S(1)}, u32[]{:S(2)}, u32[]{:S(2)}) collective-permute-start(bf16[80,256]{1,0:T(8,128)(2,1)S(1)} %get-tuple-element.54), channel_id=1, source_target_pairs={{0,12},{1,13},{2,14},{3,15},{4,8},{5,9},{6,10},{7,11},{8,4},{9,5},... | collective-permute-start | bytes 122888 | tf_op jit(solution)/shard_map/ppermute | solution.py:374
  11.8 3.8 %collective-permute-start.2 = (bf16[80,256]{1,0:T(8,128)(2,1)S(1)}, bf16[80,256]{1,0:T(8,128)(2,1)S(1)}, u32[]{:S(2)}, u32[]{:S(2)}) collective-permute-start(bf16[80,256]{1,0:T(8,128)(2,1)S(1)} %get-tuple-element.55), channel_id=1, source_target_pairs={{0,8},{1,9},{2,10},{3,11},{4,12},{5,13},{6,14},{7,15},{8,0},{9,1},... | collective-permute-start | bytes 122888 | tf_op jit(solution)/shard_map/ppermute | solution.py:374
  13.0 3.0 %collective-permute-start.3 = (bf16[80,256]{1,0:T(8,128)(2,1)S(1)}, bf16[80,256]{1,0:T(8,128)(2,1)S(1)}, u32[]{:S(2)}, u32[]{:S(2)}) collective-permute-start(bf16[80,256]{1,0:T(8,128)(2,1)S(1)} %get-tuple-element.56), channel_id=1, source_target_pairs={{0,4},{1,5},{2,6},{3,7},{4,0},{5,1},{6,2},{7,3},{8,12},{9,13},{10,... | collective-permute-start | bytes 122888 | tf_op jit(solution)/shard_map/ppermute | solution.py:374
  13.7 1.0 %copy-start.1 = (bf16[1,2,400,256]{3,2,1,0:T(8,128)(2,1)S(1)}, bf16[1,2,400,256]{3,2,1,0:T(8,128)(2,1)}, u32[]{:S(2)}) copy-start(bf16[1,2,400,256]{3,2,1,0:T(8,128)(2,1)} %param.13) | copy-start | bytes 1228804
  16.1 5.6 %collective-permute-start.6 = (bf16[288,256]{1,0:T(8,128)(2,1)S(1)}, bf16[288,256]{1,0:T(8,128)(2,1)S(1)}, u32[]{:S(2)}, u32[]{:S(2)}) collective-permute-start(bf16[288,256]{1,0:T(8,128)(2,1)S(1)} %get-tuple-element.65), channel_id=1, source_target_pairs={{0,2},{1,3},{2,0},{3,1},{4,6},{5,7},{6,4},{7,5},{8,10},{9,11},{10,... | collective-permute-start | bytes 442376 | tf_op jit(solution)/shard_map/ppermute | solution.py:374
  19.1 4.5 %collective-permute-start.5 = (bf16[288,256]{1,0:T(8,128)(2,1)S(1)}, bf16[288,256]{1,0:T(8,128)(2,1)S(1)}, u32[]{:S(2)}, u32[]{:S(2)}) collective-permute-start(bf16[288,256]{1,0:T(8,128)(2,1)S(1)} %get-tuple-element.64), channel_id=1, source_target_pairs={{0,1},{1,0},{2,3},{3,2},{4,5},{5,4},{6,7},{7,6},{8,9},{9,8},{10,11... | collective-permute-start | bytes 442376 | tf_op jit(solution)/shard_map/ppermute | solution.py:374
  19.5 6.8 %collective-permute-start.4 = (bf16[288,256]{1,0:T(8,128)(2,1)S(1)}, bf16[288,256]{1,0:T(8,128)(2,1)S(1)}, u32[]{:S(2)}, u32[]{:S(2)}) collective-permute-start(bf16[288,256]{1,0:T(8,128)(2,1)S(1)} %get-tuple-element.63), channel_id=1, source_target_pairs={{0,3},{1,2},{2,1},{3,0},{4,7},{5,6},{6,5},{7,4},{8,11},{9,10},{10,... | collective-permute-start | bytes 442376 | tf_op jit(solution)/shard_map/ppermute | solution.py:374
  24.7 2.8 %copy-start.3 = (bf16[2304,256]{1,0:T(8,128)(2,1)S(1)}, bf16[2304,256]{1,0:T(8,128)(2,1)}, u32[]{:S(2)}) copy-start(bf16[2304,256]{1,0:T(8,128)(2,1)} %weight.4) | copy-start | bytes 3538948
  30.6 5.1 %collective-permute-start.7 = (bf16[2304,128]{1,0:T(8,128)(2,1)S(1)}, bf16[2304,128]{1,0:T(8,128)(2,1)S(1)}, u32[]{:S(2)}, u32[]{:S(2)}) collective-permute-start(bf16[2304,128]{1,0:T(8,128)(2,1)S(1)} %get-tuple-element.70), channel_id=1, source_target_pairs={{0,32},{32,0},{64,96},{96,64},{128,160},{160,128},{192,224},{224,1... | collective-permute-start | bytes 1769480 | tf_op jit(solution)/shard_map/ppermute | solution.py:374
  35.1 3.8 %copy-start = (bf16[2304,256]{1,0:T(8,128)(2,1)S(1)}, bf16[2304,256]{1,0:T(8,128)(2,1)}, u32[]{:S(2)}) copy-start(bf16[2304,256]{1,0:T(8,128)(2,1)} %weight.7) | copy-start | bytes 3538948
  35.1 3.8 %copy-start.2 = (bf16[1,2,400,256]{3,2,1,0:T(8,128)(2,1)S(1)}, bf16[1,2,400,256]{3,2,1,0:T(8,128)(2,1)}, u32[]{:S(2)}) copy-start(bf16[1,2,400,256]{3,2,1,0:T(8,128)(2,1)} %param.13) | copy-start | bytes 1228804
  35.9 6.7 %collective-permute-start.8 = (bf16[8,72,128]{2,1,0:T(8,128)(2,1)S(1)}, bf16[8,72,128]{2,1,0:T(8,128)(2,1)S(1)}, u32[]{:S(2)}, u32[]{:S(2)}) collective-permute-start(bf16[8,72,128]{2,1,0:T(8,128)(2,1)S(1)} %get-tuple-element.73), channel_id=1, source_target_pairs={{0,2},{1,3},{2,0},{3,1},{4,6},{5,7},{6,4},{7,5},{8,10},{9,11},{10,... | collective-permute-start | bytes 442376 | tf_op jit(solution)/shard_map/ppermute | solution.py:374
  37.6 8.8 %collective-permute-start.9 = (bf16[8,72,128]{2,1,0:T(8,128)(2,1)S(1)}, bf16[8,72,128]{2,1,0:T(8,128)(2,1)S(1)}, u32[]{:S(2)}, u32[]{:S(2)}) collective-permute-start(bf16[8,72,128]{2,1,0:T(8,128)(2,1)S(1)} %get-tuple-element.74), channel_id=1, source_target_pairs={{0,3},{1,2},{2,1},{3,0},{4,7},{5,6},{6,5},{7,4},{8,11},{9,10},{10,... | collective-permute-start | bytes 442376 | tf_op jit(solution)/shard_map/ppermute | solution.py:374
  38.9 7.5 %collective-permute-start.10 = (bf16[8,72,128]{2,1,0:T(8,128)(2,1)S(1)}, bf16[8,72,128]{2,1,0:T(8,128)(2,1)S(1)}, u32[]{:S(2)}, u32[]{:S(2)}) collective-permute-start(bf16[8,72,128]{2,1,0:T(8,128)(2,1)S(1)} %get-tuple-element.75), channel_id=1, source_target_pairs={{0,1},{1,0},{2,3},{3,2},{4,5},{5,4},{6,7},{7,6},{8,9},{9,8},{10,11... | collective-permute-start | bytes 442376 | tf_op jit(solution)/shard_map/ppermute | solution.py:374
  46.5 3.6 %collective-permute-start.11 = (bf16[2,72,128]{2,1,0:T(8,128)(2,1)S(1)}, bf16[2,72,128]{2,1,0:T(8,128)(2,1)S(1)}, u32[]{:S(2)}, u32[]{:S(2)}) collective-permute-start(bf16[2,72,128]{2,1,0:T(8,128)(2,1)S(1)} %get-tuple-element.86), channel_id=1, source_target_pairs={{0,4},{1,5},{2,6},{3,7},{4,0},{5,1},{6,2},{7,3},{8,12},{9,13},{10,... | collective-permute-start | bytes 110600 | tf_op jit(solution)/shard_map/ppermute | solution.py:374
  47.3 3.7 %collective-permute-start.12 = (bf16[2,72,128]{2,1,0:T(8,128)(2,1)S(1)}, bf16[2,72,128]{2,1,0:T(8,128)(2,1)S(1)}, u32[]{:S(2)}, u32[]{:S(2)}) collective-permute-start(bf16[2,72,128]{2,1,0:T(8,128)(2,1)S(1)} %get-tuple-element.87), channel_id=1, source_target_pairs={{0,8},{1,9},{2,10},{3,11},{4,12},{5,13},{6,14},{7,15},{8,0},{9,1},... | collective-permute-start | bytes 110600 | tf_op jit(solution)/shard_map/ppermute | solution.py:374
  48.6 4.6 %collective-permute-start.13 = (bf16[2,72,128]{2,1,0:T(8,128)(2,1)S(1)}, bf16[2,72,128]{2,1,0:T(8,128)(2,1)S(1)}, u32[]{:S(2)}, u32[]{:S(2)}) collective-permute-start(bf16[2,72,128]{2,1,0:T(8,128)(2,1)S(1)} %get-tuple-element.88), channel_id=1, source_target_pairs={{0,12},{1,13},{2,14},{3,15},{4,8},{5,9},{6,10},{7,11},{8,4},{9,5},... | collective-permute-start | bytes 110600 | tf_op jit(solution)/shard_map/ppermute | solution.py:374
  53.2 5.6 %collective-permute-start.14 = (bf16[72,128]{1,0:T(8,128)(2,1)S(1)}, bf16[72,128]{1,0:T(8,128)(2,1)S(1)}, u32[]{:S(2)}, u32[]{:S(2)}) collective-permute-start(bf16[72,128]{1,0:T(8,128)(2,1)S(1)} %fusion.2), channel_id=1, source_target_pairs={{0,28},{1,29},{2,30},{3,31},{4,24},{5,25},{6,26},{7,27},{8,20},{9,... | collective-permute-start | bytes 55304 | tf_op jit(solution)/shard_map/ppermute | solution.py:374
  57.1 9.2 %collective-permute-start.18 = (bf16[400,256]{1,0:T(8,128)(2,1)S(1)}, bf16[400,256]{1,0:T(8,128)(2,1)S(1)}, u32[]{:S(2)}, u32[]{:S(2)}) collective-permute-start(bf16[400,256]{1,0:T(8,128)(2,1)S(1)} %get-tuple-element.92), channel_id=1, source_target_pairs={{0,1},{1,0},{2,3},{3,2},{4,5},{5,4},{6,7},{7,6},{8,9},{9,8},{10,11... | collective-permute-start | bytes 614408 | tf_op jit(solution)/shard_map/ppermute | solution.py:374
  57.7 8.7 %collective-permute-start.19 = (bf16[400,256]{1,0:T(8,128)(2,1)S(1)}, bf16[400,256]{1,0:T(8,128)(2,1)S(1)}, u32[]{:S(2)}, u32[]{:S(2)}) collective-permute-start(bf16[400,256]{1,0:T(8,128)(2,1)S(1)} %get-tuple-element.93), channel_id=1, source_target_pairs={{0,31},{1,2},{2,1},{3,4},{4,3},{5,6},{6,5},{7,8},{8,7},{9,10},{10,... | collective-permute-start | bytes 614408 | tf_op jit(solution)/shard_map/ppermute | solution.py:374
  58.8 3.9 %collective-permute-start.17 = (bf16[72,128]{1,0:T(8,128)(2,1)S(1)}, bf16[72,128]{1,0:T(8,128)(2,1)S(1)}, u32[]{:S(2)}, u32[]{:S(2)}) collective-permute-start(bf16[72,128]{1,0:T(8,128)(2,1)S(1)} %fusion.1), channel_id=1, source_target_pairs={{0,64},{32,96},{64,0},{96,32},{128,192},{160,224},{192,128},{224,1... | collective-permute-start | bytes 55304 | tf_op jit(solution)/shard_map/ppermute | solution.py:374
  60.1 4.1 %collective-permute-start.16 = (bf16[72,128]{1,0:T(8,128)(2,1)S(1)}, bf16[72,128]{1,0:T(8,128)(2,1)S(1)}, u32[]{:S(2)}, u32[]{:S(2)}) collective-permute-start(bf16[72,128]{1,0:T(8,128)(2,1)S(1)} %fusion.1), channel_id=1, source_target_pairs={{0,128},{32,160},{64,192},{96,224},{128,0},{160,32},{192,64},{224,... | collective-permute-start | bytes 55304 | tf_op jit(solution)/shard_map/ppermute | solution.py:374
  62.6 3.8 %collective-permute-start.15 = (bf16[72,128]{1,0:T(8,128)(2,1)S(1)}, bf16[72,128]{1,0:T(8,128)(2,1)S(1)}, u32[]{:S(2)}, u32[]{:S(2)}) collective-permute-start(bf16[72,128]{1,0:T(8,128)(2,1)S(1)} %fusion.1), channel_id=1, source_target_pairs={{0,192},{32,224},{64,128},{96,160},{128,64},{160,96},{192,0},{224,... | collective-permute-start | bytes 55304 | tf_op jit(solution)/shard_map/ppermute | solution.py:374
  66.4 5.7 %collective-permute-start.20 = (f32[72,128]{1,0:T(8,128)S(1)}, f32[72,128]{1,0:T(8,128)S(1)}, u32[]{:S(2)}, u32[]{:S(2)}) collective-permute-start(f32[72,128]{1,0:T(8,128)S(1)} %convert_add_fusion.1.ours), channel_id=1, source_target_pairs={{0,32},{32,0},{64,96},{96,64},{128,160},{160,128},{192,224},{224,1... | collective-permute-start | bytes 110600 | tf_op jit(solution)/shard_map/ppermute | solution.py:374

commit v9 on v7

--- a/solution.py
+++ b/solution.py
@@ -48,7 +48,7 @@
     ]
     for copy in copies:
         copy.start()
-    for copy in copies:
+    for copy in copies[:-1]:
         copy.wait()
     pixels, bins = scores.shape
     strips, slots = points.shape
@@ -80,6 +80,7 @@
     weights = jnp.where(low, coarse, pltpu.roll(weight - coarse, slots, 1))
     codes = jnp.where(low, upper, pltpu.roll(under, slots, 1))
     packed[pixels:] = jnp.concatenate([weights, codes], axis=1).astype(BF16)
+    copies[-1].wait()
 
 
 def line_kernel(*refs):

time: 70.8 us -> 70.7 us (level)
  no operation moved by 1% of the time
where the time goes in v9:
time: 70.7 us; the launch traced here: 70.4 us
  starting transfers between devices  36.1 us (51%)
  waiting for transfers between devices  16.6 us (23%)
  Pallas kernels  15.8 us (22%)
  local copies, waits for them, and re-layouts  1.02 us (1%)
  between operations  0.8 us (1%)
    ppermute x21, starting transfers between devices, swap(): lax.ppermute(values, axis, [(i, partner(i)) for i in range(lax.axis_size(...  36.1 us
    ppermute x21, waiting for transfers between devices, swap(): lax.ppermute(values, axis, [(i, partner(i)) for i in range(lax.axis_size(...  16.6 us
    pallas_call x1, Pallas kernels, on_device(): pl.pallas_call(functools.partial(hidden_kernel, breadth), out_shape=(held...  3.05 us
    pallas_call x2, Pallas kernels, on_device(): pl.pallas_call(more_kernel, out_shape=held((6, breadth, planes), F32), in...  2.2 us
    pallas_call x1, Pallas kernels, on_device(): pl.pallas_call(functools.partial(scene_kernel, breadth), out_shape=struct...  1.92 us
    pallas_call x1, Pallas kernels, on_device(): pl.pallas_call(pack_kernel, out_shape=held((places, planes), BF16), in_sp...  1.49 us
    pallas_call x1, Pallas kernels, on_device(): pl.pallas_call(functools.partial(derivative_kernel, breadth), out_shape=s...  1.42 us
  transfers between devices with their start and end apart: 21, of which 14 were waited for; matrix products, arithmetic and copies ran while one was open for 0% of the time, Pallas kernels for 13%

profile of v9, /device:TPU:1, one launch (start us, length us, event | category | flops | bytes accessed | tf_op | source)
XLA Modules:
  0.0 70.4 jit_solution(8827881731726084546)
XLA Ops:
  0.6 1.5 %pack.1.refs_0_ = bf16[64,256]{1,0:T(8,128)(2,1)S(1)} custom-call(bf16[32,256]{1,0:T(8,128)(2,1)} %bitcast.26, bf16[32,64]{1,0:T(8,128)(2,1)} %bitcast.29, s32[32,64]{1,0:T(8,128)} %bitcast.27, s32[32,64]{1,0:T(8,128)} %bitcast.28, s32[1,32]{1,0:T(1,128)} %bitcast.30), custom_call_target="tpu_custom_call" | custom-call | tf_op jit(solution)/shard_map/pack/pallas_call | solution.py:410
  2.1 6.5 %collective-permute-start = (bf16[64,256]{1,0:T(8,128)(2,1)S(1)}, bf16[64,256]{1,0:T(8,128)(2,1)S(1)}, u32[]{:S(2)}, u32[]{:S(2)}) collective-permute-start(bf16[64,256]{1,0:T(8,128)(2,1)S(1)} %pack.1.refs_0_), channel_id=1, source_target_pairs={{0,28},{1,29},{2,30},{3,31},{4,24},{5,25},{6,26},{7,27},{8,20},{9,... | collective-permute-start | bytes 98312 | tf_op jit(solution)/shard_map/ppermute | solution.py:373
  8.6 1.3 %collective-permute-done.refs_1_ = bf16[64,256]{1,0:T(8,128)(2,1)S(1)} collective-permute-done((bf16[64,256]{1,0:T(8,128)(2,1)S(1)}, bf16[64,256]{1,0:T(8,128)(2,1)S(1)}, u32[]{:S(2)}, u32[]{:S(2)}) %collective-permute-start) | collective-permute-done | bytes 32800 | tf_op jit(solution)/shard_map/ppermute | solution.py:373
  9.9 0.2 line.1
  10.1 1.7 %collective-permute-start.1 = (bf16[80,256]{1,0:T(8,128)(2,1)S(1)}, bf16[80,256]{1,0:T(8,128)(2,1)S(1)}, u32[]{:S(2)}, u32[]{:S(2)}) collective-permute-start(bf16[80,256]{1,0:T(8,128)(2,1)S(1)} %get-tuple-element.51), channel_id=1, source_target_pairs={{0,12},{1,13},{2,14},{3,15},{4,8},{5,9},{6,10},{7,11},{8,4},{9,5},... | collective-permute-start | bytes 122888 | tf_op jit(solution)/shard_map/ppermute | solution.py:373
  11.8 1.2 %collective-permute-start.2 = (bf16[80,256]{1,0:T(8,128)(2,1)S(1)}, bf16[80,256]{1,0:T(8,128)(2,1)S(1)}, u32[]{:S(2)}, u32[]{:S(2)}) collective-permute-start(bf16[80,256]{1,0:T(8,128)(2,1)S(1)} %get-tuple-element.52), channel_id=1, source_target_pairs={{0,8},{1,9},{2,10},{3,11},{4,12},{5,13},{6,14},{7,15},{8,0},{9,1},... | collective-permute-start | bytes 122888 | tf_op jit(solution)/shard_map/ppermute | solution.py:373
  13.0 0.7 %collective-permute-start.3 = (bf16[80,256]{1,0:T(8,128)(2,1)S(1)}, bf16[80,256]{1,0:T(8,128)(2,1)S(1)}, u32[]{:S(2)}, u32[]{:S(2)}) collective-permute-start(bf16[80,256]{1,0:T(8,128)(2,1)S(1)} %get-tuple-element.53), channel_id=1, source_target_pairs={{0,4},{1,5},{2,6},{3,7},{4,0},{5,1},{6,2},{7,3},{8,12},{9,13},{10,... | collective-permute-start | bytes 122888 | tf_op jit(solution)/shard_map/ppermute | solution.py:373
  13.7 1.0 %copy-done.1 = bf16[1,2,400,256]{3,2,1,0:T(8,128)(2,1)S(1)} copy-done((bf16[1,2,400,256]{3,2,1,0:T(8,128)(2,1)S(1)}, bf16[1,2,400,256]{3,2,1,0:T(8,128)(2,1)}, u32[]{:S(2)}) %copy-start.1) | copy-done | bytes 409624
  14.7 0.4 moved.1
  15.1 0.4 collective-permute-done.2.refs_2_
  15.6 0.4 collective-permute-done.3.refs_3_
  16.1 3.0 %collective-permute-start.6 = (bf16[288,256]{1,0:T(8,128)(2,1)S(1)}, bf16[288,256]{1,0:T(8,128)(2,1)S(1)}, u32[]{:S(2)}, u32[]{:S(2)}) collective-permute-start(bf16[288,256]{1,0:T(8,128)(2,1)S(1)} %get-tuple-element.62), channel_id=1, source_target_pairs={{0,2},{1,3},{2,0},{3,1},{4,6},{5,7},{6,4},{7,5},{8,10},{9,11},{10,... | collective-permute-start | bytes 442376 | tf_op jit(solution)/shard_map/ppermute | solution.py:373
  19.1 0.4 collective-permute-start.5
  19.5 0.4 collective-permute-start.4
  19.9 1.1 %plane.1.before = f32[6,400,256]{2,1,0:T(8,128)S(1)} custom-call(bf16[288,256]{1,0:T(8,128)(2,1)S(1)} %get-tuple-element.63.message), custom_call_target="tpu_custom_call" | custom-call | flops 629145600 | bytes 1000000 | tf_op jit(solution)/shard_map/plane/pallas_call | solution.py:471
  21.0 0.7 collective-permute-done.6.message
  21.7 1.1 %more.1.before = f32[6,400,256]{2,1,0:T(8,128)S(1)} custom-call(bf16[288,256]{1,0:T(8,128)(2,1)S(1)} %collective-permute-done.6.message, f32[6,400,256]{2,1,0:T(8,128)S(1)} %plane.1.before), custom_call_target="tpu_custom_call" | custom-call | flops 629145600 | bytes 1000000 | tf_op jit(solution)/shard_map/more/pallas_call | solution.py:481
  22.8 0.8 %collective-permute-done.5.message = bf16[288,256]{1,0:T(8,128)(2,1)S(1)} collective-permute-done((bf16[288,256]{1,0:T(8,128)(2,1)S(1)}, bf16[288,256]{1,0:T(8,128)(2,1)S(1)}, u32[]{:S(2)}, u32[]{:S(2)}) %collective-permute-start.5) | collective-permute-done | bytes 147488 | tf_op jit(solution)/shard_map/ppermute | solution.py:373
  23.6 1.1 %again.1.before = f32[6,400,256]{2,1,0:T(8,128)S(1)} custom-call(bf16[288,256]{1,0:T(8,128)(2,1)S(1)} %collective-permute-done.5.message, f32[6,400,256]{2,1,0:T(8,128)S(1)} %more.1.before), custom_call_target="tpu_custom_call" | custom-call | flops 629145600 | bytes 1000000 | tf_op jit(solution)/shard_map/again/pallas_call | solution.py:491
  24.7 1.6 %collective-permute-done.4.message = bf16[288,256]{1,0:T(8,128)(2,1)S(1)} collective-permute-done((bf16[288,256]{1,0:T(8,128)(2,1)S(1)}, bf16[288,256]{1,0:T(8,128)(2,1)S(1)}, u32[]{:S(2)}, u32[]{:S(2)}) %collective-permute-start.4) | collective-permute-done | bytes 147488 | tf_op jit(solution)/shard_map/ppermute | solution.py:373
  26.3 1.3 %splat.1.bev = bf16[6,416,256]{2,1,0:T(8,128)(2,1)S(1)} custom-call(bf16[288,256]{1,0:T(8,128)(2,1)S(1)} %collective-permute-done.4.message, f32[6,400,256]{2,1,0:T(8,128)S(1)} %again.1.before), custom_call_target="tpu_custom_call" | custom-call | tf_op jit(solution)/shard_map/splat/pallas_call | solution.py:501
  27.5 3.0 %hidden.1 = (f32[2,416,256]{2,1,0:T(8,128)S(1)}, bf16[4,416,256]{2,1,0:T(8,128)(2,1)S(1)}, bf16[4,256,416]{2,1,0:T(8,128)(2,1)S(1)}, bf16[2304,128]{1,0:T(8,128)(2,1)S(1)}) custom-call(bf16[6,416,256]{2,1,0:T(8,128)(2,1)S(1)} %splat.1.bev, bf16[2304,256]{1,0:T(8,128)(2,1)S(1)} %copy-done.3, bf16[2,416,384]{2,1,0:T(8,128)(2,1)S(1)} %get-tuple-element.64.cotangent), custom_call_target="tpu_custom_call" | custom-call | tf_op jit(solution)/shard_map/hidden/pallas_call | solution.py:510
  30.6 3.5 %collective-permute-start.7 = (bf16[2304,128]{1,0:T(8,128)(2,1)S(1)}, bf16[2304,128]{1,0:T(8,128)(2,1)S(1)}, u32[]{:S(2)}, u32[]{:S(2)}) collective-permute-start(bf16[2304,128]{1,0:T(8,128)(2,1)S(1)} %get-tuple-element.67), channel_id=1, source_target_pairs={{0,32},{32,0},{64,96},{96,64},{128,160},{160,128},{192,224},{224,1... | collective-permute-start | bytes 1769480 | tf_op jit(solution)/shard_map/ppermute | solution.py:373
  34.1 1.0 %kept.1 = f32[2304,128]{1,0:T(8,128)S(1)} custom-call(bf16[4,256,416]{2,1,0:T(8,128)(2,1)S(1)} %get-tuple-element.65.columns, bf16[2,416,384]{2,1,0:T(8,128)(2,1)S(1)} %get-tuple-element.66.cotangent), custom_call_target="tpu_custom_call" | custom-call | flops 490733568 | bytes 1000000 | tf_op jit(solution)/shard_map/kept/pallas_call | solution.py:524
  35.1 0.6 collective-permute-done.7
  35.9 1.7 %collective-permute-start.8 = (bf16[8,72,128]{2,1,0:T(8,128)(2,1)S(1)}, bf16[8,72,128]{2,1,0:T(8,128)(2,1)S(1)}, u32[]{:S(2)}, u32[]{:S(2)}) collective-permute-start(bf16[8,72,128]{2,1,0:T(8,128)(2,1)S(1)} %get-tuple-element.70), channel_id=1, source_target_pairs={{0,2},{1,3},{2,0},{3,1},{4,6},{5,7},{6,4},{7,5},{8,10},{9,11},{10,... | collective-permute-start | bytes 442376 | tf_op jit(solution)/shard_map/ppermute | solution.py:373
  37.6 1.3 %collective-permute-start.9 = (bf16[8,72,128]{2,1,0:T(8,128)(2,1)S(1)}, bf16[8,72,128]{2,1,0:T(8,128)(2,1)S(1)}, u32[]{:S(2)}, u32[]{:S(2)}) collective-permute-start(bf16[8,72,128]{2,1,0:T(8,128)(2,1)S(1)} %get-tuple-element.71), channel_id=1, source_target_pairs={{0,3},{1,2},{2,1},{3,0},{4,7},{5,6},{6,5},{7,4},{8,11},{9,10},{10,... | collective-permute-start | bytes 442376 | tf_op jit(solution)/shard_map/ppermute | solution.py:373
  38.9 0.9 %inner.1.back = f32[2,416,256]{2,1,0:T(8,128)S(1)} custom-call(bf16[2,400,256]{2,1,0:T(8,128)(2,1)S(1)} %bitcast.22, bf16[2304,256]{1,0:T(8,128)(2,1)S(1)} %copy-done), custom_call_target="tpu_custom_call" | custom-call | flops 654311424 | bytes 1000000 | tf_op jit(solution)/shard_map/inner/pallas_call | solution.py:554
  39.8 1.9 %scene.1 = bf16[2,400,256]{2,1,0:T(8,128)(2,1)} custom-call(bf16[6,416,256]{2,1,0:T(8,128)(2,1)S(1)} %splat.1.bev, bf16[4,416,256]{2,1,0:T(8,128)(2,1)S(1)} %get-tuple-element.73.hidden, bf16[2304,256]{1,0:T(8,128)(2,1)S(1)} %copy-done), custom_call_target="tpu_custom_call" | custom-call | flops 981467136 | bytes 1000000 | tf_op jit(solution)/shard_map/scene/pallas_call | solution.py:545
  41.7 0.8 %collective-permute-done.8.one = bf16[8,72,128]{2,1,0:T(8,128)(2,1)S(1)} collective-permute-done((bf16[8,72,128]{2,1,0:T(8,128)(2,1)S(1)}, bf16[8,72,128]{2,1,0:T(8,128)(2,1)S(1)}, u32[]{:S(2)}, u32[]{:S(2)}) %collective-permute-start.8) | collective-permute-done | bytes 147488 | tf_op jit(solution)/shard_map/ppermute | solution.py:373
  42.5 3.9 %collective-permute-done.9.two = bf16[8,72,128]{2,1,0:T(8,128)(2,1)S(1)} collective-permute-done((bf16[8,72,128]{2,1,0:T(8,128)(2,1)S(1)}, bf16[8,72,128]{2,1,0:T(8,128)(2,1)S(1)}, u32[]{:S(2)}, u32[]{:S(2)}) %collective-permute-start.9) | collective-permute-done | bytes 147488 | tf_op jit(solution)/shard_map/ppermute | solution.py:373
  46.5 1.8 %collective-permute-start.13 = (bf16[2,72,128]{2,1,0:T(8,128)(2,1)S(1)}, bf16[2,72,128]{2,1,0:T(8,128)(2,1)S(1)}, u32[]{:S(2)}, u32[]{:S(2)}) collective-permute-start(bf16[2,72,128]{2,1,0:T(8,128)(2,1)S(1)} %get-tuple-element.82), channel_id=1, source_target_pairs={{0,12},{1,13},{2,14},{3,15},{4,8},{5,9},{6,10},{7,11},{8,4},{9,5},... | collective-permute-start | bytes 110600 | tf_op jit(solution)/shard_map/ppermute | solution.py:373
  48.3 0.2 collective-permute-start.12
  48.5 1.6 %collective-permute-start.11 = (bf16[2,72,128]{2,1,0:T(8,128)(2,1)S(1)}, bf16[2,72,128]{2,1,0:T(8,128)(2,1)S(1)}, u32[]{:S(2)}, u32[]{:S(2)}) collective-permute-start(bf16[2,72,128]{2,1,0:T(8,128)(2,1)S(1)} %get-tuple-element.80), channel_id=1, source_target_pairs={{0,4},{1,5},{2,6},{3,7},{4,0},{5,1},{6,2},{7,3},{8,12},{9,13},{10,... | collective-permute-start | bytes 110600 | tf_op jit(solution)/shard_map/ppermute | solution.py:373
  50.1 1.1 %collective-permute-done.13 = bf16[2,72,128]{2,1,0:T(8,128)(2,1)S(1)} collective-permute-done((bf16[2,72,128]{2,1,0:T(8,128)(2,1)S(1)}, bf16[2,72,128]{2,1,0:T(8,128)(2,1)S(1)}, u32[]{:S(2)}, u32[]{:S(2)}) %collective-permute-start.13) | collective-permute-done | bytes 36896 | tf_op jit(solution)/shard_map/ppermute | solution.py:373
  51.2 1.2 %collective-permute-done.12 = bf16[2,72,128]{2,1,0:T(8,128)(2,1)S(1)} collective-permute-done((bf16[2,72,128]{2,1,0:T(8,128)(2,1)S(1)}, bf16[2,72,128]{2,1,0:T(8,128)(2,1)S(1)}, u32[]{:S(2)}, u32[]{:S(2)}) %collective-permute-start.12) | collective-permute-done | bytes 36896 | tf_op jit(solution)/shard_map/ppermute | solution.py:373
  52.5 4.3 %collective-permute-start.14 = (bf16[72,128]{1,0:T(8,128)(2,1)S(1)}, bf16[72,128]{1,0:T(8,128)(2,1)S(1)}, u32[]{:S(2)}, u32[]{:S(2)}) collective-permute-start(bf16[72,128]{1,0:T(8,128)(2,1)S(1)} %fusion.2), channel_id=1, source_target_pairs={{0,28},{1,29},{2,30},{3,31},{4,24},{5,25},{6,26},{7,27},{8,20},{9,... | collective-permute-start | bytes 55304 | tf_op jit(solution)/shard_map/ppermute | solution.py:373
  56.7 0.6 collective-permute-start.18
  57.3 0.8 %collective-permute-start.19 = (bf16[400,256]{1,0:T(8,128)(2,1)S(1)}, bf16[400,256]{1,0:T(8,128)(2,1)S(1)}, u32[]{:S(2)}, u32[]{:S(2)}) collective-permute-start(bf16[400,256]{1,0:T(8,128)(2,1)S(1)} %get-tuple-element.87), channel_id=1, source_target_pairs={{0,31},{1,2},{2,1},{3,4},{4,3},{5,6},{6,5},{7,8},{8,7},{9,10},{10,... | collective-permute-start | bytes 614408 | tf_op jit(solution)/shard_map/ppermute | solution.py:373
  58.2 2.6 %collective-permute-start.15 = (bf16[72,128]{1,0:T(8,128)(2,1)S(1)}, bf16[72,128]{1,0:T(8,128)(2,1)S(1)}, u32[]{:S(2)}, u32[]{:S(2)}) collective-permute-start(bf16[72,128]{1,0:T(8,128)(2,1)S(1)} %fusion.1), channel_id=1, source_target_pairs={{0,192},{32,224},{64,128},{96,160},{128,64},{160,96},{192,0},{224,... | collective-permute-start | bytes 55304 | tf_op jit(solution)/shard_map/ppermute | solution.py:373
  60.7 0.5 collective-permute-start.16
  61.3 0.3 collective-permute-start.17
  61.5 0.6 collective-permute-done.15
  62.1 2.8 %collective-permute-done.16 = bf16[72,128]{1,0:T(8,128)(2,1)S(1)} collective-permute-done((bf16[72,128]{1,0:T(8,128)(2,1)S(1)}, bf16[72,128]{1,0:T(8,128)(2,1)S(1)}, u32[]{:S(2)}, u32[]{:S(2)}) %collective-permute-start.16) | collective-permute-done | bytes 18464 | tf_op jit(solution)/shard_map/ppermute | solution.py:373
  64.8 0.4 collective-permute-done.19.second
  65.3 3.0 %collective-permute-start.20 = (f32[72,128]{1,0:T(8,128)S(1)}, f32[72,128]{1,0:T(8,128)S(1)}, u32[]{:S(2)}, u32[]{:S(2)}) collective-permute-start(f32[72,128]{1,0:T(8,128)S(1)} %convert_add_fusion.1.ours), channel_id=1, source_target_pairs={{0,32},{32,0},{64,96},{96,64},{128,160},{160,128},{192,224},{224,1... | collective-permute-start | bytes 110600 | tf_op jit(solution)/shard_map/ppermute | solution.py:373
  68.3 1.4 %derivative.1 = bf16[2,400,256]{2,1,0:T(8,128)(2,1)} custom-call(bf16[400,256]{1,0:T(8,128)(2,1)S(1)} %collective-permute-done.18.first, bf16[400,256]{1,0:T(8,128)(2,1)S(1)} %collective-permute-done.19.second, f32[2,416,256]{2,1,0:T(8,128)S(1)} %inner.1.back, bf16[2304,256]{1,0:T(8,128)(2,1)S(1)} %copy-done, f32[2,416,256]{2,1,0:T(8,128)S(1)} %get-tuple-element.94.pre), custom_call_target="tpu_custom_call" | custom-call | flops 327155712 | bytes 1000000 | tf_op jit(solution)/shard_map/derivative/pallas_call | solution.py:582
  69.7 0.6 gradient.1
  (22 shorter events, 0.4 us)
Async XLA Ops:
  2.1 7.8 %collective-permute-start = (bf16[64,256]{1,0:T(8,128)(2,1)S(1)}, bf16[64,256]{1,0:T(8,128)(2,1)S(1)}, u32[]{:S(2)}, u32[]{:S(2)}) collective-permute-start(bf16[64,256]{1,0:T(8,128)(2,1)S(1)} %pack.1.refs_0_), channel_id=1, source_target_pairs={{0,28},{1,29},{2,30},{3,31},{4,24},{5,25},{6,26},{7,27},{8,20},{9,... | collective-permute-start | bytes 98312 | tf_op jit(solution)/shard_map/ppermute | solution.py:373
  10.1 5.0 %collective-permute-start.1 = (bf16[80,256]{1,0:T(8,128)(2,1)S(1)}, bf16[80,256]{1,0:T(8,128)(2,1)S(1)}, u32[]{:S(2)}, u32[]{:S(2)}) collective-permute-start(bf16[80,256]{1,0:T(8,128)(2,1)S(1)} %get-tuple-element.51), channel_id=1, source_target_pairs={{0,12},{1,13},{2,14},{3,15},{4,8},{5,9},{6,10},{7,11},{8,4},{9,5},... | collective-permute-start | bytes 122888 | tf_op jit(solution)/shard_map/ppermute | solution.py:373
  11.8 3.8 %collective-permute-start.2 = (bf16[80,256]{1,0:T(8,128)(2,1)S(1)}, bf16[80,256]{1,0:T(8,128)(2,1)S(1)}, u32[]{:S(2)}, u32[]{:S(2)}) collective-permute-start(bf16[80,256]{1,0:T(8,128)(2,1)S(1)} %get-tuple-element.52), channel_id=1, source_target_pairs={{0,8},{1,9},{2,10},{3,11},{4,12},{5,13},{6,14},{7,15},{8,0},{9,1},... | collective-permute-start | bytes 122888 | tf_op jit(solution)/shard_map/ppermute | solution.py:373
  13.0 3.0 %collective-permute-start.3 = (bf16[80,256]{1,0:T(8,128)(2,1)S(1)}, bf16[80,256]{1,0:T(8,128)(2,1)S(1)}, u32[]{:S(2)}, u32[]{:S(2)}) collective-permute-start(bf16[80,256]{1,0:T(8,128)(2,1)S(1)} %get-tuple-element.53), channel_id=1, source_target_pairs={{0,4},{1,5},{2,6},{3,7},{4,0},{5,1},{6,2},{7,3},{8,12},{9,13},{10,... | collective-permute-start | bytes 122888 | tf_op jit(solution)/shard_map/ppermute | solution.py:373
  13.7 1.0 %copy-start.1 = (bf16[1,2,400,256]{3,2,1,0:T(8,128)(2,1)S(1)}, bf16[1,2,400,256]{3,2,1,0:T(8,128)(2,1)}, u32[]{:S(2)}) copy-start(bf16[1,2,400,256]{3,2,1,0:T(8,128)(2,1)} %param.13) | copy-start | bytes 1228804
  16.1 5.6 %collective-permute-start.6 = (bf16[288,256]{1,0:T(8,128)(2,1)S(1)}, bf16[288,256]{1,0:T(8,128)(2,1)S(1)}, u32[]{:S(2)}, u32[]{:S(2)}) collective-permute-start(bf16[288,256]{1,0:T(8,128)(2,1)S(1)} %get-tuple-element.62), channel_id=1, source_target_pairs={{0,2},{1,3},{2,0},{3,1},{4,6},{5,7},{6,4},{7,5},{8,10},{9,11},{10,... | collective-permute-start | bytes 442376 | tf_op jit(solution)/shard_map/ppermute | solution.py:373
  19.1 4.5 %collective-permute-start.5 = (bf16[288,256]{1,0:T(8,128)(2,1)S(1)}, bf16[288,256]{1,0:T(8,128)(2,1)S(1)}, u32[]{:S(2)}, u32[]{:S(2)}) collective-permute-start(bf16[288,256]{1,0:T(8,128)(2,1)S(1)} %get-tuple-element.61), channel_id=1, source_target_pairs={{0,1},{1,0},{2,3},{3,2},{4,5},{5,4},{6,7},{7,6},{8,9},{9,8},{10,11... | collective-permute-start | bytes 442376 | tf_op jit(solution)/shard_map/ppermute | solution.py:373
  19.5 6.8 %collective-permute-start.4 = (bf16[288,256]{1,0:T(8,128)(2,1)S(1)}, bf16[288,256]{1,0:T(8,128)(2,1)S(1)}, u32[]{:S(2)}, u32[]{:S(2)}) collective-permute-start(bf16[288,256]{1,0:T(8,128)(2,1)S(1)} %get-tuple-element.60), channel_id=1, source_target_pairs={{0,3},{1,2},{2,1},{3,0},{4,7},{5,6},{6,5},{7,4},{8,11},{9,10},{10,... | collective-permute-start | bytes 442376 | tf_op jit(solution)/shard_map/ppermute | solution.py:373
  24.7 2.8 %copy-start.3 = (bf16[2304,256]{1,0:T(8,128)(2,1)S(1)}, bf16[2304,256]{1,0:T(8,128)(2,1)}, u32[]{:S(2)}) copy-start(bf16[2304,256]{1,0:T(8,128)(2,1)} %weight.4) | copy-start | bytes 3538948
  30.6 5.1 %collective-permute-start.7 = (bf16[2304,128]{1,0:T(8,128)(2,1)S(1)}, bf16[2304,128]{1,0:T(8,128)(2,1)S(1)}, u32[]{:S(2)}, u32[]{:S(2)}) collective-permute-start(bf16[2304,128]{1,0:T(8,128)(2,1)S(1)} %get-tuple-element.67), channel_id=1, source_target_pairs={{0,32},{32,0},{64,96},{96,64},{128,160},{160,128},{192,224},{224,1... | collective-permute-start | bytes 1769480 | tf_op jit(solution)/shard_map/ppermute | solution.py:373
  35.1 3.8 %copy-start = (bf16[2304,256]{1,0:T(8,128)(2,1)S(1)}, bf16[2304,256]{1,0:T(8,128)(2,1)}, u32[]{:S(2)}) copy-start(bf16[2304,256]{1,0:T(8,128)(2,1)} %weight.7) | copy-start | bytes 3538948
  35.1 3.8 %copy-start.2 = (bf16[1,2,400,256]{3,2,1,0:T(8,128)(2,1)S(1)}, bf16[1,2,400,256]{3,2,1,0:T(8,128)(2,1)}, u32[]{:S(2)}) copy-start(bf16[1,2,400,256]{3,2,1,0:T(8,128)(2,1)} %param.13) | copy-start | bytes 1228804
  35.9 6.7 %collective-permute-start.8 = (bf16[8,72,128]{2,1,0:T(8,128)(2,1)S(1)}, bf16[8,72,128]{2,1,0:T(8,128)(2,1)S(1)}, u32[]{:S(2)}, u32[]{:S(2)}) collective-permute-start(bf16[8,72,128]{2,1,0:T(8,128)(2,1)S(1)} %get-tuple-element.70), channel_id=1, source_target_pairs={{0,2},{1,3},{2,0},{3,1},{4,6},{5,7},{6,4},{7,5},{8,10},{9,11},{10,... | collective-permute-start | bytes 442376 | tf_op jit(solution)/shard_map/ppermute | solution.py:373
  37.6 8.8 %collective-permute-start.9 = (bf16[8,72,128]{2,1,0:T(8,128)(2,1)S(1)}, bf16[8,72,128]{2,1,0:T(8,128)(2,1)S(1)}, u32[]{:S(2)}, u32[]{:S(2)}) collective-permute-start(bf16[8,72,128]{2,1,0:T(8,128)(2,1)S(1)} %get-tuple-element.71), channel_id=1, source_target_pairs={{0,3},{1,2},{2,1},{3,0},{4,7},{5,6},{6,5},{7,4},{8,11},{9,10},{10,... | collective-permute-start | bytes 442376 | tf_op jit(solution)/shard_map/ppermute | solution.py:373
  38.9 7.5 %collective-permute-start.10 = (bf16[8,72,128]{2,1,0:T(8,128)(2,1)S(1)}, bf16[8,72,128]{2,1,0:T(8,128)(2,1)S(1)}, u32[]{:S(2)}, u32[]{:S(2)}) collective-permute-start(bf16[8,72,128]{2,1,0:T(8,128)(2,1)S(1)} %get-tuple-element.72), channel_id=1, source_target_pairs={{0,1},{1,0},{2,3},{3,2},{4,5},{5,4},{6,7},{7,6},{8,9},{9,8},{10,11... | collective-permute-start | bytes 442376 | tf_op jit(solution)/shard_map/ppermute | solution.py:373
  46.5 4.7 %collective-permute-start.13 = (bf16[2,72,128]{2,1,0:T(8,128)(2,1)S(1)}, bf16[2,72,128]{2,1,0:T(8,128)(2,1)S(1)}, u32[]{:S(2)}, u32[]{:S(2)}) collective-permute-start(bf16[2,72,128]{2,1,0:T(8,128)(2,1)S(1)} %get-tuple-element.82), channel_id=1, source_target_pairs={{0,12},{1,13},{2,14},{3,15},{4,8},{5,9},{6,10},{7,11},{8,4},{9,5},... | collective-permute-start | bytes 110600 | tf_op jit(solution)/shard_map/ppermute | solution.py:373
  48.3 4.1 %collective-permute-start.12 = (bf16[2,72,128]{2,1,0:T(8,128)(2,1)S(1)}, bf16[2,72,128]{2,1,0:T(8,128)(2,1)S(1)}, u32[]{:S(2)}, u32[]{:S(2)}) collective-permute-start(bf16[2,72,128]{2,1,0:T(8,128)(2,1)S(1)} %get-tuple-element.81), channel_id=1, source_target_pairs={{0,8},{1,9},{2,10},{3,11},{4,12},{5,13},{6,14},{7,15},{8,0},{9,1},... | collective-permute-start | bytes 110600 | tf_op jit(solution)/shard_map/ppermute | solution.py:373
  48.5 3.9 %collective-permute-start.11 = (bf16[2,72,128]{2,1,0:T(8,128)(2,1)S(1)}, bf16[2,72,128]{2,1,0:T(8,128)(2,1)S(1)}, u32[]{:S(2)}, u32[]{:S(2)}) collective-permute-start(bf16[2,72,128]{2,1,0:T(8,128)(2,1)S(1)} %get-tuple-element.80), channel_id=1, source_target_pairs={{0,4},{1,5},{2,6},{3,7},{4,0},{5,1},{6,2},{7,3},{8,12},{9,13},{10,... | collective-permute-start | bytes 110600 | tf_op jit(solution)/shard_map/ppermute | solution.py:373
  52.5 5.7 %collective-permute-start.14 = (bf16[72,128]{1,0:T(8,128)(2,1)S(1)}, bf16[72,128]{1,0:T(8,128)(2,1)S(1)}, u32[]{:S(2)}, u32[]{:S(2)}) collective-permute-start(bf16[72,128]{1,0:T(8,128)(2,1)S(1)} %fusion.2), channel_id=1, source_target_pairs={{0,28},{1,29},{2,30},{3,31},{4,24},{5,25},{6,26},{7,27},{8,20},{9,... | collective-permute-start | bytes 55304 | tf_op jit(solution)/shard_map/ppermute | solution.py:373
  56.7 8.1 %collective-permute-start.18 = (bf16[400,256]{1,0:T(8,128)(2,1)S(1)}, bf16[400,256]{1,0:T(8,128)(2,1)S(1)}, u32[]{:S(2)}, u32[]{:S(2)}) collective-permute-start(bf16[400,256]{1,0:T(8,128)(2,1)S(1)} %get-tuple-element.86), channel_id=1, source_target_pairs={{0,1},{1,0},{2,3},{3,2},{4,5},{5,4},{6,7},{7,6},{8,9},{9,8},{10,11... | collective-permute-start | bytes 614408 | tf_op jit(solution)/shard_map/ppermute | solution.py:373
  57.3 7.9 %collective-permute-start.19 = (bf16[400,256]{1,0:T(8,128)(2,1)S(1)}, bf16[400,256]{1,0:T(8,128)(2,1)S(1)}, u32[]{:S(2)}, u32[]{:S(2)}) collective-permute-start(bf16[400,256]{1,0:T(8,128)(2,1)S(1)} %get-tuple-element.87), channel_id=1, source_target_pairs={{0,31},{1,2},{2,1},{3,4},{4,3},{5,6},{6,5},{7,8},{8,7},{9,10},{10,... | collective-permute-start | bytes 614408 | tf_op jit(solution)/shard_map/ppermute | solution.py:373
  58.2 3.9 %collective-permute-start.15 = (bf16[72,128]{1,0:T(8,128)(2,1)S(1)}, bf16[72,128]{1,0:T(8,128)(2,1)S(1)}, u32[]{:S(2)}, u32[]{:S(2)}) collective-permute-start(bf16[72,128]{1,0:T(8,128)(2,1)S(1)} %fusion.1), channel_id=1, source_target_pairs={{0,192},{32,224},{64,128},{96,160},{128,64},{160,96},{192,0},{224,... | collective-permute-start | bytes 55304 | tf_op jit(solution)/shard_map/ppermute | solution.py:373
  60.7 4.1 %collective-permute-start.16 = (bf16[72,128]{1,0:T(8,128)(2,1)S(1)}, bf16[72,128]{1,0:T(8,128)(2,1)S(1)}, u32[]{:S(2)}, u32[]{:S(2)}) collective-permute-start(bf16[72,128]{1,0:T(8,128)(2,1)S(1)} %fusion.1), channel_id=1, source_target_pairs={{0,128},{32,160},{64,192},{96,224},{128,0},{160,32},{192,64},{224,... | collective-permute-start | bytes 55304 | tf_op jit(solution)/shard_map/ppermute | solution.py:373
  61.3 3.6 %collective-permute-start.17 = (bf16[72,128]{1,0:T(8,128)(2,1)S(1)}, bf16[72,128]{1,0:T(8,128)(2,1)S(1)}, u32[]{:S(2)}, u32[]{:S(2)}) collective-permute-start(bf16[72,128]{1,0:T(8,128)(2,1)S(1)} %fusion.1), channel_id=1, source_target_pairs={{0,64},{32,96},{64,0},{96,32},{128,192},{160,224},{192,128},{224,1... | collective-permute-start | bytes 55304 | tf_op jit(solution)/shard_map/ppermute | solution.py:373
  65.3 4.4 %collective-permute-start.20 = (f32[72,128]{1,0:T(8,128)S(1)}, f32[72,128]{1,0:T(8,128)S(1)}, u32[]{:S(2)}, u32[]{:S(2)}) collective-permute-start(f32[72,128]{1,0:T(8,128)S(1)} %convert_add_fusion.1.ours), channel_id=1, source_target_pairs={{0,32},{32,0},{64,96},{96,64},{128,160},{160,128},{192,224},{224,1... | collective-permute-start | bytes 110600 | tf_op jit(solution)/shard_map/ppermute | solution.py:373
